TPU v7x, 32 devices: a whole 2x2x4 slice. The times are simulated.
32 devices in a mesh: ctx: 8 (over y, x, core), sp: 4 (over z).
Axes of the slice: x: 2, y: 2, z: 4, core: 2. Of those that a mesh axis runs over, the one named last changes fastest.
Arguments:
- layer_input: bfloat16 [4096, 2560], P(('ctx', 'sp')), may hold values from -6 to 6
- proj_weight: bfloat16 [2560, 5120], P('ctx', 'sp'), may hold values from -0.125 to 0.125
- state_weight: bfloat16 [2560, 256], replicated, may hold values from -0.125 to 0.125
- out_grad: bfloat16 [4096, 5120], P('ctx', 'sp'), may hold values from -6 to 6
- log_decay: float32 [80, 4096], P('sp', 'ctx'), may hold values from -1 to 0, as said below
- skip_gain: float32 [80], P('sp'), may hold values from 0.5 to 1.5
Outputs:
- grad_input: bfloat16 [4096, 2560], P(('ctx', 'sp'))
- grad_proj: float32 [2560, 5120], P('ctx', 'sp')
- grad_state: float32 [2560, 256], P(('ctx', 'sp'))
Inputs may be any that keep to these rules, and one draw needn't show every extreme that they name: `log_decay`: every entry is below zero.
All inputs are finite; a program needn't handle non-finite values.
Results may differ from a plain program's by a relative error of at most 0.025.
Values may be sent and summed in bfloat16 or wider, within the bound.
A program may use at most 128 MiB of HBM per device.

v0:
```python
import jax
import jax.numpy as jnp
from jax import lax
from jax.sharding import PartitionSpec as P

BLOCK = 256


def passed_along(shard, axis, by):
    peers = lax.axis_size(axis)
    pairs = [(i, i + by) for i in range(peers) if 0 <= i + by < peers]
    return lax.ppermute(shard, axis, pairs)


def contract(form, left, right):
    return jnp.einsum(form, left, right, preferred_element_type=jnp.float32)


def combine(preceding_tokens, later):
    leading_decay, first_state = preceding_tokens
    last_decay, last_state = later
    return (leading_decay * last_decay, last_decay[:, None, None] * first_state + last_state)


def forward_step(carried, element):
    return (combine(carried, element), carried)


def split_heads(matrix, count_of_heads):
    row_total, col_total = matrix.shape
    block_count = row_total // BLOCK
    shaped = matrix.reshape(block_count, BLOCK, count_of_heads, col_total // count_of_heads)
    return shaped.transpose(0, 2, 1, 3)


def merge_heads(grads):
    block_count, count_of_heads, length, head_width = grads.shape
    return grads.transpose(0, 2, 1, 3).reshape(block_count * length, count_of_heads * head_width)


def decay_blocks(log_decay):
    count_of_heads, row_total = log_decay.shape
    shaped = log_decay.reshape(count_of_heads, row_total // BLOCK, BLOCK)
    cumulative = jnp.cumsum(shaped, axis=2).transpose(1, 0, 2)
    input_gate = jnp.sqrt(-jnp.expm1(2.0 * shaped)).transpose(1, 0, 2)
    return (cumulative, input_gate)


def weighted_inputs(values, cotangent, cumulative, input_gate):
    to_end = jnp.exp(cumulative[:, -1:] - cumulative)
    gated_values = (values * (input_gate * to_end)[:, :, None]).astype(jnp.bfloat16)
    scaled_cot = (cotangent * jnp.exp(cumulative)[:, :, None]).astype(jnp.bfloat16)
    return (gated_values, scaled_cot)


def block_summary(values, cotangent, writer, reader, cumulative, input_gate):
    norm_scale = writer.shape[1] ** (-0.5)
    gated_values, scaled_cot = weighted_inputs(values, cotangent, cumulative, input_gate)
    written = contract("sn,hsp->hnp", writer, gated_values)
    pending = contract("sn,hsp->hnp", reader, scaled_cot) * norm_scale
    return (jnp.exp(cumulative[:, -1]), written, pending)


def block_grads(
    values, cotangent, writer, reader, cumulative, input_gate, state_in, adjoint_in, skip_gain
):
    norm_scale = writer.shape[1] ** (-0.5)
    length = cumulative.shape[1]
    causal = (jnp.arange(length)[:, None] >= jnp.arange(length)[None, :])[None]
    exponent = cumulative[:, :, None] - cumulative[:, None, :]
    decays = jnp.where(causal, jnp.exp(jnp.where(causal, exponent, 0.0)), 0.0)
    to_end = jnp.exp(cumulative[:, -1:] - cumulative)
    gated_values, scaled_cot = weighted_inputs(values, cotangent, cumulative, input_gate)
    state_low = state_in.astype(jnp.bfloat16)
    adjoint_low = adjoint_in.astype(jnp.bfloat16)
    gram_grad = contract("htp,hsp->hts", cotangent, values)
    weighted = (decays * gram_grad * input_gate[:, None, :]).astype(jnp.bfloat16)
    read_write = contract("tn,sn->ts", reader, writer)
    mixing = (decays * read_write[None]).astype(jnp.bfloat16)
    grad_reader = (
        contract("hts,sn->tn", weighted, writer) + contract("htp,hnp->tn", scaled_cot, state_low)
    ) * norm_scale
    grad_writer = contract("hst,sn->tn", weighted, reader) * norm_scale + contract(
        "htp,hnp->tn", gated_values, adjoint_low
    )
    carried_part = contract("hst,hsp->htp", mixing, cotangent) * norm_scale
    state_part = to_end[:, :, None] * contract("tn,hnp->htp", writer, adjoint_low)
    grad_values = input_gate[:, :, None] * (carried_part + state_part) + skip_gain[
        :, None, None
    ] * cotangent.astype(jnp.float32)
    return (grad_values, grad_writer, grad_reader)


def shards(layer_input, proj_weight, state_weight, out_grad, log_decay, skip_gain):
    count_of_heads = skip_gain.shape[0]
    state_size = state_weight.shape[1] // 2
    gathered = lax.all_gather(layer_input, "sp", axis=0, tiled=True)
    full_weight = lax.all_gather(proj_weight, "ctx", axis=0, tiled=True)
    values_all = jnp.dot(gathered, full_weight, preferred_element_type=jnp.float32).astype(
        jnp.bfloat16
    )
    projected = jnp.dot(gathered, state_weight, preferred_element_type=jnp.float32).astype(
        jnp.bfloat16
    )
    values = split_heads(values_all, count_of_heads)
    cotangent = split_heads(out_grad, count_of_heads)
    block_count = values.shape[0]
    head_width = values.shape[3]
    writer = projected[:, :state_size].reshape(block_count, BLOCK, state_size)
    reader = projected[:, state_size:].reshape(block_count, BLOCK, state_size)
    cumulative, input_gate = decay_blocks(log_decay)
    block_decay, written, pending = jax.vmap(block_summary)(
        values, cotangent, writer, reader, cumulative, input_gate
    )
    identity = (
        jnp.ones((count_of_heads,), jnp.float32),
        jnp.zeros((count_of_heads, state_size, head_width), jnp.float32),
    )
    device_state, prefix = lax.scan(forward_step, identity, (block_decay, written))
    device_adjoint, suffix = lax.scan(forward_step, identity, (block_decay, pending), reverse=True)

    def relay_step(iteration, carried):
        state_prev, adjoint_prev = carried
        state_next = passed_along(
            (device_state[0][:, None, None] * state_prev + device_state[1]).astype(jnp.bfloat16),
            "ctx",
            1,
        ).astype(jnp.float32)
        adjoint_next = passed_along(
            (device_adjoint[0][:, None, None] * adjoint_prev + device_adjoint[1]).astype(
                jnp.bfloat16
            ),
            "ctx",
            -1,
        ).astype(jnp.float32)
        return (state_next, adjoint_next)

    state_from, adjoint_from = lax.fori_loop(
        0, lax.axis_size("ctx") - 1, relay_step, (identity[1], identity[1])
    )
    state_in = prefix[1] + prefix[0][:, :, None, None] * state_from[None]
    adjoint_in = suffix[1] + suffix[0][:, :, None, None] * adjoint_from[None]
    grad_values, grad_writer, grad_reader = lax.map(
        lambda element: block_grads(*element, skip_gain),
        (values, cotangent, writer, reader, cumulative, input_gate, state_in, adjoint_in),
    )
    grad_heads = merge_heads(grad_values).astype(jnp.bfloat16)
    partial_grads = jnp.concatenate([grad_writer, grad_reader], axis=2).reshape(
        block_count * BLOCK, 2 * state_size
    )
    grad_projected = lax.psum_scatter(
        partial_grads.astype(jnp.bfloat16), "sp", scatter_dimension=0, tiled=True
    )
    summed = lax.psum_scatter(
        lax.dot_general(
            grad_heads, full_weight, (((1,), (1,)), ((), ())), preferred_element_type=jnp.float32
        ).astype(jnp.bfloat16),
        "sp",
        scatter_dimension=0,
        tiled=True,
    ).astype(jnp.float32)
    grad_input = (
        summed + jnp.dot(grad_projected, state_weight.T, preferred_element_type=jnp.float32)
    ).astype(jnp.bfloat16)
    grad_scale = (gathered.shape[0] * lax.axis_size("ctx")) ** (-0.5)
    columns = gathered
    grad_proj = (
        lax.psum_scatter(
            lax.dot_general(
                columns, grad_heads, (((0,), (0,)), ((), ())), preferred_element_type=jnp.float32
            ).astype(jnp.bfloat16),
            "ctx",
            scatter_dimension=0,
            tiled=True,
        ).astype(jnp.float32)
        * grad_scale
    )
    columns = layer_input
    grad_state = (
        lax.psum_scatter(
            lax.dot_general(
                columns,
                grad_projected,
                (((0,), (0,)), ((), ())),
                preferred_element_type=jnp.float32,
            ),
            ("ctx", "sp"),
            scatter_dimension=0,
            tiled=True,
        )
        * grad_scale
    )
    return (grad_input, grad_proj, grad_state)


def solution(mesh):
    in_specs = (
        P(("ctx", "sp"), None),
        P("ctx", "sp"),
        P(),
        P("ctx", "sp"),
        P("sp", "ctx"),
        P("sp"),
    )
    out_specs = (P(("ctx", "sp"), None), P("ctx", "sp"), P(("ctx", "sp"), None))
    return jax.shard_map(shards, mesh=mesh, in_specs=in_specs, out_specs=out_specs, check_vma=False)
```

profile of v0, /device:TPU:0, one launch (start us, length us, event | category | flops | bytes accessed | tf_op | source)
XLA Modules:
  0.0 586.1 jit_solution(15638801374339521446)
XLA Ops:
  14.0 4.0 reshape.133
  18.1 49.1 %all-gather.3.cloned.1.call-done = bf16[512,2560]{1,0:T(8,128)(2,1)} async-done(((bf16[128,2560]{1,0:T(8,128)(2,1)}), bf16[512,2560]{1,0:T(8,128)(2,1)}) %all-gather.3.cloned.1.call-update) | async-done | bytes 2621456 | tf_op jit(solution)/shard_map/all_gather | solution.py:97
  67.2 2.7 convolution_convert_fusion.3
  73.9 14.6 %while.66 = (s32[]{:T(128)}, f32[20]{0:T(128)S(1)}, f32[20,128,64]{2,1,0:T(8,128)}, f32[2,20]{1,0:T(2,128)}, f32[2,20,128,64]{3,2,1,0:T(8,128)}, /*index=5*/f32[...) while((s32[]{:T(128)}, f32[20]{0:T(128)S(1)}, f32[20,128,64]{2,1,0:T(8,128)}, ...), condition=%wide.region_5.6_spmd.clone, body=%wide.region_4.5_spmd.clone.sunk | while | flops 655404 | bytes 12455313 | solution.py:120
  84.8 3.1 bitcast_add_fusion.4
  91.0 23.5 %all-gather.5.cloned.1.call-done = bf16[2560,1280]{1,0:T(8,128)(2,1)} async-done(((bf16[320,1280]{1,0:T(8,128)(2,1)}), bf16[2560,1280]{1,0:T(8,128)(2,1)}) %all-gather.5.cloned.1.call-update) | async-done | bytes 6553616 | tf_op jit(solution)/shard_map/all_gather | solution.py:98
  114.5 8.3 %convolution_convert_fusion.2 = bf16[512,1280]{1,0:T(8,128)(2,1)} fusion(bf16[512,2560]{1,0:T(8,128)(2,1)} %all-gather.3.cloned.1.call-done, bf16[2560,1280]{1,0:T(8,128)(2,1)} %all-gather.5.cloned.1.call-done), kind=kOutput, calls=%fused_computation.103 | convolution fusion | flops 3356098560 | bytes 10485760 | tf_op jit(solution)/shard_map/dot_general | solution.py:99
  125.2 4.0 reshape.134
  129.3 4.0 copy_bitcast_fusion.2
  137.2 11.1 %while.67 = (s32[]{:T(128)}, f32[20]{0:T(128)S(1)}, f32[20,128,64]{2,1,0:T(8,128)S(1)}, f32[2,20]{1,0:T(2,128)}, f32[2,20,128,64]{3,2,1,0:T(8,128)}, /*index=5*/...) while((s32[]{:T(128)}, f32[20]{0:T(128)S(1)}, ...), condition=%wide.region_3.4_spmd.clone, body=%wide.region_2.3_spmd.clone.sunk | while | flops 655403 | bytes 11800449 | solution.py:119
  149.5 102.1 %while.68 = (s32[]{:T(128)}, f32[20,128,64]{1,2,0:T(8,128)S(1)}, f32[20,128,64]{1,2,0:T(8,128)}, f32[20]{0:T(128)S(1)}, f32[20,128,64]{1,2,0:T(8,128)}, /*index=...) while((s32[]{:T(128)}, f32[20,128,64]{1,2,0:T(8,128)S(1)}, ...), condition=%wide.region_7.8_spmd.clone, body=%wide.region_6.7_spmd.clone.sunk | while | flops 1638403 | bytes 13107600 | solution.py:138
  151.6 2.9 collective-permute-start
  162.2 8.0 %collective-permute-start = (bf16[20,128,64]{1,2,0:T(8,128)(2,1)}, bf16[20,128,64]{1,2,0:T(8,128)(2,1)}, u32[]{:S(2)}, u32[]{:S(2)}) collective-permute-start(bf16[20,128,64]{1,2,0:T(8,128)(2,1)} %fusion.142), channel_id=1, source_target_pairs={{0,4},{4,8},{8,12},{12,16},{16,20},{20,24},{24,28},{1,5},{5,9},{9,... | collective-permute-start | bytes 983048 | tf_op jit(solution)/shard_map/while/body/eval_jaxpr/ppermute | solution.py:12
  177.7 7.3 %collective-permute-start = (bf16[20,128,64]{1,2,0:T(8,128)(2,1)}, bf16[20,128,64]{1,2,0:T(8,128)(2,1)}, u32[]{:S(2)}, u32[]{:S(2)}) collective-permute-start(bf16[20,128,64]{1,2,0:T(8,128)(2,1)} %fusion.142), channel_id=1, source_target_pairs={{0,4},{4,8},{8,12},{12,16},{16,20},{20,24},{24,28},{1,5},{5,9},{9,... | collective-permute-start | bytes 983048 | tf_op jit(solution)/shard_map/while/body/eval_jaxpr/ppermute | solution.py:12
  192.6 7.7 %collective-permute-start = (bf16[20,128,64]{1,2,0:T(8,128)(2,1)}, bf16[20,128,64]{1,2,0:T(8,128)(2,1)}, u32[]{:S(2)}, u32[]{:S(2)}) collective-permute-start(bf16[20,128,64]{1,2,0:T(8,128)(2,1)} %fusion.142), channel_id=1, source_target_pairs={{0,4},{4,8},{8,12},{12,16},{16,20},{20,24},{24,28},{1,5},{5,9},{9,... | collective-permute-start | bytes 983048 | tf_op jit(solution)/shard_map/while/body/eval_jaxpr/ppermute | solution.py:12
  207.9 7.7 %collective-permute-start = (bf16[20,128,64]{1,2,0:T(8,128)(2,1)}, bf16[20,128,64]{1,2,0:T(8,128)(2,1)}, u32[]{:S(2)}, u32[]{:S(2)}) collective-permute-start(bf16[20,128,64]{1,2,0:T(8,128)(2,1)} %fusion.142), channel_id=1, source_target_pairs={{0,4},{4,8},{8,12},{12,16},{16,20},{20,24},{24,28},{1,5},{5,9},{9,... | collective-permute-start | bytes 983048 | tf_op jit(solution)/shard_map/while/body/eval_jaxpr/ppermute | solution.py:12
  223.2 7.7 %collective-permute-start = (bf16[20,128,64]{1,2,0:T(8,128)(2,1)}, bf16[20,128,64]{1,2,0:T(8,128)(2,1)}, u32[]{:S(2)}, u32[]{:S(2)}) collective-permute-start(bf16[20,128,64]{1,2,0:T(8,128)(2,1)} %fusion.142), channel_id=1, source_target_pairs={{0,4},{4,8},{8,12},{12,16},{16,20},{20,24},{24,28},{1,5},{5,9},{9,... | collective-permute-start | bytes 983048 | tf_op jit(solution)/shard_map/while/body/eval_jaxpr/ppermute | solution.py:12
  238.4 7.7 %collective-permute-start = (bf16[20,128,64]{1,2,0:T(8,128)(2,1)}, bf16[20,128,64]{1,2,0:T(8,128)(2,1)}, u32[]{:S(2)}, u32[]{:S(2)}) collective-permute-start(bf16[20,128,64]{1,2,0:T(8,128)(2,1)} %fusion.142), channel_id=1, source_target_pairs={{0,4},{4,8},{8,12},{12,16},{16,20},{20,24},{24,28},{1,5},{5,9},{9,... | collective-permute-start | bytes 983048 | tf_op jit(solution)/shard_map/while/body/eval_jaxpr/ppermute | solution.py:12
  252.3 3.2 multiply_add_fusion
  262.5 20.4 %while.65 = (s32[]{:T(128)}, bf16[2,20,256,64]{2,3,1,0:T(8,128)(2,1)}, bf16[2,256,128]{2,1,0:T(8,128)(2,1)}, bf16[2,256,128]{2,1,0:T(8,128)(2,1)}, f32[2,20,256]...) while((s32[]{:T(128)}, ...), condition=%wide.region_10.11_spmd, body=%wide.region_8.10_spmd.sunk | while | flops 658974720 | bytes 37262452 | solution.py:143
  263.6 2.9 fusion.135
  273.8 2.9 fusion.135
  287.7 8.4 %convolution_convert_fusion.1 = bf16[512,2560]{1,0:T(8,128)(2,1)} fusion(bf16[512,1280]{0,1:T(8,128)(2,1)} %bitcast.233, bf16[2560,1280]{1,0:T(8,128)(2,1)} %all-gather.5.cloned.1.call-done), kind=kOutput, calls=%fused_computation.99 | convolution fusion | flops 3356753920 | bytes 10485760 | tf_op jit(solution)/shard_map/dot_general | solution.py:155
  296.1 17.1 %reduce-scatter.11.cloned.1.call-done = bf16[128,256]{1,0:T(8,128)(2,1)} async-done(((bf16[512,256]{1,0:T(8,128)(2,1)}), bf16[128,256]{1,0:T(8,128)(2,1)}) %reduce-scatter.11.cloned.1.call-update) | async-done | bytes 65552 | tf_op jit(solution)/shard_map/reduce_scatter | solution.py:151
  313.2 2.8 convolution_bitcast_fusion.2
  316.0 3.2 copy.143
  320.8 7.3 %fusion.70 = bf16[2560,1280]{0,1:T(8,128)(2,1)} fusion(bf16[512,1280]{0,1:T(8,128)(2,1)S(1)} %bitcast.234, bf16[512,2560]{1,0:T(8,128)(2,1)} %all-gather.3.cloned.1.call-done), kind=kOutput, calls=%fused_computation.98 | convolution fusion | flops 3358720000 | bytes 10485760 | tf_op jit(solution)/shard_map/dot_general | solution.py:169
  328.1 9.5 %copy.141 = bf16[2560,1280]{1,0:T(8,128)(2,1)} copy(bf16[2560,1280]{0,1:T(8,128)(2,1)} %fusion.70) | data formatting | bytes 13107200
  337.6 28.2 %reduce-scatter.9.cloned.1.call-done = bf16[128,2560]{1,0:T(8,128)(2,1)} async-done(((bf16[512,2560]{1,0:T(8,128)(2,1)}), bf16[128,2560]{1,0:T(8,128)(2,1)}) %reduce-scatter.9.cloned.1.call-update) | async-done | bytes 655376 | tf_op jit(solution)/shard_map/reduce_scatter | solution.py:154
  368.4 139.5 %reduce-scatter.15.cloned.1.call-done = f32[80,256]{1,0:T(8,128)} async-done(((f32[2560,256]{1,0:T(8,128)}), f32[80,256]{1,0:T(8,128)}) %reduce-scatter.15.cloned.1.call-update) | async-done | bytes 81936
  509.6 63.9 %reduce-scatter.13.cloned.1.call-done = bf16[320,1280]{1,0:T(8,128)(2,1)} async-done(((bf16[2560,1280]{1,0:T(8,128)(2,1)}), bf16[320,1280]{1,0:T(8,128)(2,1)}) %reduce-scatter.13.cloned.1.call-update) | async-done | bytes 819216
  576.5 2.7 copy.137
  (302 shorter events, 131.6 us)
Async XLA Ops:
  7.2 60.0 %copy-start = (bf16[2560,256]{1,0:T(8,128)(2,1)S(1)}, bf16[2560,256]{1,0:T(8,128)(2,1)}, u32[]{:S(2)}) copy-start(bf16[2560,256]{1,0:T(8,128)(2,1)} %param.16) | copy-start | bytes 3932164
  7.2 60.0 %all-gather.3.cloned.1.call-start = ((), (), s32[]{:S(2)}) async-start(), calls=%async_computation.4 | async-start | bytes 3276800 | tf_op jit(solution)/shard_map/all_gather | solution.py:97
  7.9 106.6 %all-gather.5.cloned.1.call-start = ((), (), s32[]{:S(2)}) async-start(), calls=%async_computation.5 | async-start | bytes 7372800 | tf_op jit(solution)/shard_map/all_gather | solution.py:98
  8.7 304.5 %reduce-scatter.11.cloned.1.call-start = ((), (), s32[]{:S(2)}) async-start(), calls=%async_computation.7 | async-start | bytes 327680 | tf_op jit(solution)/shard_map/reduce_scatter | solution.py:151
  151.6 5.0 collective-permute-start
  155.3 3.9 collective-permute-start.1
  160.1 10.0 %copy-start.2 = (f32[20,128,64]{1,2,0:T(8,128)S(1)}, f32[20,128,64]{1,2,0:T(8,128)}, u32[]{:S(2)}) copy-start(f32[20,128,64]{1,2,0:T(8,128)} %get-tuple-element.930) | copy-start | bytes 1966084 | tf_op jit(solution)/shard_map/while
  160.1 10.1 %copy-start.4 = (f32[20,128,64]{1,2,0:T(8,128)S(1)}, f32[20,128,64]{1,2,0:T(8,128)}, u32[]{:S(2)}) copy-start(f32[20,128,64]{1,2,0:T(8,128)} %get-tuple-element.943) | copy-start | bytes 1966084 | tf_op jit(solution)/shard_map/while
  162.2 10.2 %collective-permute-start = (bf16[20,128,64]{1,2,0:T(8,128)(2,1)}, bf16[20,128,64]{1,2,0:T(8,128)(2,1)}, u32[]{:S(2)}, u32[]{:S(2)}) collective-permute-start(bf16[20,128,64]{1,2,0:T(8,128)(2,1)} %fusion.142), channel_id=1, source_target_pairs={{0,4},{4,8},{8,12},{12,16},{16,20},{20,24},{24,28},{1,5},{5,9},{9,... | collective-permute-start | bytes 983048 | tf_op jit(solution)/shard_map/while/body/eval_jaxpr/ppermute | solution.py:12
  171.0 3.7 collective-permute-start.1
  177.7 9.5 %collective-permute-start = (bf16[20,128,64]{1,2,0:T(8,128)(2,1)}, bf16[20,128,64]{1,2,0:T(8,128)(2,1)}, u32[]{:S(2)}, u32[]{:S(2)}) collective-permute-start(bf16[20,128,64]{1,2,0:T(8,128)(2,1)} %fusion.142), channel_id=1, source_target_pairs={{0,4},{4,8},{8,12},{12,16},{16,20},{20,24},{24,28},{1,5},{5,9},{9,... | collective-permute-start | bytes 983048 | tf_op jit(solution)/shard_map/while/body/eval_jaxpr/ppermute | solution.py:12
  185.9 3.7 collective-permute-start.1
  190.5 9.8 %copy-start.2 = (f32[20,128,64]{1,2,0:T(8,128)S(1)}, f32[20,128,64]{1,2,0:T(8,128)}, u32[]{:S(2)}) copy-start(f32[20,128,64]{1,2,0:T(8,128)} %get-tuple-element.930) | copy-start | bytes 1966084 | tf_op jit(solution)/shard_map/while
  190.5 9.8 %copy-start.4 = (f32[20,128,64]{1,2,0:T(8,128)S(1)}, f32[20,128,64]{1,2,0:T(8,128)}, u32[]{:S(2)}) copy-start(f32[20,128,64]{1,2,0:T(8,128)} %get-tuple-element.943) | copy-start | bytes 1966084 | tf_op jit(solution)/shard_map/while
  192.6 9.9 %collective-permute-start = (bf16[20,128,64]{1,2,0:T(8,128)(2,1)}, bf16[20,128,64]{1,2,0:T(8,128)(2,1)}, u32[]{:S(2)}, u32[]{:S(2)}) collective-permute-start(bf16[20,128,64]{1,2,0:T(8,128)(2,1)} %fusion.142), channel_id=1, source_target_pairs={{0,4},{4,8},{8,12},{12,16},{16,20},{20,24},{24,28},{1,5},{5,9},{9,... | collective-permute-start | bytes 983048 | tf_op jit(solution)/shard_map/while/body/eval_jaxpr/ppermute | solution.py:12
  201.2 3.7 collective-permute-start.1
  205.8 9.8 %copy-start.4 = (f32[20,128,64]{1,2,0:T(8,128)S(1)}, f32[20,128,64]{1,2,0:T(8,128)}, u32[]{:S(2)}) copy-start(f32[20,128,64]{1,2,0:T(8,128)} %get-tuple-element.943) | copy-start | bytes 1966084 | tf_op jit(solution)/shard_map/while
  207.9 9.9 %collective-permute-start = (bf16[20,128,64]{1,2,0:T(8,128)(2,1)}, bf16[20,128,64]{1,2,0:T(8,128)(2,1)}, u32[]{:S(2)}, u32[]{:S(2)}) collective-permute-start(bf16[20,128,64]{1,2,0:T(8,128)(2,1)} %fusion.142), channel_id=1, source_target_pairs={{0,4},{4,8},{8,12},{12,16},{16,20},{20,24},{24,28},{1,5},{5,9},{9,... | collective-permute-start | bytes 983048 | tf_op jit(solution)/shard_map/while/body/eval_jaxpr/ppermute | solution.py:12
  216.5 3.7 collective-permute-start.1
  221.1 9.8 %copy-start.2 = (f32[20,128,64]{1,2,0:T(8,128)S(1)}, f32[20,128,64]{1,2,0:T(8,128)}, u32[]{:S(2)}) copy-start(f32[20,128,64]{1,2,0:T(8,128)} %get-tuple-element.930) | copy-start | bytes 1966084 | tf_op jit(solution)/shard_map/while
  221.1 9.8 %copy-start.4 = (f32[20,128,64]{1,2,0:T(8,128)S(1)}, f32[20,128,64]{1,2,0:T(8,128)}, u32[]{:S(2)}) copy-start(f32[20,128,64]{1,2,0:T(8,128)} %get-tuple-element.943) | copy-start | bytes 1966084 | tf_op jit(solution)/shard_map/while
  223.2 9.9 %collective-permute-start = (bf16[20,128,64]{1,2,0:T(8,128)(2,1)}, bf16[20,128,64]{1,2,0:T(8,128)(2,1)}, u32[]{:S(2)}, u32[]{:S(2)}) collective-permute-start(bf16[20,128,64]{1,2,0:T(8,128)(2,1)} %fusion.142), channel_id=1, source_target_pairs={{0,4},{4,8},{8,12},{12,16},{16,20},{20,24},{24,28},{1,5},{5,9},{9,... | collective-permute-start | bytes 983048 | tf_op jit(solution)/shard_map/while/body/eval_jaxpr/ppermute | solution.py:12
  231.7 3.7 collective-permute-start.1
  236.4 9.8 %copy-start.2 = (f32[20,128,64]{1,2,0:T(8,128)S(1)}, f32[20,128,64]{1,2,0:T(8,128)}, u32[]{:S(2)}) copy-start(f32[20,128,64]{1,2,0:T(8,128)} %get-tuple-element.930) | copy-start | bytes 1966084 | tf_op jit(solution)/shard_map/while
  236.4 9.8 %copy-start.4 = (f32[20,128,64]{1,2,0:T(8,128)S(1)}, f32[20,128,64]{1,2,0:T(8,128)}, u32[]{:S(2)}) copy-start(f32[20,128,64]{1,2,0:T(8,128)} %get-tuple-element.943) | copy-start | bytes 1966084 | tf_op jit(solution)/shard_map/while
  238.4 9.9 %collective-permute-start = (bf16[20,128,64]{1,2,0:T(8,128)(2,1)}, bf16[20,128,64]{1,2,0:T(8,128)(2,1)}, u32[]{:S(2)}, u32[]{:S(2)}) collective-permute-start(bf16[20,128,64]{1,2,0:T(8,128)(2,1)} %fusion.142), channel_id=1, source_target_pairs={{0,4},{4,8},{8,12},{12,16},{16,20},{20,24},{24,28},{1,5},{5,9},{9,... | collective-permute-start | bytes 983048 | tf_op jit(solution)/shard_map/while/body/eval_jaxpr/ppermute | solution.py:12
  247.0 3.7 collective-permute-start.1
  287.6 78.2 %reduce-scatter.9.cloned.1.call-start = ((), (), s32[]{:S(2)}) async-start(), calls=%async_computation.6 | async-start | bytes 3276800 | tf_op jit(solution)/shard_map/reduce_scatter | solution.py:154
  296.1 17.1 %copy-start.10 = (bf16[128,2560]{1,0:T(8,128)(2,1)S(1)}, bf16[128,2560]{1,0:T(8,128)(2,1)}, u32[]{:S(2)}) copy-start(bf16[128,2560]{1,0:T(8,128)(2,1)} %param.14) | copy-start | bytes 1966084
  296.1 211.8 %reduce-scatter.15.cloned.1.call-start = ((), (), s32[]{:S(2)}) async-start(), calls=%async_computation.9 | async-start | bytes 2703360
  319.3 254.2 %reduce-scatter.13.cloned.1.call-start = ((), (), s32[]{:S(2)}) async-start(), calls=%async_computation.8 | async-start | bytes 7372800
  337.6 28.2 %copy-start.18 = (bf16[128,256]{1,0:T(8,128)(2,1)S(1)}, bf16[128,256]{1,0:T(8,128)(2,1)}, u32[]{:S(2)}) copy-start(bf16[128,256]{1,0:T(8,128)(2,1)} %reduce-scatter.11.cloned.1.call-done) | copy-start | bytes 196612
  (57 other events, 137.2 us)
Sparse Core Ops, SparseCore 0:
  9.6 57.5 all-gather.2
  69.0 45.3 all-gather.4
  287.8 25.4 reduce-scatter.10
  315.5 50.3 reduce-scatter.8
  368.1 139.7 reduce-scatter.14
  511.5 61.9 reduce-scatter.12
where the time goes:
time: 588 us; the launch traced here: 586 us
  waiting for transfers between devices  333 us (57%)
  local copies, waits for them, and re-layouts  72.4 us (12%)
  other arithmetic  58.8 us (10%)
  starting transfers between devices  58.2 us (10%)
  matrix products  48.9 us (8%)
  between operations  14.4 us (2%)
    unnamed x8, waiting for transfers between devices  205 us
    ppermute x14, starting transfers between devices, passed_along(): return lax.ppermute(shard, axis, pairs)  57.9 us
    all_gather x1, waiting for transfers between devices, shards(): gathered = lax.all_gather(layer_input, 'sp', axis=0, tiled=True)  49.1 us
    reduce_scatter x1, waiting for transfers between devices, shards(): lax.psum_scatter(lax.dot_general(grad_heads, full_weight, (((1,), (1,)),...  28.2 us
    unnamed x44, local copies, waits for them, and re-layouts  28.1 us
    all_gather x1, waiting for transfers between devices, shards(): full_weight = lax.all_gather(proj_weight, 'ctx', axis=0, tiled=True)  23.5 us
    reduce_scatter x1, waiting for transfers between devices, shards(): lax.psum_scatter(partial_grads.astype(jnp.bfloat16), 'sp', scatter_dimens...  17.1 us
    dot_general x18, matrix products, contract(): return jnp.einsum(form, left, right, preferred_element_type=jnp.float32)  17 us
  transfers between devices with their start and end apart: 20, of which 13 were waited for; matrix products, arithmetic and copies ran while one was open for 14% of the time, Pallas kernels for 0%

commit v1 on v0

v1 whole, which is shorter than its diff:
```python
import functools

import jax
import jax.numpy as jnp
from jax import lax
from jax.experimental import pallas as pl
from jax.experimental.pallas import tpu as pltpu
from jax.sharding import PartitionSpec as P

BLOCK = 256
PAIR = 128
VMEM_LIMIT = 48 * 1024 * 1024


def exchange(array, axis, bit):
    peers = lax.axis_size(axis)
    return lax.ppermute(array, axis, [(i, i ^ bit) for i in range(peers)])


def bits_of(axis):
    peers = lax.axis_size(axis)
    return [1 << k for k in range(peers.bit_length() - 1)]


def has_bit(axis, bit):
    return (lax.axis_index(axis) // bit) % 2


def cube_gather(shard, axis, order):
    bits = bits_of(axis)
    array = shard.reshape((1,) * len(bits) + shard.shape)
    for bit in order:
        dim = len(bits) - bit.bit_length()
        other = exchange(array, axis, bit)
        upper = has_bit(axis, bit) == 1
        array = jnp.concatenate(
            [jnp.where(upper, other, array), jnp.where(upper, array, other)], axis=dim
        )
    return array.reshape((-1,) + shard.shape[1:])


def cube_scatter(partial, axis, order):
    bits = bits_of(axis)
    rows = partial.shape[0] // lax.axis_size(axis)
    array = partial.reshape((2,) * len(bits) + (rows,) + partial.shape[1:])
    for bit in order:
        dim = len(bits) - bit.bit_length()
        own = has_bit(axis, bit)
        keep = lax.dynamic_slice_in_dim(array, own, 1, dim)
        send = lax.dynamic_slice_in_dim(array, 1 - own, 1, dim)
        got = exchange(send, axis, bit)
        total = keep.astype(jnp.float32) + got.astype(jnp.float32)
        array = total.astype(jnp.bfloat16)
    return total.reshape((rows,) + partial.shape[1:])


def per_head(columns, pair):
    low = jnp.broadcast_to(columns[:, 2 * pair : 2 * pair + 1], (columns.shape[0], PAIR // 2))
    high = jnp.broadcast_to(columns[:, 2 * pair + 1 : 2 * pair + 2], (columns.shape[0], PAIR // 2))
    return jnp.concatenate([low, high], axis=1)


def weigh_kernel(x_ref, weight_ref, left_ref, weighted_ref, out_ref):
    weights = weight_ref[0, 0]
    for pair in range(x_ref.shape[1] // PAIR):
        cols = slice(pair * PAIR, (pair + 1) * PAIR)
        scaled = (x_ref[:, cols].astype(jnp.float32) * per_head(weights, pair)).astype(jnp.bfloat16)
        weighted_ref[:, cols] = scaled
        out_ref[0, :, cols] = jnp.dot(left_ref[0], scaled, preferred_element_type=jnp.float32)


def weigh(x, weights, left):
    rows, width = x.shape
    blocks, groups, _, heads = weights.shape
    cols = width // groups
    state = left.shape[1]
    return pl.pallas_call(
        weigh_kernel,
        grid=(blocks, groups),
        in_specs=[
            pl.BlockSpec((BLOCK, cols), lambda b, g: (b, g)),
            pl.BlockSpec((1, 1, BLOCK, heads), lambda b, g: (b, g, 0, 0)),
            pl.BlockSpec((1, state, BLOCK), lambda b, g: (b, 0, 0)),
        ],
        out_specs=[
            pl.BlockSpec((BLOCK, cols), lambda b, g: (b, g)),
            pl.BlockSpec((1, state, cols), lambda b, g: (b, 0, g)),
        ],
        out_shape=[
            jax.ShapeDtypeStruct((rows, width), jnp.bfloat16),
            jax.ShapeDtypeStruct((blocks, state, width), jnp.float32),
        ],
        cost_estimate=pl.CostEstimate(
            flops=2 * rows * width * state, bytes_accessed=6 * rows * width, transcendentals=0
        ),
        compiler_params=pltpu.CompilerParams(vmem_limit_bytes=VMEM_LIMIT),
    )(x, weights, left)


def inner_kernel(
    scale, x_ref, c_ref, cumc_ref, cumr_ref, gate_ref, skip_ref, both_ref,
    part_ref, grads_ref, mix_ref, sum_ref,
):
    group = pl.program_id(1)
    state = both_ref.shape[1] // 2
    writer = both_ref[:, :state]
    reader = both_ref[:, state:]
    cross = (((1,), (1,)), ((), ()))

    @pl.when(group == 0)
    def _():
        mix_ref[...] = lax.dot_general(
            writer, reader, cross, preferred_element_type=jnp.float32
        )
        sum_ref[...] = jnp.zeros_like(sum_ref)

    source = lax.broadcasted_iota(jnp.int32, (BLOCK, BLOCK), 0)
    target = lax.broadcasted_iota(jnp.int32, (BLOCK, BLOCK), 1)
    causal = target >= source
    half = PAIR // 2
    for pair in range(x_ref.shape[1] // PAIR):
        carried = []
        for side in range(2):
            head = 2 * pair + side
            cols = slice(head * half, (head + 1) * half)
            cot = c_ref[:, cols]
            exponent = cumr_ref[0, 0, head : head + 1, :] - cumc_ref[0, 0, :, head : head + 1]
            decays = jnp.exp(jnp.where(causal, exponent, -1e30))
            gram = lax.dot_general(x_ref[:, cols], cot, cross, preferred_element_type=jnp.float32)
            gate = gate_ref[0, 0, :, head : head + 1]
            sum_ref[...] += (decays * gram) * gate
            mixing = (decays * mix_ref[...]).astype(jnp.bfloat16)
            carried.append(
                jnp.dot(mixing, cot, preferred_element_type=jnp.float32) * (gate * scale)
            )
        cols = slice(pair * PAIR, (pair + 1) * PAIR)
        part_ref[:, cols] = jnp.concatenate(carried, axis=1) + skip_ref[:, cols] * c_ref[
            :, cols
        ].astype(jnp.float32)

    @pl.when(group == pl.num_programs(1) - 1)
    def _():
        low = sum_ref[...].astype(jnp.bfloat16)
        grads_ref[:, :state] = scale * jnp.dot(low, reader, preferred_element_type=jnp.float32)
        grads_ref[:, state:] = scale * lax.dot_general(
            low, writer, (((0,), (0,)), ((), ())), preferred_element_type=jnp.float32
        )


def inner(values, cotangent, cum_cols, cum_rows, gate_cols, skip_lanes, projected):
    rows, width = values.shape
    blocks, groups, _, heads = cum_cols.shape
    cols = width // groups
    both = projected.shape[1]
    scale = (both // 2) ** (-0.5)
    column_spec = pl.BlockSpec((1, 1, BLOCK, heads), lambda b, g: (b, g, 0, 0))
    wide = pl.BlockSpec((BLOCK, cols), lambda b, g: (b, g))
    whole = pl.BlockSpec((BLOCK, both), lambda b, g: (b, 0))
    return pl.pallas_call(
        lambda x, c, cc, cr, gt, sk, bo, part, grads, mix, total: inner_kernel(
            scale, x, c, cc, cr, gt, sk, bo, part, grads, mix, total
        ),
        grid=(blocks, groups),
        in_specs=[
            wide,
            wide,
            column_spec,
            pl.BlockSpec((1, 1, heads, BLOCK), lambda b, g: (b, g, 0, 0)),
            column_spec,
            pl.BlockSpec((1, cols), lambda b, g: (0, g)),
            whole,
        ],
        out_specs=[wide, whole],
        out_shape=[
            jax.ShapeDtypeStruct((rows, width), jnp.float32),
            jax.ShapeDtypeStruct((rows, both), jnp.float32),
        ],
        scratch_shapes=[
            pltpu.VMEM((BLOCK, BLOCK), jnp.float32),
            pltpu.VMEM((BLOCK, BLOCK), jnp.float32),
        ],
        cost_estimate=pl.CostEstimate(
            flops=16 * rows * width * BLOCK, bytes_accessed=8 * rows * width, transcendentals=0
        ),
        compiler_params=pltpu.CompilerParams(vmem_limit_bytes=VMEM_LIMIT),
    )(values, cotangent, cum_cols, cum_rows, gate_cols, skip_lanes, projected)


def outer_kernel(
    scale, gated_ref, scaled_ref, part_ref, weight_ref, both_ref, inner_ref, state_ref, adjoint_ref,
    heads_ref, grads_ref,
):
    group = pl.program_id(1)
    state = both_ref.shape[1] // 2
    writer = both_ref[:, :state]
    adjoint = adjoint_ref[0]
    cross = (((1,), (1,)), ((), ()))

    @pl.when(group == 0)
    def _():
        grads_ref[...] = inner_ref[...]

    grads_ref[:, :state] += lax.dot_general(
        gated_ref[...], adjoint, cross, preferred_element_type=jnp.float32
    )
    grads_ref[:, state:] += scale * lax.dot_general(
        scaled_ref[...], state_ref[0], cross, preferred_element_type=jnp.float32
    )
    weights = weight_ref[0, 0]
    for pair in range(gated_ref.shape[1] // PAIR):
        cols = slice(pair * PAIR, (pair + 1) * PAIR)
        entering = jnp.dot(writer, adjoint[:, cols], preferred_element_type=jnp.float32)
        total = part_ref[:, cols] + per_head(weights, pair) * entering
        heads_ref[:, cols] = total.astype(jnp.bfloat16)


def outer(gated, scaled, part, weight_cols, projected, inner_grads, state_in, adjoint_in):
    rows, width = gated.shape
    blocks, groups, _, heads = weight_cols.shape
    cols = width // groups
    both = projected.shape[1]
    state = both // 2
    wide = pl.BlockSpec((BLOCK, cols), lambda b, g: (b, g))
    whole = pl.BlockSpec((BLOCK, both), lambda b, g: (b, 0))
    carried = pl.BlockSpec((1, state, cols), lambda b, g: (b, 0, g))
    return pl.pallas_call(
        functools.partial(outer_kernel, state ** (-0.5)),
        grid=(blocks, groups),
        in_specs=[
            wide,
            wide,
            wide,
            pl.BlockSpec((1, 1, BLOCK, heads), lambda b, g: (b, g, 0, 0)),
            whole,
            whole,
            carried,
            carried,
        ],
        out_specs=[wide, whole],
        out_shape=[
            jax.ShapeDtypeStruct((rows, width), jnp.bfloat16),
            jax.ShapeDtypeStruct((rows, both), jnp.float32),
        ],
        cost_estimate=pl.CostEstimate(
            flops=6 * rows * width * state, bytes_accessed=10 * rows * width, transcendentals=0
        ),
        compiler_params=pltpu.CompilerParams(vmem_limit_bytes=VMEM_LIMIT),
    )(gated, scaled, part, weight_cols, projected, inner_grads, state_in, adjoint_in)


def arriving(total, logs, lanes, forward):
    peers = lax.axis_size("ctx")
    me = lax.axis_index("ctx")
    index = jnp.arange(peers)

    def decay(first, last):
        inside = ((index >= first) & (index < last))[:, None]
        return jnp.exp(lanes(jnp.sum(jnp.where(inside, logs, 0.0), axis=0)))[None, :]

    entering = jnp.zeros_like(total)
    for bit in bits_of("ctx"):
        got = exchange(total.astype(jnp.bfloat16), "ctx", bit).astype(jnp.float32)
        start = (me // bit) * bit
        upper = has_bit("ctx", bit) == 1
        takes = upper if forward else jnp.logical_not(upper)
        between = decay(start, me) if forward else decay(me + 1, start + bit)
        entering = entering + jnp.where(takes, between * got, 0.0)
        partner = start ^ bit
        far_first = jnp.where(takes, start, partner)
        passed = decay(far_first, far_first + bit)
        total = jnp.where(takes, got, total) * passed + jnp.where(takes, total, got)
    return entering


def entering_blocks(terms, block_decay, arrived, forward):
    blocks = terms.shape[0]
    order = range(blocks) if forward else range(blocks - 1, -1, -1)
    held = [None] * blocks
    carried = arrived
    for block in order:
        held[block] = carried.astype(jnp.bfloat16)
        carried = block_decay[block][None, :] * carried + terms[block]
    return jnp.stack(held)


def piece_total(terms, block_decay, forward):
    blocks = terms.shape[0]
    order = range(blocks) if forward else range(blocks - 1, -1, -1)
    total = None
    for block in order:
        total = terms[block] if total is None else block_decay[block][None, :] * total + terms[block]
    return total


def shards(layer_input, proj_weight, state_weight, out_grad, log_decay, skip_gain):
    heads = skip_gain.shape[0]
    width = out_grad.shape[1]
    head_width = width // heads
    blocks = out_grad.shape[0] // BLOCK
    state = state_weight.shape[1] // 2
    scale = state ** (-0.5)
    groups = max(1, heads // 10)
    bits = bits_of("ctx")
    high = bits[1:]

    def lanes(per_head_values):
        return jnp.repeat(per_head_values, head_width, axis=-1)

    gathered = lax.all_gather(layer_input, "sp", axis=0, tiled=True)
    half = width // 2
    weight_a = cube_gather(proj_weight[:, :half], "ctx", high + bits[:1])
    weight_b = cube_gather(proj_weight[:, half:], "ctx", high[::-1] + bits[:1])

    shaped = log_decay.reshape(groups, heads // groups, blocks, BLOCK)
    cum_rows = jnp.cumsum(shaped, axis=3).transpose(2, 0, 1, 3)
    gate_rows = jnp.sqrt(-jnp.expm1(2.0 * shaped)).transpose(2, 0, 1, 3)
    to_end_rows = jnp.exp(cum_rows[..., -1:] - cum_rows)
    block_logs = cum_rows[..., -1].reshape(blocks, heads)
    block_decay = jnp.exp(lanes(block_logs))
    logs = cube_gather(jnp.sum(block_logs, axis=0)[None], "ctx", bits)
    cum_cols = cum_rows.transpose(0, 1, 3, 2)
    gate_cols = gate_rows.transpose(0, 1, 3, 2)
    from_start_cols = jnp.exp(cum_cols)
    gate_end_cols = (gate_rows * to_end_rows).transpose(0, 1, 3, 2)

    projected = jnp.dot(gathered, state_weight, preferred_element_type=jnp.float32).astype(
        jnp.bfloat16
    )
    turned = projected.reshape(blocks, BLOCK, 2 * state).transpose(0, 2, 1)
    scaled_cot, pending = weigh(out_grad, from_start_cols, turned[:, state:])
    pending = pending * scale
    adjoint_from = arriving(piece_total(pending, block_decay, False), logs, lanes, False)

    values = jnp.concatenate(
        [
            jnp.dot(gathered, w, preferred_element_type=jnp.float32).astype(jnp.bfloat16)
            for w in (weight_a, weight_b)
        ],
        axis=1,
    )
    gated, written = weigh(values, gate_end_cols, turned[:, :state])
    state_from = arriving(piece_total(written, block_decay, True), logs, lanes, True)
    part, inner_grads = inner(
        values, out_grad, cum_cols, cum_rows, gate_cols, lanes(skip_gain)[None, :], projected
    )
    state_in = entering_blocks(written, block_decay, state_from, True)
    adjoint_in = entering_blocks(pending, block_decay, adjoint_from, False)
    grad_heads, partial_grads = outer(
        gated, scaled_cot, part, gate_end_cols, projected, inner_grads, state_in, adjoint_in
    )
    low_grads = partial_grads.astype(jnp.bfloat16)

    across = (((1,), (1,)), ((), ()))
    down = (((0,), (0,)), ((), ()))
    dot = functools.partial(lax.dot_general, preferred_element_type=jnp.float32)
    grad_input = lax.psum_scatter(
        (
            dot(grad_heads[:, :half], weight_a, across)
            + dot(grad_heads[:, half:], weight_b, across)
            + dot(low_grads, state_weight, across)
        ).astype(jnp.bfloat16),
        "sp",
        scatter_dimension=0,
        tiled=True,
    )
    grad_scale = (gathered.shape[0] * lax.axis_size("ctx")) ** (-0.5)
    term_a = dot(gathered, grad_heads[:, :half], down).astype(jnp.bfloat16)
    term_b = dot(gathered, grad_heads[:, half:], down).astype(jnp.bfloat16)
    term_s = dot(gathered, low_grads, down).astype(jnp.bfloat16)
    sum_a = cube_scatter(term_a, "ctx", bits[:1] + high)
    sum_b = cube_scatter(term_b, "ctx", bits[:1] + high[::-1])
    sum_s = cube_scatter(term_s, "ctx", bits)
    grad_proj = jnp.concatenate([sum_a, sum_b], axis=1) * grad_scale
    grad_state = cube_scatter(sum_s.astype(jnp.bfloat16), "sp", bits_of("sp")) * grad_scale
    return (grad_input, grad_proj, grad_state)


def solution(mesh):
    in_specs = (
        P(("ctx", "sp"), None),
        P("ctx", "sp"),
        P(),
        P("ctx", "sp"),
        P("sp", "ctx"),
        P("sp"),
    )
    out_specs = (P(("ctx", "sp"), None), P("ctx", "sp"), P(("ctx", "sp"), None))
    return jax.shard_map(shards, mesh=mesh, in_specs=in_specs, out_specs=out_specs, check_vma=False)
```

time: 588 us -> 286 us (0.49)
  waiting for transfers between devices: 333 us -> 95.1 us
  starting transfers between devices: 58.2 us -> 18.8 us
  local copies, waits for them, and re-layouts: 72.4 us -> 48.4 us
  Pallas kernels: 0 us -> 21.4 us
  other arithmetic: 58.8 us -> 47.2 us
  matrix products: 48.9 us -> 38.5 us
    unnamed x8 -> x2, waiting for transfers between devices: 205 us -> 0.03 us
    ppermute x14 -> x26, waiting for transfers between devices: 9.85 us -> 83.3 us  [exchange(): return lax.ppermute(array, axis, [(i, i ^ bit) for i in range(peers)])]
    reduce_scatter x2 -> x1, waiting for transfers between devices: 45.3 us -> 0.01 us  [shards(): lax.psum_scatter((dot(grad_heads[:, :half], weight_a, across) + dot(grad_...]
    ppermute x14 -> x26, starting transfers between devices: 57.9 us -> 18.7 us  [exchange(): return lax.ppermute(array, axis, [(i, i ^ bit) for i in range(peers)])]
    all_gather x1, waiting for transfers between devices: 49.1 us -> 11.7 us  [shards(): gathered = lax.all_gather(layer_input, 'sp', axis=0, tiled=True)]
    all_gather x1 -> x0, waiting for transfers between devices: 23.5 us -> none  [shards(): full_weight = lax.all_gather(proj_weight, 'ctx', axis=0, tiled=True)]
    pallas_call x0 -> x4, Pallas kernels: none -> 21.4 us  [the longest x1 11.4 us: inner(): pl.pallas_call(lambda x, c, cc, cr, gt, sk, bo, part, grads, mix, total:...]
    unnamed x44 -> x112, local copies, waits for them, and re-layouts: 28.1 us -> 8.37 us
  transfers between devices with their start and end apart: 20 -> 28, of which waited for: 13 -> 16; matrix products, arithmetic and copies ran while one was open for 14% -> 37% of each run, Pallas kernels for 0% -> 6%
where the time goes in v1:
time: 286 us; the launch traced here: 284 us
  waiting for transfers between devices  95.1 us (33%)
  local copies, waits for them, and re-layouts  48.4 us (17%)
  other arithmetic  47.2 us (17%)
  matrix products  38.5 us (13%)
  Pallas kernels  21.4 us (7%)
  starting transfers between devices  18.8 us (7%)
  between operations  15.1 us (5%)
    ppermute x26, waiting for transfers between devices, exchange(): return lax.ppermute(array, axis, [(i, i ^ bit) for i in range(peers)])  83.3 us
    ppermute x26, starting transfers between devices, exchange(): return lax.ppermute(array, axis, [(i, i ^ bit) for i in range(peers)])  18.7 us
    all_gather x1, waiting for transfers between devices, shards(): gathered = lax.all_gather(layer_input, 'sp', axis=0, tiled=True)  11.7 us
    pallas_call x1, Pallas kernels, inner(): pl.pallas_call(lambda x, c, cc, cr, gt, sk, bo, part, grads, mix, total:...  11.4 us
    exp x20, local copies, waits for them, and re-layouts, decay(): jnp.exp(lanes(jnp.sum(jnp.where(inside, logs, 0.0), axis=0)))[None, :]  9.22 us
    concatenate x8, other arithmetic, cube_gather(): jnp.concatenate([jnp.where(upper, other, array), jnp.where(upper, array,...  8.67 us
    convert_element_type x7, other arithmetic, cube_scatter(): array = total.astype(jnp.bfloat16)  8.66 us
    unnamed x112, local copies, waits for them, and re-layouts  8.37 us
  transfers between devices with their start and end apart: 28, of which 16 were waited for; matrix products, arithmetic and copies ran while one was open for 37% of the time, Pallas kernels for 6%

profile of v1, /device:TPU:0, one launch (start us, length us, event | category | flops | bytes accessed | tf_op | source)
XLA Modules:
  0.0 284.5 jit_solution(12079930330252474162)
XLA Ops:
  8.6 3.0 %collective-permute-start = (bf16[1,1,1,320,640]{4,3,2,1,0:T(8,128)(2,1)S(1)}, bf16[1,1,1,320,640]{4,3,2,1,0:T(8,128)(2,1)S(1)}, u32[]{:S(2)}, u32[]{:S(2)}) collective-permute-start(bf16[1,1,1,320,640]{4,3,2,1,0:T(8,128)(2,1)S(1)} %get-tuple-element.53), channel_id=1, source_target_pairs={{0,8},{4,12},{8,0},{12,4},{16,24},{20,28},{24,16},{28,20},{1,9},{5... | collective-permute-start | bytes 1228808 | tf_op jit(solution)/shard_map/ppermute | solution.py:17
  13.1 7.9 %collective-permute-done = bf16[1,1,1,320,640]{4,3,2,1,0:T(8,128)(2,1)S(1)} collective-permute-done((bf16[1,1,1,320,640]{4,3,2,1,0:T(8,128)(2,1)S(1)}, bf16[1,1,1,320,640]{4,3,2,1,0:T(8,128)(2,1)S(1)}, u32[]{:S(2)}, u32[]{:S(2)}) %collective-permute-start) | collective-permute-done | bytes 409632 | tf_op jit(solution)/shard_map/ppermute | solution.py:17
  26.4 2.3 reduce-window.6
  30.9 12.7 %collective-permute-done.1 = bf16[1,2,1,320,640]{4,3,2,1,0:T(8,128)(2,1)} collective-permute-done((bf16[1,2,1,320,640]{4,3,2,1,0:T(8,128)(2,1)S(1)}, bf16[1,2,1,320,640]{4,3,2,1,0:T(8,128)(2,1)}, u32[]{:S(2)}, u32[]{:S(2)}) %collective-permute-start.1) | collective-permute-done | bytes 819232 | tf_op jit(solution)/shard_map/ppermute | solution.py:17
  57.8 2.7 collective-permute-done.7
  61.6 3.0 %broadcast_select_fusion.1 = (bf16[2,2,1,320,640]{4,3,2,1,0:T(8,128)(2,1)S(1)}, bf16[2,2,1,320,640]{4,3,2,1,0:T(8,128)(2,1)S(1)}, bf16[2,2,1,320,640]{4,3,2,1,0:T(8,128)(2,1)S(1)}, bf16[2,2,1,320,640]{4,3,2,1,0:T(8,128)(2,1)S(1)}) fusion(bf16[2,2,1,320,640]{4,3,2,1,0:T(8,128)(2,1)} %collective-permute-done.5, pred[]{:T(512)S(6)} %eq.48, ...), kind=kLoop, calls=%fused_computation.17 | loop fusion | flops 4915200 | bytes 13107201 | tf_op jit(solution)/shard_map/jit(_where)/select_n | solution.py:37
  68.8 11.7 %all-gather.2.cloned.1.call-done = bf16[512,2560]{1,0:T(8,128)(2,1)} async-done(((bf16[128,2560]{1,0:T(8,128)(2,1)}), bf16[512,2560]{1,0:T(8,128)(2,1)}) %all-gather.2.cloned.1.call-update) | async-done | bytes 2621456 | tf_op jit(solution)/shard_map/all_gather | solution.py:309
  80.6 2.6 convolution_convert_fusion.5.bo.both_ref
  83.4 5.1 %fusion.3 = bf16[512,640]{1,0:T(8,128)(2,1)S(1)} fusion(bf16[512,2560]{1,0:T(8,128)(2,1)} %all-gather.2.cloned.1.call-done, bf16[2560,640]{1,0:T(8,128)(2,1)} %bitcast.103), kind=kOutput, calls=%fused_computation.24 | convolution fusion | flops 1678049280 | bytes 6553600 | tf_op jit(solution)/shard_map/dot_general | solution.py:336
  88.4 2.2 fusion.4
  91.7 2.9 %shard_map.85 = (bf16[512,1280]{1,0:T(8,128)(2,1)S(1)}, f32[2,128,1280]{2,1,0:T(8,128)S(1)}) custom-call(bf16[512,1280]{1,0:T(8,128)(2,1)S(1)} %pad_maximum_fusion.4.x_ref.x, f32[2,2,256,10]{3,2,1,0:T(8,128)S(1)} %copy-done.2, bf16[2,128,256]{2,1,0:T(8,128)(2,1)S(1)} %get-tuple-element.61.left_ref), custom_call_target="tpu_custom_call" | custom-call | flops 167772160 | bytes 3932160 | tf_op jit(solution)/shard_map/pallas_call | solution.py:77
  120.3 2.9 %shard_map.86 = (bf16[512,1280]{1,0:T(8,128)(2,1)S(1)}, f32[2,128,1280]{2,1,0:T(8,128)S(1)}) custom-call(bf16[512,1280]{1,0:T(8,128)(2,1)S(1)} %copy-done.9, f32[2,2,256,10]{3,2,1,0:T(8,128)S(1)} %copy-done.8, bf16[2,128,256]{2,1,0:T(8,128)(2,1)S(1)} %get-tuple-element.60.left_ref), custom_call_target="tpu_custom_call" | custom-call | flops 167772160 | bytes 3932160 | tf_op jit(solution)/shard_map/pallas_call | solution.py:77
  126.8 8.2 %collective-permute-done.11 = bf16[128,1280]{1,0:T(8,128)(2,1)S(1)} collective-permute-done((bf16[128,1280]{1,0:T(8,128)(2,1)S(1)}, bf16[128,1280]{1,0:T(8,128)(2,1)S(1)}, u32[]{:S(2)}, u32[]{:S(2)}) %collective-permute-start.11) | collective-permute-done | bytes 327712 | tf_op jit(solution)/shard_map/ppermute | solution.py:17
  135.0 2.5 convert_bitcast_fusion.1
  143.2 8.5 %collective-permute-done.13 = bf16[128,1280]{1,0:T(8,128)(2,1)} collective-permute-done((bf16[128,1280]{1,0:T(8,128)(2,1)}, bf16[128,1280]{1,0:T(8,128)(2,1)}, u32[]{:S(2)}, u32[]{:S(2)}) %collective-permute-start.13) | collective-permute-done | bytes 327712 | tf_op jit(solution)/shard_map/ppermute | solution.py:17
  156.1 11.4 %shard_map.87 = (f32[512,1280]{1,0:T(8,128)}, f32[512,256]{1,0:T(8,128)S(1)}) custom-call(bf16[512,1280]{1,0:T(8,128)(2,1)S(1)} %pad_maximum_fusion.4.x_ref.x, bf16[512,1280]{1,0:T(8,128)(2,1)S(1)} %copy-done.10, f32[2,2,256,10]{3,2,1,0:T(8,128)S(1)} %bitcast.96, f32[2,2,10,256]{3,2,1,0:T(8,128)S(1)} %copy.30.cr, f32[2,2,256,10]{3,2,1,0:T(8,128)S(1)} %bitcast.97, ...), custom_call_target="tpu_custom_call" | custom-call | flops 2684354560 | bytes 5242880 | tf_op jit(solution)/shard_map/pallas_call | solution.py:159
  170.2 4.2 %shard_map.88 = (bf16[512,1280]{1,0:T(8,128)(2,1)S(1)}, f32[512,256]{1,0:T(8,128)S(1)}) custom-call(bf16[512,1280]{1,0:T(8,128)(2,1)S(1)} %copy-done.12, bf16[512,1280]{1,0:T(8,128)(2,1)} %copy-done.13, f32[512,1280]{1,0:T(8,128)} %get-tuple-element.13.part_ref, f32[2,2,256,10]{3,2,1,0:T(8,128)S(1)} %copy-done.3, ...), custom_call_target="tpu_custom_call" | custom-call | flops 503316480 | bytes 6553600 | tf_op jit(solution)/shard_map/pallas_call | solution.py:226
  174.4 3.2 %fusion.35 = f32[512,2560]{1,0:T(8,128)} fusion(bf16[2560,256]{1,0:T(8,128)(2,1)S(1)} %copy-done, f32[512,256]{1,0:T(8,128)S(1)} %get-tuple-element.18), kind=kOutput, calls=%fused_computation.98 | convolution fusion | flops 671219712 | bytes 7077888 | tf_op jit(solution)/shard_map/dot_general | solution.py:360
  181.3 6.7 %fusion.26 = f32[512,2560]{1,0:T(8,128)} fusion(bf16[2560,640]{1,0:T(8,128)(2,1)} %bitcast.107, bf16[512,1280]{1,0:T(8,128)(2,1)S(1)} %get-tuple-element.17), kind=kOutput, calls=%fused_computation.78 | convolution fusion | flops 1677721600 | bytes 9175040 | tf_op jit(solution)/shard_map/dot_general | solution.py:359
  188.0 3.6 %fusion = bf16[2560,640]{0,1:T(8,128)(2,1)} fusion(bf16[512,2560]{1,0:T(8,128)(2,1)S(1)} %copy-done.31, bf16[512,1280]{1,0:T(8,128)(2,1)S(1)} %get-tuple-element.17), kind=kOutput, calls=%fused_computation.3 | convolution fusion | flops 1679360000 | bytes 6553600 | tf_op jit(solution)/shard_map/dot_general | solution.py:367
  191.6 5.6 %copy.31 = bf16[2560,640]{1,0:T(8,128)(2,1)} copy(bf16[2560,640]{0,1:T(8,128)(2,1)} %fusion) | data formatting | bytes 6553600 | tf_op jit(solution)/shard_map/convert_element_type | solution.py:367
  197.2 2.9 %constant_dynamic-slice_fusion.10 = bf16[2,2,1,320,640]{4,3,2,1,0:T(8,128)(2,1)} fusion(bf16[2,2,2,320,640]{4,3,2,1,0:T(8,128)(2,1)} %bitcast.99, s32[]{:T(128)S(6)} %select_n.499), kind=kLoop, calls=%fused_computation.123 | loop fusion | bytes 3276804 | tf_op jit(solution)/shard_map/dynamic_slice | solution.py:50
  200.6 7.9 %add_convert_fusion = bf16[512,2560]{1,0:T(8,128)(2,1)} fusion(f32[512,2560]{1,0:T(8,128)} %fusion.35, f32[512,2560]{1,0:T(8,128)} %fusion.26, bf16[2560,640]{1,0:T(8,128)(2,1)S(1)} %bitcast.104, bf16[512,1280]{1,0:T(8,128)(2,1)S(1)} %get-tuple-element.17), kind=kOutput, calls=%fused_computation | convolution fusion | flops 1681653760 | bytes 17039360 | tf_op jit(solution)/shard_map/dot_general | solution.py:358
  208.5 5.4 %fusion.1 = bf16[2560,640]{0,1:T(8,128)(2,1)} fusion(bf16[512,2560]{1,0:T(8,128)(2,1)} %all-gather.2.cloned.1.call-done, bf16[512,1280]{1,0:T(8,128)(2,1)S(1)} %get-tuple-element.17), kind=kOutput, calls=%fused_computation.4 | convolution fusion | flops 1679360000 | bytes 6553600 | tf_op jit(solution)/shard_map/dot_general | solution.py:368
  213.9 5.6 %copy.32 = bf16[2560,640]{1,0:T(8,128)(2,1)} copy(bf16[2560,640]{0,1:T(8,128)(2,1)} %fusion.1) | data formatting | bytes 6553600 | tf_op jit(solution)/shard_map/convert_element_type | solution.py:368
  219.4 2.7 constant_dynamic-slice_fusion.7
  224.1 9.5 %collective-permute-done.22 = bf16[2,1,1,320,256]{4,3,2,1,0:T(8,128)(2,1)S(1)} collective-permute-done((bf16[2,1,1,320,256]{4,3,2,1,0:T(8,128)(2,1)S(1)}, bf16[2,1,1,320,256]{4,3,2,1,0:T(8,128)(2,1)S(1)}, u32[]{:S(2)}, u32[]{:S(2)}) %collective-permute-start.22) | collective-permute-done | bytes 327712 | tf_op jit(solution)/shard_map/ppermute | solution.py:17
  234.4 5.3 %collective-permute-done.23 = bf16[1,1,1,320,256]{4,3,2,1,0:T(8,128)(2,1)S(1)} collective-permute-done((bf16[1,1,1,320,256]{4,3,2,1,0:T(8,128)(2,1)S(1)}, bf16[1,1,1,320,256]{4,3,2,1,0:T(8,128)(2,1)S(1)}, u32[]{:S(2)}, u32[]{:S(2)}) %collective-permute-start.23) | collective-permute-done | bytes 163872 | tf_op jit(solution)/shard_map/ppermute | solution.py:17
  239.8 2.5 add_convert_fusion.2
  246.5 8.6 %collective-permute-done.24 = bf16[2,1,80,256]{3,2,1,0:T(8,128)(2,1)S(1)} collective-permute-done((bf16[2,1,80,256]{3,2,1,0:T(8,128)(2,1)S(1)}, bf16[2,1,80,256]{3,2,1,0:T(8,128)(2,1)S(1)}, u32[]{:S(2)}, u32[]{:S(2)}) %collective-permute-start.24) | collective-permute-done | bytes 81952 | tf_op jit(solution)/shard_map/ppermute | solution.py:17
  255.2 6.6 %collective-permute-done.16 = bf16[2,1,1,320,640]{4,3,2,1,0:T(8,128)(2,1)} collective-permute-done((bf16[2,1,1,320,640]{4,3,2,1,0:T(8,128)(2,1)S(1)}, bf16[2,1,1,320,640]{4,3,2,1,0:T(8,128)(2,1)}, u32[]{:S(2)}, u32[]{:S(2)}) %collective-permute-start.16) | collective-permute-done | bytes 819232 | tf_op jit(solution)/shard_map/ppermute | solution.py:17
  270.2 3.7 %collective-permute-done.17 = bf16[1,1,1,320,640]{4,3,2,1,0:T(8,128)(2,1)S(1)} collective-permute-done((bf16[1,1,1,320,640]{4,3,2,1,0:T(8,128)(2,1)S(1)}, bf16[1,1,1,320,640]{4,3,2,1,0:T(8,128)(2,1)S(1)}, u32[]{:S(2)}, u32[]{:S(2)}) %collective-permute-start.17) | collective-permute-done | bytes 409632 | tf_op jit(solution)/shard_map/ppermute | solution.py:17
  (268 shorter events, 95.6 us)
Async XLA Ops:
  7.2 73.4 %copy-start = (bf16[2560,256]{1,0:T(8,128)(2,1)S(1)}, bf16[2560,256]{1,0:T(8,128)(2,1)}, u32[]{:S(2)}) copy-start(bf16[2560,256]{1,0:T(8,128)(2,1)} %param.8) | copy-start | bytes 3932164
  7.2 15.4 %copy-start.28 = (bf16[320,1280]{1,0:T(8,128)(2,1)S(1)}, bf16[320,1280]{1,0:T(8,128)(2,1)}, u32[]{:S(2)}) copy-start(bf16[320,1280]{1,0:T(8,128)(2,1)} %param.7) | copy-start | bytes 2457604
  7.2 73.4 %all-gather.2.cloned.1.call-start = ((), (), s32[]{:S(2)}) async-start(), calls=%async_computation.1 | async-start | bytes 3276800 | tf_op jit(solution)/shard_map/all_gather | solution.py:309
  8.6 12.5 %collective-permute-start = (bf16[1,1,1,320,640]{4,3,2,1,0:T(8,128)(2,1)S(1)}, bf16[1,1,1,320,640]{4,3,2,1,0:T(8,128)(2,1)S(1)}, u32[]{:S(2)}, u32[]{:S(2)}) collective-permute-start(bf16[1,1,1,320,640]{4,3,2,1,0:T(8,128)(2,1)S(1)} %get-tuple-element.53), channel_id=1, source_target_pairs={{0,8},{4,12},{8,0},{12,4},{16,24},{20,28},{24,16},{28,20},{1,9},{5... | collective-permute-start | bytes 1228808 | tf_op jit(solution)/shard_map/ppermute | solution.py:17
  11.6 11.0 %collective-permute-start.3 = (bf16[1,1,1,320,640]{4,3,2,1,0:T(8,128)(2,1)S(1)}, bf16[1,1,1,320,640]{4,3,2,1,0:T(8,128)(2,1)}, u32[]{:S(2)}, u32[]{:S(2)}) collective-permute-start(bf16[1,1,1,320,640]{4,3,2,1,0:T(8,128)(2,1)S(1)} %get-tuple-element.54), channel_id=1, source_target_pairs={{0,16},{4,20},{8,24},{12,28},{16,0},{20,4},{24,8},{28,12},{1,17},{... | collective-permute-start | bytes 1228808 | tf_op jit(solution)/shard_map/ppermute | solution.py:17
  24.7 18.9 %collective-permute-start.1 = (bf16[1,2,1,320,640]{4,3,2,1,0:T(8,128)(2,1)S(1)}, bf16[1,2,1,320,640]{4,3,2,1,0:T(8,128)(2,1)}, u32[]{:S(2)}, u32[]{:S(2)}) collective-permute-start(bf16[1,2,1,320,640]{4,3,2,1,0:T(8,128)(2,1)S(1)} %pad_maximum_fusion.5), channel_id=1, source_target_pairs={{0,16},{4,20},{8,24},{12,28},{16,0},{20,4},{24,8},{28,12},{1,17},{... | collective-permute-start | bytes 2457608 | tf_op jit(solution)/shard_map/ppermute | solution.py:17
  26.2 251.0 %reduce-scatter.2.cloned.1.call-start = ((), (), s32[]{:S(2)}) async-start(), calls=%async_computation.2 | async-start | bytes 3276800 | tf_op jit(solution)/shard_map/reduce_scatter | solution.py:356
  29.9 18.8 %collective-permute-start.4 = (bf16[2,1,1,320,640]{4,3,2,1,0:T(8,128)(2,1)}, bf16[2,1,1,320,640]{4,3,2,1,0:T(8,128)(2,1)}, u32[]{:S(2)}, u32[]{:S(2)}) collective-permute-start(bf16[2,1,1,320,640]{4,3,2,1,0:T(8,128)(2,1)} %pad_maximum_fusion.6), channel_id=1, source_target_pairs={{0,8},{4,12},{8,0},{12,4},{16,24},{20,28},{24,16},{28,20},{1,9},{5... | collective-permute-start | bytes 2457608 | tf_op jit(solution)/shard_map/ppermute | solution.py:17
  30.9 26.0 %collective-permute-start.6 = (f32[1,1,1,1,20]{4,3,2,1,0:T(1,128)S(1)}, f32[1,1,1,1,20]{4,3,2,1,0:T(1,128)S(1)}, u32[]{:S(2)}, u32[]{:S(2)}) collective-permute-start(f32[1,1,1,1,20]{4,3,2,1,0:T(1,128)S(1)} %reshape_broadcast_in_dim.3), channel_id=1, source_target_pairs={{0,4},{4,0},{8,12},{12,8},{16,20},{20,16},{24,28},{28,24},{1,5},{5... | collective-permute-start | bytes 248 | tf_op jit(solution)/shard_map/ppermute | solution.py:17
  46.6 15.0 %collective-permute-start.2 = (bf16[2,2,1,320,640]{4,3,2,1,0:T(8,128)(2,1)}, bf16[2,2,1,320,640]{4,3,2,1,0:T(8,128)(2,1)}, u32[]{:S(2)}, u32[]{:S(2)}) collective-permute-start(bf16[2,2,1,320,640]{4,3,2,1,0:T(8,128)(2,1)} %pad_maximum_fusion.2), channel_id=1, source_target_pairs={{0,4},{4,0},{8,12},{12,8},{16,20},{20,16},{24,28},{28,24},{1,5},{5... | collective-permute-start | bytes 4915208 | tf_op jit(solution)/shard_map/ppermute | solution.py:17
  51.8 9.9 %collective-permute-start.5 = (bf16[2,2,1,320,640]{4,3,2,1,0:T(8,128)(2,1)}, bf16[2,2,1,320,640]{4,3,2,1,0:T(8,128)(2,1)}, u32[]{:S(2)}, u32[]{:S(2)}) collective-permute-start(bf16[2,2,1,320,640]{4,3,2,1,0:T(8,128)(2,1)} %pad_maximum_fusion.3), channel_id=1, source_target_pairs={{0,4},{4,0},{8,12},{12,8},{16,20},{20,16},{24,28},{28,24},{1,5},{5... | collective-permute-start | bytes 4915208 | tf_op jit(solution)/shard_map/ppermute | solution.py:17
  52.1 12.6 %copy-start.6 = (f32[2,10,2,256]{1,3,0,2:T(8,128)}, f32[2,10,2,256]{1,3,0,2:T(8,128)S(1)}, u32[]{:S(2)}) copy-start(f32[2,10,2,256]{1,3,0,2:T(8,128)S(1)} %copy.24) | copy-start | bytes 122884
  56.9 3.6 %collective-permute-start.7 = (f32[1,1,2,1,20]{4,3,2,1,0:T(1,128)S(1)}, f32[1,1,2,1,20]{4,3,2,1,0:T(1,128)S(1)}, u32[]{:S(2)}, u32[]{:S(2)}) collective-permute-start(f32[1,1,2,1,20]{4,3,2,1,0:T(1,128)S(1)} %pad_maximum_fusion.11), channel_id=1, source_target_pairs={{0,8},{4,12},{8,0},{12,4},{16,24},{20,28},{24,16},{28,20},{1,9},{5... | collective-permute-start | bytes 488 | tf_op jit(solution)/shard_map/ppermute | solution.py:17
  61.1 35.6 %collective-permute-start.8 = (f32[1,2,2,1,20]{4,3,2,1,0:T(1,128)}, f32[1,2,2,1,20]{4,3,2,1,0:T(1,128)}, u32[]{:S(2)}, u32[]{:S(2)}) collective-permute-start(f32[1,2,2,1,20]{4,3,2,1,0:T(1,128)} %pad_maximum_fusion.10), channel_id=1, source_target_pairs={{0,16},{4,20},{8,24},{12,28},{16,0},{20,4},{24,8},{28,12},{1,17},{... | collective-permute-start | bytes 968 | tf_op jit(solution)/shard_map/ppermute | solution.py:17
  96.8 3.0 %collective-permute-start.9 = (bf16[128,1280]{1,0:T(8,128)(2,1)}, bf16[128,1280]{1,0:T(8,128)(2,1)}, u32[]{:S(2)}, u32[]{:S(2)}) collective-permute-start(bf16[128,1280]{1,0:T(8,128)(2,1)} %get-tuple-element.33), channel_id=1, source_target_pairs={{0,4},{4,0},{8,12},{12,8},{16,20},{20,16},{24,28},{28,24},{1,5},{5... | collective-permute-start | bytes 983048 | tf_op jit(solution)/shard_map/ppermute | solution.py:17
  101.8 21.5 %collective-permute-start.10 = (bf16[128,1280]{1,0:T(8,128)(2,1)}, bf16[128,1280]{1,0:T(8,128)(2,1)}, u32[]{:S(2)}, u32[]{:S(2)}) collective-permute-start(bf16[128,1280]{1,0:T(8,128)(2,1)} %fusion.31), channel_id=1, source_target_pairs={{0,8},{4,12},{8,0},{12,4},{16,24},{20,28},{24,16},{28,20},{1,9},{5... | collective-permute-start | bytes 983048 | tf_op jit(solution)/shard_map/ppermute | solution.py:17
  125.1 9.9 %collective-permute-start.11 = (bf16[128,1280]{1,0:T(8,128)(2,1)S(1)}, bf16[128,1280]{1,0:T(8,128)(2,1)S(1)}, u32[]{:S(2)}, u32[]{:S(2)}) collective-permute-start(bf16[128,1280]{1,0:T(8,128)(2,1)S(1)} %fusion.13), channel_id=1, source_target_pairs={{0,16},{4,20},{8,24},{12,28},{16,0},{20,4},{24,8},{28,12},{1,17},{... | collective-permute-start | bytes 983048 | tf_op jit(solution)/shard_map/ppermute | solution.py:17
  137.6 2.0 collective-permute-start.12
  141.6 10.1 %collective-permute-start.13 = (bf16[128,1280]{1,0:T(8,128)(2,1)}, bf16[128,1280]{1,0:T(8,128)(2,1)}, u32[]{:S(2)}, u32[]{:S(2)}) collective-permute-start(bf16[128,1280]{1,0:T(8,128)(2,1)} %fusion.30), channel_id=1, source_target_pairs={{0,8},{4,12},{8,0},{12,4},{16,24},{20,28},{24,16},{28,20},{1,9},{5... | collective-permute-start | bytes 983048 | tf_op jit(solution)/shard_map/ppermute | solution.py:17
  143.2 11.6 %copy-start.7 = (f32[2,10,2,256]{1,3,0,2:T(8,128)S(1)}, f32[2,10,2,256]{1,3,0,2:T(8,128)}, u32[]{:S(2)}) copy-start(f32[2,10,2,256]{1,3,0,2:T(8,128)} %copy-done.6) | copy-start | bytes 122884
  153.2 14.3 %collective-permute-start.14 = (bf16[128,1280]{1,0:T(8,128)(2,1)S(1)}, bf16[128,1280]{1,0:T(8,128)(2,1)S(1)}, u32[]{:S(2)}, u32[]{:S(2)}) collective-permute-start(bf16[128,1280]{1,0:T(8,128)(2,1)S(1)} %fusion.22), channel_id=1, source_target_pairs={{0,16},{4,20},{8,24},{12,28},{16,0},{20,4},{24,8},{28,12},{1,17},{... | collective-permute-start | bytes 983048 | tf_op jit(solution)/shard_map/ppermute | solution.py:17
  181.2 41.0 %collective-permute-start.21 = (bf16[2,2,1,320,256]{4,3,2,1,0:T(8,128)(2,1)S(1)}, bf16[2,2,1,320,256]{4,3,2,1,0:T(8,128)(2,1)}, u32[]{:S(2)}, u32[]{:S(2)}) collective-permute-start(bf16[2,2,1,320,256]{4,3,2,1,0:T(8,128)(2,1)S(1)} %constant_dynamic-slice_fusion.4), channel_id=1, source_target_pairs={{0,4},{4,0},{8,12},{12,8},{16,20},{20,16},{24,28},{28,24},{1,5},{5... | collective-permute-start | bytes 1966088 | tf_op jit(solution)/shard_map/ppermute | solution.py:17
  200.1 39.7 %collective-permute-start.15 = (bf16[2,2,1,320,640]{4,3,2,1,0:T(8,128)(2,1)}, bf16[2,2,1,320,640]{4,3,2,1,0:T(8,128)(2,1)}, u32[]{:S(2)}, u32[]{:S(2)}) collective-permute-start(bf16[2,2,1,320,640]{4,3,2,1,0:T(8,128)(2,1)} %constant_dynamic-slice_fusion.10), channel_id=1, source_target_pairs={{0,4},{4,0},{8,12},{12,8},{16,20},{20,16},{24,28},{28,24},{1,5},{5... | collective-permute-start | bytes 4915208 | tf_op jit(solution)/shard_map/ppermute | solution.py:17
  222.2 20.9 %collective-permute-start.18 = (bf16[2,2,1,320,640]{4,3,2,1,0:T(8,128)(2,1)}, bf16[2,2,1,320,640]{4,3,2,1,0:T(8,128)(2,1)}, u32[]{:S(2)}, u32[]{:S(2)}) collective-permute-start(bf16[2,2,1,320,640]{4,3,2,1,0:T(8,128)(2,1)} %constant_dynamic-slice_fusion.7), channel_id=1, source_target_pairs={{0,4},{4,0},{8,12},{12,8},{16,20},{20,16},{24,28},{28,24},{1,5},{5... | collective-permute-start | bytes 4915208 | tf_op jit(solution)/shard_map/ppermute | solution.py:17
  223.5 10.2 %collective-permute-start.22 = (bf16[2,1,1,320,256]{4,3,2,1,0:T(8,128)(2,1)S(1)}, bf16[2,1,1,320,256]{4,3,2,1,0:T(8,128)(2,1)S(1)}, u32[]{:S(2)}, u32[]{:S(2)}) collective-permute-start(bf16[2,1,1,320,256]{4,3,2,1,0:T(8,128)(2,1)S(1)} %constant_dynamic-slice_fusion.3), channel_id=1, source_target_pairs={{0,8},{4,12},{8,0},{12,4},{16,24},{20,28},{24,16},{28,20},{1,9},{5... | collective-permute-start | bytes 983048 | tf_op jit(solution)/shard_map/ppermute | solution.py:17
  233.8 6.0 %collective-permute-start.23 = (bf16[1,1,1,320,256]{4,3,2,1,0:T(8,128)(2,1)S(1)}, bf16[1,1,1,320,256]{4,3,2,1,0:T(8,128)(2,1)S(1)}, u32[]{:S(2)}, u32[]{:S(2)}) collective-permute-start(bf16[1,1,1,320,256]{4,3,2,1,0:T(8,128)(2,1)S(1)} %constant_dynamic-slice_fusion.2), channel_id=1, source_target_pairs={{0,16},{4,20},{8,24},{12,28},{16,0},{20,4},{24,8},{28,12},{1,17},{... | collective-permute-start | bytes 491528 | tf_op jit(solution)/shard_map/ppermute | solution.py:17
  242.4 19.3 %collective-permute-start.16 = (bf16[2,1,1,320,640]{4,3,2,1,0:T(8,128)(2,1)S(1)}, bf16[2,1,1,320,640]{4,3,2,1,0:T(8,128)(2,1)}, u32[]{:S(2)}, u32[]{:S(2)}) collective-permute-start(bf16[2,1,1,320,640]{4,3,2,1,0:T(8,128)(2,1)S(1)} %constant_dynamic-slice_fusion.9), channel_id=1, source_target_pairs={{0,8},{4,12},{8,0},{12,4},{16,24},{20,28},{24,16},{28,20},{1,9},{5... | collective-permute-start | bytes 2457608 | tf_op jit(solution)/shard_map/ppermute | solution.py:17
  245.9 20.2 %collective-permute-start.19 = (bf16[1,2,1,320,640]{4,3,2,1,0:T(8,128)(2,1)}, bf16[1,2,1,320,640]{4,3,2,1,0:T(8,128)(2,1)}, u32[]{:S(2)}, u32[]{:S(2)}) collective-permute-start(bf16[1,2,1,320,640]{4,3,2,1,0:T(8,128)(2,1)} %constant_dynamic-slice_fusion.6), channel_id=1, source_target_pairs={{0,16},{4,20},{8,24},{12,28},{16,0},{20,4},{24,8},{28,12},{1,17},{... | collective-permute-start | bytes 2457608 | tf_op jit(solution)/shard_map/ppermute | solution.py:17
  246.4 8.6 %collective-permute-start.24 = (bf16[2,1,80,256]{3,2,1,0:T(8,128)(2,1)S(1)}, bf16[2,1,80,256]{3,2,1,0:T(8,128)(2,1)S(1)}, u32[]{:S(2)}, u32[]{:S(2)}) collective-permute-start(bf16[2,1,80,256]{3,2,1,0:T(8,128)(2,1)S(1)} %constant_dynamic-slice_fusion.1), channel_id=1, source_target_pairs={{0,1},{1,0},{2,3},{3,2},{4,5},{5,4},{6,7},{7,6},{8,9},{9,8},{10,11... | collective-permute-start | bytes 245768 | tf_op jit(solution)/shard_map/ppermute | solution.py:17
  255.1 14.4 %collective-permute-start.25 = (bf16[1,1,80,256]{3,2,1,0:T(8,128)(2,1)S(1)}, bf16[1,1,80,256]{3,2,1,0:T(8,128)(2,1)S(1)}, u32[]{:S(2)}, u32[]{:S(2)}) collective-permute-start(bf16[1,1,80,256]{3,2,1,0:T(8,128)(2,1)S(1)} %constant_dynamic-slice_fusion), channel_id=1, source_target_pairs={{0,2},{1,3},{2,0},{3,1},{4,6},{5,7},{6,4},{7,5},{8,10},{9,11},{10,... | collective-permute-start | bytes 122888 | tf_op jit(solution)/shard_map/ppermute | solution.py:17
  263.4 10.5 %collective-permute-start.17 = (bf16[1,1,1,320,640]{4,3,2,1,0:T(8,128)(2,1)S(1)}, bf16[1,1,1,320,640]{4,3,2,1,0:T(8,128)(2,1)S(1)}, u32[]{:S(2)}, u32[]{:S(2)}) collective-permute-start(bf16[1,1,1,320,640]{4,3,2,1,0:T(8,128)(2,1)S(1)} %constant_dynamic-slice_fusion.8), channel_id=1, source_target_pairs={{0,16},{4,20},{8,24},{12,28},{16,0},{20,4},{24,8},{28,12},{1,17},{... | collective-permute-start | bytes 1228808 | tf_op jit(solution)/shard_map/ppermute | solution.py:17
  267.5 8.4 %collective-permute-start.20 = (bf16[1,1,1,320,640]{4,3,2,1,0:T(8,128)(2,1)S(1)}, bf16[1,1,1,320,640]{4,3,2,1,0:T(8,128)(2,1)S(1)}, u32[]{:S(2)}, u32[]{:S(2)}) collective-permute-start(bf16[1,1,1,320,640]{4,3,2,1,0:T(8,128)(2,1)S(1)} %constant_dynamic-slice_fusion.5), channel_id=1, source_target_pairs={{0,8},{4,12},{8,0},{12,4},{16,24},{20,28},{24,16},{28,20},{1,9},{5... | collective-permute-start | bytes 1228808 | tf_op jit(solution)/shard_map/ppermute | solution.py:17
  (52 other events, 221.5 us)
Sparse Core Ops, SparseCore 0:
  26.4 54.1 all-gather.1
  208.6 51.2 reduce-scatter.1

commit v2 on v1

--- a/solution.py
+++ b/solution.py
@@ -248,28 +248,48 @@
     )(gated, scaled, part, weight_cols, projected, inner_grads, state_in, adjoint_in)
 
 
-def arriving(total, logs, lanes, forward):
-    peers = lax.axis_size("ctx")
+def span_logs(logs, first, last):
+    index = jnp.arange(logs.shape[0])
+    inside = ((index >= first) & (index < last))[:, None]
+    return jnp.sum(jnp.where(inside, logs, 0.0), axis=0)
+
+
+def step_logs(logs, forward):
     me = lax.axis_index("ctx")
-    index = jnp.arange(peers)
-
-    def decay(first, last):
-        inside = ((index >= first) & (index < last))[:, None]
-        return jnp.exp(lanes(jnp.sum(jnp.where(inside, logs, 0.0), axis=0)))[None, :]
-
-    entering = jnp.zeros_like(total)
+    rows = []
     for bit in bits_of("ctx"):
-        got = exchange(total.astype(jnp.bfloat16), "ctx", bit).astype(jnp.float32)
         start = (me // bit) * bit
-        upper = has_bit("ctx", bit) == 1
-        takes = upper if forward else jnp.logical_not(upper)
-        between = decay(start, me) if forward else decay(me + 1, start + bit)
-        entering = entering + jnp.where(takes, between * got, 0.0)
-        partner = start ^ bit
-        far_first = jnp.where(takes, start, partner)
-        passed = decay(far_first, far_first + bit)
-        total = jnp.where(takes, got, total) * passed + jnp.where(takes, total, got)
-    return entering
+        takes = has_bit("ctx", bit) == (1 if forward else 0)
+        far_first = jnp.where(takes, start, start ^ bit)
+        rows.append(span_logs(logs, start, me) if forward else span_logs(logs, me + 1, start + bit))
+        rows.append(span_logs(logs, far_first, far_first + bit))
+    return rows
+
+
+def arriving_step(carried, bit, between, passed, forward):
+    total, entering = carried
+    got = exchange(total.astype(jnp.bfloat16), "ctx", bit).astype(jnp.float32)
+    takes = has_bit("ctx", bit) == (1 if forward else 0)
+    entering = entering + jnp.where(takes, between[None] * got, 0.0)
+    total = jnp.where(takes, got, total) * passed[None] + jnp.where(takes, total, got)
+    return (total, entering)
+
+
+def chain_gather(shard, axis):
+    peers = lax.axis_size(axis)
+    me = lax.axis_index(axis)
+    rows = shard.shape[0]
+    full = jnp.zeros((peers * rows,) + shard.shape[1:], shard.dtype)
+    from_left = from_right = shard
+    arrived = []
+    for step in range(1, peers):
+        from_left = lax.ppermute(from_left, axis, [(i, i + 1) for i in range(peers - 1)])
+        from_right = lax.ppermute(from_right, axis, [(i, i - 1) for i in range(1, peers)])
+        arrived += [(from_left, me - step), (from_right, me + step)]
+    for piece, owner in arrived:
+        place = jnp.where((owner >= 0) & (owner < peers), owner, me)
+        full = lax.dynamic_update_slice_in_dim(full, piece, place * rows, 0)
+    return lax.dynamic_update_slice_in_dim(full, shard, me * rows, 0)
 
 
 def entering_blocks(terms, block_decay, arrived, forward):
@@ -290,6 +310,35 @@
     for block in order:
         total = terms[block] if total is None else block_decay[block][None, :] * total + terms[block]
     return total
+
+
+def product_kernel(left_ref, right_ref, out_ref):
+    out_ref[...] = jnp.dot(
+        left_ref[...], right_ref[...], preferred_element_type=jnp.float32
+    ).astype(jnp.bfloat16)
+
+
+def columns_product(left, right, first, width):
+    rows, depth = left.shape
+    tile = rows // 5
+    if width % PAIR:
+        right, first = right[:, first : first + width], 0
+    return pl.pallas_call(
+        product_kernel,
+        grid=(rows // tile,),
+        in_specs=[
+            pl.BlockSpec((tile, depth), lambda i: (i, 0)),
+            pl.BlockSpec((depth, width), lambda i: (0, first // width)),
+        ],
+        out_specs=pl.BlockSpec((tile, width), lambda i: (i, 0)),
+        out_shape=jax.ShapeDtypeStruct((rows, width), jnp.bfloat16),
+        cost_estimate=pl.CostEstimate(
+            flops=2 * rows * depth * width,
+            bytes_accessed=2 * (rows * depth + rows * width + depth * width),
+            transcendentals=0,
+        ),
+        compiler_params=pltpu.CompilerParams(vmem_limit_bytes=VMEM_LIMIT),
+    )(left, right)
 
 
 def shards(layer_input, proj_weight, state_weight, out_grad, log_decay, skip_gain):
@@ -306,42 +355,70 @@
     def lanes(per_head_values):
         return jnp.repeat(per_head_values, head_width, axis=-1)
 
-    gathered = lax.all_gather(layer_input, "sp", axis=0, tiled=True)
+    full_weight = lax.all_gather(proj_weight, "ctx", axis=0, tiled=True)
+    gathered = chain_gather(layer_input, "sp")
     half = width // 2
-    weight_a = cube_gather(proj_weight[:, :half], "ctx", high + bits[:1])
-    weight_b = cube_gather(proj_weight[:, half:], "ctx", high[::-1] + bits[:1])
 
     shaped = log_decay.reshape(groups, heads // groups, blocks, BLOCK)
     cum_rows = jnp.cumsum(shaped, axis=3).transpose(2, 0, 1, 3)
     gate_rows = jnp.sqrt(-jnp.expm1(2.0 * shaped)).transpose(2, 0, 1, 3)
     to_end_rows = jnp.exp(cum_rows[..., -1:] - cum_rows)
     block_logs = cum_rows[..., -1].reshape(blocks, heads)
-    block_decay = jnp.exp(lanes(block_logs))
     logs = cube_gather(jnp.sum(block_logs, axis=0)[None], "ctx", bits)
+    ahead, back = step_logs(logs, True), step_logs(logs, False)
+    factors = lanes(jnp.exp(jnp.stack(list(block_logs) + ahead + back)))
     cum_cols = cum_rows.transpose(0, 1, 3, 2)
     gate_cols = gate_rows.transpose(0, 1, 3, 2)
     from_start_cols = jnp.exp(cum_cols)
     gate_end_cols = (gate_rows * to_end_rows).transpose(0, 1, 3, 2)
 
+    skip_lanes = lanes(skip_gain)[None, :]
+    factors, skip_lanes, cum_cols, cum_rows, gate_cols, from_start_cols, gate_end_cols, gathered = (
+        lax.optimization_barrier(
+            (
+                factors,
+                skip_lanes,
+                cum_cols,
+                cum_rows,
+                gate_cols,
+                from_start_cols,
+                gate_end_cols,
+                gathered,
+            )
+        )
+    )
+    block_decay = factors[:blocks]
+    ahead = factors[blocks : blocks + len(ahead)]
+    back = factors[blocks + len(ahead) :]
+
+    def step(carried, number, forward):
+        rows = ahead if forward else back
+        return arriving_step(
+            carried, bits[number], rows[2 * number], rows[2 * number + 1], forward
+        )
+
     projected = jnp.dot(gathered, state_weight, preferred_element_type=jnp.float32).astype(
         jnp.bfloat16
     )
     turned = projected.reshape(blocks, BLOCK, 2 * state).transpose(0, 2, 1)
     scaled_cot, pending = weigh(out_grad, from_start_cols, turned[:, state:])
     pending = pending * scale
-    adjoint_from = arriving(piece_total(pending, block_decay, False), logs, lanes, False)
-
-    values = jnp.concatenate(
-        [
-            jnp.dot(gathered, w, preferred_element_type=jnp.float32).astype(jnp.bfloat16)
-            for w in (weight_a, weight_b)
-        ],
-        axis=1,
-    )
+    total = piece_total(pending, block_decay, False)
+    adjoint = step((total, jnp.zeros_like(total)), 0, False)
+    adjoint, gathered = lax.optimization_barrier((adjoint, gathered))
+    values = jnp.dot(gathered, full_weight, preferred_element_type=jnp.float32).astype(jnp.bfloat16)
+    adjoint = step(adjoint, 1, False)
     gated, written = weigh(values, gate_end_cols, turned[:, :state])
-    state_from = arriving(piece_total(written, block_decay, True), logs, lanes, True)
+    total = piece_total(written, block_decay, True)
+    arriving = step((total, jnp.zeros_like(total)), 0, True)
+    adjoint, arriving, values = lax.optimization_barrier((adjoint, arriving, values))
+    for number in range(2, len(bits)):
+        adjoint = step(adjoint, number, False)
+    for number in range(1, len(bits)):
+        arriving = step(arriving, number, True)
+    state_from, adjoint_from = arriving[1], adjoint[1]
     part, inner_grads = inner(
-        values, out_grad, cum_cols, cum_rows, gate_cols, lanes(skip_gain)[None, :], projected
+        values, out_grad, cum_cols, cum_rows, gate_cols, skip_lanes, projected
     )
     state_in = entering_blocks(written, block_decay, state_from, True)
     adjoint_in = entering_blocks(pending, block_decay, adjoint_from, False)
@@ -350,23 +427,18 @@
     )
     low_grads = partial_grads.astype(jnp.bfloat16)
 
+    turned_input = lax.optimization_barrier(gathered.T)
     across = (((1,), (1,)), ((), ()))
-    down = (((0,), (0,)), ((), ()))
     dot = functools.partial(lax.dot_general, preferred_element_type=jnp.float32)
-    grad_input = lax.psum_scatter(
-        (
-            dot(grad_heads[:, :half], weight_a, across)
-            + dot(grad_heads[:, half:], weight_b, across)
-            + dot(low_grads, state_weight, across)
-        ).astype(jnp.bfloat16),
-        "sp",
-        scatter_dimension=0,
-        tiled=True,
-    )
+    input_terms = (
+        dot(grad_heads, full_weight, across) + dot(low_grads, state_weight, across)
+    ).astype(jnp.bfloat16)
+    input_terms, turned_input = lax.optimization_barrier((input_terms, turned_input))
+    grad_input = lax.psum_scatter(input_terms, "sp", scatter_dimension=0, tiled=True)
     grad_scale = (gathered.shape[0] * lax.axis_size("ctx")) ** (-0.5)
-    term_a = dot(gathered, grad_heads[:, :half], down).astype(jnp.bfloat16)
-    term_b = dot(gathered, grad_heads[:, half:], down).astype(jnp.bfloat16)
-    term_s = dot(gathered, low_grads, down).astype(jnp.bfloat16)
+    term_a = columns_product(turned_input, grad_heads, 0, half)
+    term_b = columns_product(turned_input, grad_heads, half, half)
+    term_s = columns_product(turned_input, low_grads, 0, 2 * state)
     sum_a = cube_scatter(term_a, "ctx", bits[:1] + high)
     sum_b = cube_scatter(term_b, "ctx", bits[:1] + high[::-1])
     sum_s = cube_scatter(term_s, "ctx", bits)

time: 286 us -> 230 us (0.80)
  other arithmetic: 47.2 us -> 20.5 us
  matrix products: 38.5 us -> 14.2 us
  starting transfers between devices: 18.8 us -> 38.1 us
  waiting for transfers between devices: 95.1 us -> 77.6 us
  local copies, waits for them, and re-layouts: 48.4 us -> 31.4 us
  Pallas kernels: 21.4 us -> 32 us
    ppermute x26 -> x20, waiting for transfers between devices: 83.3 us -> 56.3 us  [exchange(): return lax.ppermute(array, axis, [(i, i ^ bit) for i in range(peers)])]
    dot_general x7 -> x2, matrix products: 32.7 us -> 10.9 us  [the longest x1 7.32 us: shards(): jnp.dot(gathered, full_weight, preferred_element_type=jnp.float32)]
    ppermute x0 -> x6, waiting for transfers between devices: none -> 20.5 us  [the longest x3 11.5 us: chain_gather(): lax.ppermute(from_left, axis, [(i, i + 1) for i in range(peers - 1)])]
    ppermute x0 -> x6, starting transfers between devices: none -> 19.6 us  [the longest x3 15.8 us: chain_gather(): lax.ppermute(from_left, axis, [(i, i + 1) for i in range(peers - 1)])]
    convert_element_type x3 -> x0, local copies, waits for them, and re-layouts: 12.8 us -> none  [the longest x1 5.65 us: shards(): term_a = dot(gathered, grad_heads[:, :half], down).astype(jnp.bfloat16)]
    all_gather x1, waiting for transfers between devices: 11.7 us -> 0.01 us  [shards(): full_weight = lax.all_gather(proj_weight, 'ctx', axis=0, tiled=True)]
    pallas_call x0 -> x3, Pallas kernels: none -> 10.2 us  [columns_product(): pl.pallas_call(product_kernel, grid=(rows // tile,), in_specs=[pl.BlockSp...]
    exp x20 -> x1, local copies, waits for them, and re-layouts: 9.22 us -> 0.01 us  [shards(): factors = lanes(jnp.exp(jnp.stack(list(block_logs) + ahead + back)))]
  transfers between devices with their start and end apart: 28 -> 28, of which waited for: 16 -> 15; matrix products, arithmetic and copies ran while one was open for 37% -> 16% of each run, Pallas kernels for 6% -> 10%
where the time goes in v2:
time: 230 us; the launch traced here: 229 us
  waiting for transfers between devices  77.6 us (34%)
  starting transfers between devices  38.1 us (17%)
  Pallas kernels  32 us (14%)
  local copies, waits for them, and re-layouts  31.4 us (14%)
  other arithmetic  20.5 us (9%)
  between operations  15.1 us (7%)
  matrix products  14.2 us (6%)
    ppermute x20, waiting for transfers between devices, exchange(): return lax.ppermute(array, axis, [(i, i ^ bit) for i in range(peers)])  56.3 us
    ppermute x20, starting transfers between devices, exchange(): return lax.ppermute(array, axis, [(i, i ^ bit) for i in range(peers)])  18.4 us
    ppermute x3, starting transfers between devices, chain_gather(): lax.ppermute(from_left, axis, [(i, i + 1) for i in range(peers - 1)])  15.8 us
    unnamed x85, local copies, waits for them, and re-layouts  15 us
    ppermute x3, waiting for transfers between devices, chain_gather(): lax.ppermute(from_left, axis, [(i, i + 1) for i in range(peers - 1)])  11.5 us
    pallas_call x1, Pallas kernels, inner(): pl.pallas_call(lambda x, c, cc, cr, gt, sk, bo, part, grads, mix, total:...  11.4 us
    pallas_call x3, Pallas kernels, columns_product(): pl.pallas_call(product_kernel, grid=(rows // tile,), in_specs=[pl.BlockSp...  10.2 us
    ppermute x3, waiting for transfers between devices, chain_gather(): lax.ppermute(from_right, axis, [(i, i - 1) for i in range(1, peers)])  9 us
  transfers between devices with their start and end apart: 28, of which 15 were waited for; matrix products, arithmetic and copies ran while one was open for 16% of the time, Pallas kernels for 10%

profile of v2, /device:TPU:0, one launch (start us, length us, event | category | flops | bytes accessed | tf_op | source)
XLA Modules:
  0.0 228.7 jit_solution(17319184727438964381)
XLA Ops:
  8.0 2.2 copy.23
  11.4 6.4 %collective-permute-start.3 = (bf16[128,2560]{0,1:T(8,128)(2,1)}, bf16[128,2560]{0,1:T(8,128)(2,1)}, u32[]{:S(2)}, u32[]{:S(2)}) collective-permute-start(bf16[128,2560]{0,1:T(8,128)(2,1)} %copy.23), channel_id=1, source_target_pairs={{0,1},{1,2},{2,3},{4,5},{5,6},{6,7},{8,9},{9,10},{10,11},{12,13},{... | collective-permute-start | bytes 1966088 | tf_op jit(solution)/shard_map/ppermute | solution.py:286
  17.9 2.3 %reduce-window.6 = f32[2,10,2,2,128]{4,1,2,3,0:T(8,128)S(1)} reduce-window(f32[2,10,2,2,128]{4,1,2,3,0:T(8,128)S(1)} %copy.18, f32[]{:T(128)} %constant.244.clone.1), window={size=1x1x1x1x128 pad=0_0x0_0x0_0x0_0x127_0}, to_apply=%region_0.1 | reduce-window | flops 1300480 | bytes 81924 | tf_op jit(solution)/shard_map/reduce-window
  22.7 2.0 collective-permute-start.1
  26.4 2.0 collective-permute-start.2
  31.9 4.6 %collective-permute-start.5 = (bf16[128,2560]{0,1:T(8,128)(2,1)}, bf16[128,2560]{0,1:T(8,128)(2,1)S(1)}, u32[]{:S(2)}, u32[]{:S(2)}) collective-permute-start(bf16[128,2560]{0,1:T(8,128)(2,1)} %collective-permute-done.3), channel_id=1, source_target_pairs={{0,1},{1,2},{2,3},{4,5},{5,6},{6,7},{8,9},{9,10},{10,11},{12,13},{... | collective-permute-start | bytes 1966088 | tf_op jit(solution)/shard_map/ppermute | solution.py:286
  39.4 9.0 %collective-permute-done.6 = bf16[128,2560]{0,1:T(8,128)(2,1)S(1)} collective-permute-done((bf16[128,2560]{0,1:T(8,128)(2,1)}, bf16[128,2560]{0,1:T(8,128)(2,1)S(1)}, u32[]{:S(2)}, u32[]{:S(2)}) %collective-permute-start.6) | collective-permute-done | bytes 655392 | tf_op jit(solution)/shard_map/ppermute | solution.py:287
  49.6 4.8 %collective-permute-start.7 = (bf16[128,2560]{0,1:T(8,128)(2,1)S(1)}, bf16[128,2560]{0,1:T(8,128)(2,1)S(1)}, u32[]{:S(2)}, u32[]{:S(2)}) collective-permute-start(bf16[128,2560]{0,1:T(8,128)(2,1)S(1)} %collective-permute-done.5), channel_id=1, source_target_pairs={{0,1},{1,2},{2,3},{4,5},{5,6},{6,7},{8,9},{9,10},{10,11},{12,13},{... | collective-permute-start | bytes 1966088 | tf_op jit(solution)/shard_map/ppermute | solution.py:286
  54.8 11.5 %collective-permute-done.7 = bf16[128,2560]{0,1:T(8,128)(2,1)S(1)} collective-permute-done((bf16[128,2560]{0,1:T(8,128)(2,1)S(1)}, bf16[128,2560]{0,1:T(8,128)(2,1)S(1)}, u32[]{:S(2)}, u32[]{:S(2)}) %collective-permute-start.7) | collective-permute-done | bytes 655392 | tf_op jit(solution)/shard_map/ppermute | solution.py:286
  70.9 2.9 %shard_map.85 = (bf16[512,1280]{1,0:T(8,128)(2,1)S(1)}, f32[2,128,1280]{2,1,0:T(8,128)S(1)}) custom-call(bf16[512,1280]{1,0:T(8,128)(2,1)S(1)} %copy-done.10, f32[2,2,256,10]{3,2,1,0:T(8,128)S(1)} %get-tuple-element.30.weight_ref, bf16[2,128,256]{2,1,0:T(8,128)(2,1)S(1)} %get-tuple-element.94.left_ref), custom_call_target="tpu_custom_call" | custom-call | flops 167772160 | bytes 3932160 | tf_op jit(solution)/shard_map/pallas_call | solution.py:77
  79.4 8.2 %collective-permute-done.10 = bf16[128,1280]{1,0:T(8,128)(2,1)S(1)} collective-permute-done((bf16[128,1280]{1,0:T(8,128)(2,1)S(1)}, bf16[128,1280]{1,0:T(8,128)(2,1)S(1)}, u32[]{:S(2)}, u32[]{:S(2)}) %collective-permute-start.10) | collective-permute-done | bytes 327712 | tf_op jit(solution)/shard_map/ppermute | solution.py:17
  89.3 7.3 %convolution_convert_fusion.x_ref.x = bf16[512,1280]{1,0:T(8,128)(2,1)S(1)} fusion(bf16[512,2560]{0,1:T(8,128)(2,1)} %copy-done.1, bf16[2560,1280]{1,0:T(8,128)(2,1)} %all-gather.2.cloned.1.call-done), kind=kOutput, calls=%fused_computation.3 | convolution fusion | flops 3356098560 | bytes 10485760 | tf_op jit(solution)/shard_map/dot_general | solution.py:409
  96.7 3.0 %shard_map.86 = (bf16[512,1280]{1,0:T(8,128)(2,1)S(1)}, f32[2,128,1280]{2,1,0:T(8,128)S(1)}) custom-call(bf16[512,1280]{1,0:T(8,128)(2,1)S(1)} %convolution_convert_fusion.x_ref.x, f32[2,2,256,10]{3,2,1,0:T(8,128)S(1)} %copy-done.6, bf16[2,128,256]{2,1,0:T(8,128)(2,1)S(1)} %get-tuple-element.93.left_ref), custom_call_target="tpu_custom_call" | custom-call | flops 167772160 | bytes 3932160 | tf_op jit(solution)/shard_map/pallas_call | solution.py:77
  111.1 11.4 %shard_map.87 = (f32[512,1280]{1,0:T(8,128)}, f32[512,256]{1,0:T(8,128)S(1)}) custom-call(bf16[512,1280]{1,0:T(8,128)(2,1)S(1)} %copy-done.13, bf16[512,1280]{1,0:T(8,128)(2,1)S(1)} %copy-done.11, f32[2,2,256,10]{3,2,1,0:T(8,128)S(1)} %bitcast.99, f32[2,2,10,256]{3,2,1,0:T(8,128)S(1)} %copy.27.cr, f32[2,2,256,10]{3,2,1,0:T(8,128)S(1)} %bitcast.101, ...), custom_call_target="tpu_custom_call" | custom-call | flops 2684354560 | bytes 5242880 | tf_op jit(solution)/shard_map/pallas_call | solution.py:159
  124.6 8.3 %collective-permute-done.13 = bf16[128,1280]{1,0:T(8,128)(2,1)S(1)} collective-permute-done((bf16[128,1280]{1,0:T(8,128)(2,1)S(1)}, bf16[128,1280]{1,0:T(8,128)(2,1)S(1)}, u32[]{:S(2)}, u32[]{:S(2)}) %collective-permute-start.13) | collective-permute-done | bytes 327712 | tf_op jit(solution)/shard_map/ppermute | solution.py:17
  134.6 4.5 %shard_map.88 = (bf16[512,1280]{1,0:T(8,128)(2,1)S(1)}, f32[512,256]{1,0:T(8,128)S(1)}) custom-call(bf16[512,1280]{1,0:T(8,128)(2,1)S(1)} %copy-done.16, bf16[512,1280]{1,0:T(8,128)(2,1)} %copy-done.14, f32[512,1280]{1,0:T(8,128)} %get-tuple-element.45.part_ref, f32[2,2,256,10]{3,2,1,0:T(8,128)S(1)} %copy-done.7, ...), custom_call_target="tpu_custom_call" | custom-call | flops 503316480 | bytes 6553600 | tf_op jit(solution)/shard_map/pallas_call | solution.py:226
  139.1 3.6 %fusion.38 = f32[512,2560]{1,0:T(8,128)S(1)} fusion(bf16[512,1280]{1,0:T(8,128)(2,1)S(1)} %get-tuple-element.51.right_ref, bf16[2560,1280]{1,0:T(8,128)(2,1)S(1)} %bitcast.124), kind=kOutput, calls=%fused_computation.149 | convolution fusion | flops 3355443200 | bytes 13107200 | tf_op jit(solution)/shard_map/dot_general | solution.py:434
  142.7 2.4 %add_convert_fusion = bf16[512,2560]{1,0:T(8,128)(2,1)} fusion(f32[512,2560]{1,0:T(8,128)S(1)} %fusion.38, bf16[512,256]{1,0:T(8,128)(2,1)S(1)} %convert_element_type.172.right_ref, bf16[2560,256]{1,0:T(8,128)(2,1)S(1)} %copy-done), kind=kOutput, calls=%fused_computation | convolution fusion | flops 673710080 | bytes 9437184 | tf_op jit(solution)/shard_map/dot_general | solution.py:434
  152.1 4.3 %shard_map.89 = bf16[2560,640]{1,0:T(8,128)(2,1)} custom-call(bf16[2560,512]{1,0:T(8,128)(2,1)S(1)} %bitcast.92, bf16[512,1280]{1,0:T(8,128)(2,1)S(1)} %get-tuple-element.51.right_ref), custom_call_target="tpu_custom_call" | custom-call | flops 1677721600 | bytes 6553600 | tf_op jit(solution)/shard_map/pallas_call | solution.py:326
  156.4 3.0 %constant_dynamic-slice_fusion.10 = bf16[2,2,1,320,640]{4,3,2,1,0:T(8,128)(2,1)} fusion(bf16[2,2,2,320,640]{4,3,2,1,0:T(8,128)(2,1)} %bitcast.104, s32[]{:T(128)S(6)} %select_n.498), kind=kLoop, calls=%fused_computation.87 | loop fusion | bytes 3276804 | tf_op jit(solution)/shard_map/dynamic_slice | solution.py:50
  159.9 4.3 %shard_map.90 = bf16[2560,640]{1,0:T(8,128)(2,1)} custom-call(bf16[2560,512]{1,0:T(8,128)(2,1)S(1)} %bitcast.93, bf16[512,1280]{1,0:T(8,128)(2,1)S(1)} %get-tuple-element.51.right_ref), custom_call_target="tpu_custom_call" | custom-call | flops 1677721600 | bytes 6553600 | tf_op jit(solution)/shard_map/pallas_call | solution.py:326
  164.2 2.8 %constant_dynamic-slice_fusion.7 = bf16[2,2,1,320,640]{4,3,2,1,0:T(8,128)(2,1)} fusion(bf16[2,2,2,320,640]{4,3,2,1,0:T(8,128)(2,1)} %bitcast.102, s32[]{:T(128)S(6)} %select_n.498), kind=kLoop, calls=%fused_computation.84 | loop fusion | bytes 3276804 | tf_op jit(solution)/shard_map/dynamic_slice | solution.py:50
  167.8 9.7 %collective-permute-done.22 = bf16[2,1,1,320,256]{4,3,2,1,0:T(8,128)(2,1)S(1)} collective-permute-done((bf16[2,1,1,320,256]{4,3,2,1,0:T(8,128)(2,1)S(1)}, bf16[2,1,1,320,256]{4,3,2,1,0:T(8,128)(2,1)S(1)}, u32[]{:S(2)}, u32[]{:S(2)}) %collective-permute-start.22) | collective-permute-done | bytes 327712 | tf_op jit(solution)/shard_map/ppermute | solution.py:17
  178.0 5.5 %collective-permute-done.23 = bf16[1,1,1,320,256]{4,3,2,1,0:T(8,128)(2,1)S(1)} collective-permute-done((bf16[1,1,1,320,256]{4,3,2,1,0:T(8,128)(2,1)S(1)}, bf16[1,1,1,320,256]{4,3,2,1,0:T(8,128)(2,1)S(1)}, u32[]{:S(2)}, u32[]{:S(2)}) %collective-permute-start.23) | collective-permute-done | bytes 163872 | tf_op jit(solution)/shard_map/ppermute | solution.py:17
  183.6 2.5 %add_convert_fusion.2 = bf16[2,2,1,320,640]{4,3,2,1,0:T(8,128)(2,1)S(1)} fusion(bf16[2,2,1,320,640]{4,3,2,1,0:T(8,128)(2,1)} %collective-permute-done.15, bf16[2,2,2,320,640]{4,3,2,1,0:T(8,128)(2,1)} %bitcast.105, s32[]{:T(128)S(6)} %select_n.497), kind=kLoop, calls=%fused_computation.2 | loop fusion | flops 3276800 | bytes 4915204 | tf_op jit(solution)/shard_map/convert_element_type | solution.py:53
  187.7 1.9 add_convert_fusion.1
  190.9 2.5 %collective-permute-start.24 = (bf16[2,1,80,256]{3,2,1,0:T(8,128)(2,1)S(1)}, bf16[2,1,80,256]{3,2,1,0:T(8,128)(2,1)S(1)}, u32[]{:S(2)}, u32[]{:S(2)}) collective-permute-start(bf16[2,1,80,256]{3,2,1,0:T(8,128)(2,1)S(1)} %constant_dynamic-slice_fusion.1), channel_id=1, source_target_pairs={{0,1},{1,0},{2,3},{3,2},{4,5},{5,4},{6,7},{7,6},{8,9},{9,8},{10,11... | collective-permute-start | bytes 245768 | tf_op jit(solution)/shard_map/ppermute | solution.py:17
  193.5 6.7 %collective-permute-done.24 = bf16[2,1,80,256]{3,2,1,0:T(8,128)(2,1)S(1)} collective-permute-done((bf16[2,1,80,256]{3,2,1,0:T(8,128)(2,1)S(1)}, bf16[2,1,80,256]{3,2,1,0:T(8,128)(2,1)S(1)}, u32[]{:S(2)}, u32[]{:S(2)}) %collective-permute-start.24) | collective-permute-done | bytes 81952 | tf_op jit(solution)/shard_map/ppermute | solution.py:17
  201.7 4.9 %collective-permute-done.16 = bf16[2,1,1,320,640]{4,3,2,1,0:T(8,128)(2,1)} collective-permute-done((bf16[2,1,1,320,640]{4,3,2,1,0:T(8,128)(2,1)}, bf16[2,1,1,320,640]{4,3,2,1,0:T(8,128)(2,1)}, u32[]{:S(2)}, u32[]{:S(2)}) %collective-permute-start.16) | collective-permute-done | bytes 819232 | tf_op jit(solution)/shard_map/ppermute | solution.py:17
  211.9 2.0 collective-permute-start.20
  214.5 4.0 %collective-permute-done.17 = bf16[1,1,1,320,640]{4,3,2,1,0:T(8,128)(2,1)S(1)} collective-permute-done((bf16[1,1,1,320,640]{4,3,2,1,0:T(8,128)(2,1)S(1)}, bf16[1,1,1,320,640]{4,3,2,1,0:T(8,128)(2,1)S(1)}, u32[]{:S(2)}, u32[]{:S(2)}) %collective-permute-start.17) | collective-permute-done | bytes 409632 | tf_op jit(solution)/shard_map/ppermute | solution.py:17
  218.5 2.0 collective-permute-done.20
  (210 shorter events, 61.3 us)
Async XLA Ops:
  7.2 60.7 %copy-start = (bf16[2560,256]{1,0:T(8,128)(2,1)S(1)}, bf16[2560,256]{1,0:T(8,128)(2,1)}, u32[]{:S(2)}) copy-start(bf16[2560,256]{1,0:T(8,128)(2,1)} %param.8) | copy-start | bytes 3932164
  7.2 82.1 %all-gather.2.cloned.1.call-start = ((), (), s32[]{:S(2)}) async-start(), calls=%async_computation.1 | async-start | bytes 7372800 | tf_op jit(solution)/shard_map/all_gather | solution.py:358
  7.9 214.0 %reduce-scatter.2.cloned.1.call-start = ((), (), s32[]{:S(2)}) async-start(), calls=%async_computation.2 | async-start | bytes 3276800 | tf_op jit(solution)/shard_map/reduce_scatter | solution.py:437
  10.1 20.4 %collective-permute-start.4 = (bf16[128,2560]{0,1:T(8,128)(2,1)}, bf16[128,2560]{0,1:T(8,128)(2,1)}, u32[]{:S(2)}, u32[]{:S(2)}) collective-permute-start(bf16[128,2560]{0,1:T(8,128)(2,1)} %copy.23), channel_id=1, source_target_pairs={{1,0},{2,1},{3,2},{5,4},{6,5},{7,6},{9,8},{10,9},{11,10},{13,12},{... | collective-permute-start | bytes 1966088 | tf_op jit(solution)/shard_map/ppermute | solution.py:287
  11.4 20.4 %collective-permute-start.3 = (bf16[128,2560]{0,1:T(8,128)(2,1)}, bf16[128,2560]{0,1:T(8,128)(2,1)}, u32[]{:S(2)}, u32[]{:S(2)}) collective-permute-start(bf16[128,2560]{0,1:T(8,128)(2,1)} %copy.23), channel_id=1, source_target_pairs={{0,1},{1,2},{2,3},{4,5},{5,6},{6,7},{8,9},{9,10},{10,11},{12,13},{... | collective-permute-start | bytes 1966088 | tf_op jit(solution)/shard_map/ppermute | solution.py:286
  20.9 1.8 collective-permute-start
  21.5 15.1 %copy-start.8 = (f32[2,10,2,256]{1,3,0,2:T(8,128)}, f32[2,10,2,256]{1,3,0,2:T(8,128)S(1)}, u32[]{:S(2)}) copy-start(f32[2,10,2,256]{1,3,0,2:T(8,128)S(1)} %copy.22) | copy-start | bytes 122884
  22.7 3.6 %collective-permute-start.1 = (f32[1,1,2,1,20]{4,3,2,1,0:T(1,128)S(1)}, f32[1,1,2,1,20]{4,3,2,1,0:T(1,128)S(1)}, u32[]{:S(2)}, u32[]{:S(2)}) collective-permute-start(f32[1,1,2,1,20]{4,3,2,1,0:T(1,128)S(1)} %pad_maximum_fusion.4), channel_id=1, source_target_pairs={{0,8},{4,12},{8,0},{12,4},{16,24},{20,28},{24,16},{28,20},{1,9},{5... | collective-permute-start | bytes 488 | tf_op jit(solution)/shard_map/ppermute | solution.py:17
  26.4 3.7 %collective-permute-start.2 = (f32[1,2,2,1,20]{4,3,2,1,0:T(1,128)S(1)}, f32[1,2,2,1,20]{4,3,2,1,0:T(1,128)S(1)}, u32[]{:S(2)}, u32[]{:S(2)}) collective-permute-start(f32[1,2,2,1,20]{4,3,2,1,0:T(1,128)S(1)} %pad_maximum_fusion.3), channel_id=1, source_target_pairs={{0,16},{4,20},{8,24},{12,28},{16,0},{20,4},{24,8},{28,12},{1,17},{... | collective-permute-start | bytes 968 | tf_op jit(solution)/shard_map/ppermute | solution.py:17
  30.6 17.8 %collective-permute-start.6 = (bf16[128,2560]{0,1:T(8,128)(2,1)}, bf16[128,2560]{0,1:T(8,128)(2,1)S(1)}, u32[]{:S(2)}, u32[]{:S(2)}) collective-permute-start(bf16[128,2560]{0,1:T(8,128)(2,1)} %collective-permute-done.4), channel_id=1, source_target_pairs={{1,0},{2,1},{3,2},{5,4},{6,5},{7,6},{9,8},{10,9},{11,10},{13,12},{... | collective-permute-start | bytes 1966088 | tf_op jit(solution)/shard_map/ppermute | solution.py:287
  31.9 17.8 %collective-permute-start.5 = (bf16[128,2560]{0,1:T(8,128)(2,1)}, bf16[128,2560]{0,1:T(8,128)(2,1)S(1)}, u32[]{:S(2)}, u32[]{:S(2)}) collective-permute-start(bf16[128,2560]{0,1:T(8,128)(2,1)} %collective-permute-done.3), channel_id=1, source_target_pairs={{0,1},{1,2},{2,3},{4,5},{5,6},{6,7},{8,9},{9,10},{10,11},{12,13},{... | collective-permute-start | bytes 1966088 | tf_op jit(solution)/shard_map/ppermute | solution.py:286
  48.3 18.1 %collective-permute-start.8 = (bf16[128,2560]{0,1:T(8,128)(2,1)S(1)}, bf16[128,2560]{0,1:T(8,128)(2,1)S(1)}, u32[]{:S(2)}, u32[]{:S(2)}) collective-permute-start(bf16[128,2560]{0,1:T(8,128)(2,1)S(1)} %collective-permute-done.6), channel_id=1, source_target_pairs={{1,0},{2,1},{3,2},{5,4},{6,5},{7,6},{9,8},{10,9},{11,10},{13,12},{... | collective-permute-start | bytes 1966088 | tf_op jit(solution)/shard_map/ppermute | solution.py:287
  49.6 16.6 %collective-permute-start.7 = (bf16[128,2560]{0,1:T(8,128)(2,1)S(1)}, bf16[128,2560]{0,1:T(8,128)(2,1)S(1)}, u32[]{:S(2)}, u32[]{:S(2)}) collective-permute-start(bf16[128,2560]{0,1:T(8,128)(2,1)S(1)} %collective-permute-done.5), channel_id=1, source_target_pairs={{0,1},{1,2},{2,3},{4,5},{5,6},{6,7},{8,9},{9,10},{10,11},{12,13},{... | collective-permute-start | bytes 1966088 | tf_op jit(solution)/shard_map/ppermute | solution.py:286
  75.0 1.7 collective-permute-start.9
  77.8 9.8 %collective-permute-start.10 = (bf16[128,1280]{1,0:T(8,128)(2,1)S(1)}, bf16[128,1280]{1,0:T(8,128)(2,1)S(1)}, u32[]{:S(2)}, u32[]{:S(2)}) collective-permute-start(bf16[128,1280]{1,0:T(8,128)(2,1)S(1)} %convert_element_type.158), channel_id=1, source_target_pairs={{0,8},{4,12},{8,0},{12,4},{16,24},{20,28},{24,16},{28,20},{1,9},{5... | collective-permute-start | bytes 983048 | tf_op jit(solution)/shard_map/ppermute | solution.py:17
  99.8 1.7 collective-permute-start.11
  104.1 18.4 %collective-permute-start.12 = (bf16[128,1280]{1,0:T(8,128)(2,1)}, bf16[128,1280]{1,0:T(8,128)(2,1)}, u32[]{:S(2)}, u32[]{:S(2)}) collective-permute-start(bf16[128,1280]{1,0:T(8,128)(2,1)} %convert_element_type.162), channel_id=1, source_target_pairs={{0,8},{4,12},{8,0},{12,4},{16,24},{20,28},{24,16},{28,20},{1,9},{5... | collective-permute-start | bytes 983048 | tf_op jit(solution)/shard_map/ppermute | solution.py:17
  105.8 18.5 %collective-permute-start.14 = (bf16[128,1280]{1,0:T(8,128)(2,1)}, bf16[128,1280]{1,0:T(8,128)(2,1)S(1)}, u32[]{:S(2)}, u32[]{:S(2)}) collective-permute-start(bf16[128,1280]{1,0:T(8,128)(2,1)} %fusion.4), channel_id=1, source_target_pairs={{0,16},{4,20},{8,24},{12,28},{16,0},{20,4},{24,8},{28,12},{1,17},{... | collective-permute-start | bytes 983048 | tf_op jit(solution)/shard_map/ppermute | solution.py:17
  111.1 13.2 %copy-start.34 = (f32[1280]{0:T(1024)S(1)}, f32[1280]{0:T(1024)}, u32[]{:S(2)}) copy-start(f32[1280]{0:T(1024)} %get-tuple-element.57) | copy-start | bytes 15364
  123.7 9.3 %collective-permute-start.13 = (bf16[128,1280]{1,0:T(8,128)(2,1)S(1)}, bf16[128,1280]{1,0:T(8,128)(2,1)S(1)}, u32[]{:S(2)}, u32[]{:S(2)}) collective-permute-start(bf16[128,1280]{1,0:T(8,128)(2,1)S(1)} %fusion.15), channel_id=1, source_target_pairs={{0,16},{4,20},{8,24},{12,28},{16,0},{20,4},{24,8},{28,12},{1,17},{... | collective-permute-start | bytes 983048 | tf_op jit(solution)/shard_map/ppermute | solution.py:17
  124.4 14.7 %slice-start = ((s8[6553600]{0:T(1024)(128)(4,1)}), s8[2359296]{0:T(1024)(128)(4,1)S(1)}, s32[]{:S(2)}) async-start(s8[6553600]{0:T(1024)(128)(4,1)} %bitcast.123), calls=%async_computation.3 | async-start | bytes 4718592
  150.3 16.8 %collective-permute-start.21 = (bf16[2,2,1,320,256]{4,3,2,1,0:T(8,128)(2,1)}, bf16[2,2,1,320,256]{4,3,2,1,0:T(8,128)(2,1)S(1)}, u32[]{:S(2)}, u32[]{:S(2)}) collective-permute-start(bf16[2,2,1,320,256]{4,3,2,1,0:T(8,128)(2,1)} %constant_dynamic-slice_fusion.4), channel_id=1, source_target_pairs={{0,4},{4,0},{8,12},{12,8},{16,20},{20,16},{24,28},{28,24},{1,5},{5... | collective-permute-start | bytes 1966088 | tf_op jit(solution)/shard_map/ppermute | solution.py:17
  159.4 24.1 %collective-permute-start.15 = (bf16[2,2,1,320,640]{4,3,2,1,0:T(8,128)(2,1)}, bf16[2,2,1,320,640]{4,3,2,1,0:T(8,128)(2,1)}, u32[]{:S(2)}, u32[]{:S(2)}) collective-permute-start(bf16[2,2,1,320,640]{4,3,2,1,0:T(8,128)(2,1)} %constant_dynamic-slice_fusion.10), channel_id=1, source_target_pairs={{0,4},{4,0},{8,12},{12,8},{16,20},{20,16},{24,28},{28,24},{1,5},{5... | collective-permute-start | bytes 4915208 | tf_op jit(solution)/shard_map/ppermute | solution.py:17
  167.0 20.6 %collective-permute-start.18 = (bf16[2,2,1,320,640]{4,3,2,1,0:T(8,128)(2,1)}, bf16[2,2,1,320,640]{4,3,2,1,0:T(8,128)(2,1)}, u32[]{:S(2)}, u32[]{:S(2)}) collective-permute-start(bf16[2,2,1,320,640]{4,3,2,1,0:T(8,128)(2,1)} %constant_dynamic-slice_fusion.7), channel_id=1, source_target_pairs={{0,4},{4,0},{8,12},{12,8},{16,20},{20,16},{24,28},{28,24},{1,5},{5... | collective-permute-start | bytes 4915208 | tf_op jit(solution)/shard_map/ppermute | solution.py:17
  167.4 10.1 %collective-permute-start.22 = (bf16[2,1,1,320,256]{4,3,2,1,0:T(8,128)(2,1)S(1)}, bf16[2,1,1,320,256]{4,3,2,1,0:T(8,128)(2,1)S(1)}, u32[]{:S(2)}, u32[]{:S(2)}) collective-permute-start(bf16[2,1,1,320,256]{4,3,2,1,0:T(8,128)(2,1)S(1)} %constant_dynamic-slice_fusion.3), channel_id=1, source_target_pairs={{0,8},{4,12},{8,0},{12,4},{16,24},{20,28},{24,16},{28,20},{1,9},{5... | collective-permute-start | bytes 983048 | tf_op jit(solution)/shard_map/ppermute | solution.py:17
  177.6 5.9 %collective-permute-start.23 = (bf16[1,1,1,320,256]{4,3,2,1,0:T(8,128)(2,1)S(1)}, bf16[1,1,1,320,256]{4,3,2,1,0:T(8,128)(2,1)S(1)}, u32[]{:S(2)}, u32[]{:S(2)}) collective-permute-start(bf16[1,1,1,320,256]{4,3,2,1,0:T(8,128)(2,1)S(1)} %constant_dynamic-slice_fusion.2), channel_id=1, source_target_pairs={{0,16},{4,20},{8,24},{12,28},{16,0},{20,4},{24,8},{28,12},{1,17},{... | collective-permute-start | bytes 491528 | tf_op jit(solution)/shard_map/ppermute | solution.py:17
  187.1 19.4 %collective-permute-start.16 = (bf16[2,1,1,320,640]{4,3,2,1,0:T(8,128)(2,1)}, bf16[2,1,1,320,640]{4,3,2,1,0:T(8,128)(2,1)}, u32[]{:S(2)}, u32[]{:S(2)}) collective-permute-start(bf16[2,1,1,320,640]{4,3,2,1,0:T(8,128)(2,1)} %constant_dynamic-slice_fusion.9), channel_id=1, source_target_pairs={{0,8},{4,12},{8,0},{12,4},{16,24},{20,28},{24,16},{28,20},{1,9},{5... | collective-permute-start | bytes 2457608 | tf_op jit(solution)/shard_map/ppermute | solution.py:17
  190.5 20.0 %collective-permute-start.19 = (bf16[1,2,1,320,640]{4,3,2,1,0:T(8,128)(2,1)}, bf16[1,2,1,320,640]{4,3,2,1,0:T(8,128)(2,1)}, u32[]{:S(2)}, u32[]{:S(2)}) collective-permute-start(bf16[1,2,1,320,640]{4,3,2,1,0:T(8,128)(2,1)} %constant_dynamic-slice_fusion.6), channel_id=1, source_target_pairs={{0,16},{4,20},{8,24},{12,28},{16,0},{20,4},{24,8},{28,12},{1,17},{... | collective-permute-start | bytes 2457608 | tf_op jit(solution)/shard_map/ppermute | solution.py:17
  190.9 9.2 %collective-permute-start.24 = (bf16[2,1,80,256]{3,2,1,0:T(8,128)(2,1)S(1)}, bf16[2,1,80,256]{3,2,1,0:T(8,128)(2,1)S(1)}, u32[]{:S(2)}, u32[]{:S(2)}) collective-permute-start(bf16[2,1,80,256]{3,2,1,0:T(8,128)(2,1)S(1)} %constant_dynamic-slice_fusion.1), channel_id=1, source_target_pairs={{0,1},{1,0},{2,3},{3,2},{4,5},{5,4},{6,7},{7,6},{8,9},{9,8},{10,11... | collective-permute-start | bytes 245768 | tf_op jit(solution)/shard_map/ppermute | solution.py:17
  200.2 13.7 %collective-permute-start.25 = (bf16[1,1,80,256]{3,2,1,0:T(8,128)(2,1)S(1)}, bf16[1,1,80,256]{3,2,1,0:T(8,128)(2,1)S(1)}, u32[]{:S(2)}, u32[]{:S(2)}) collective-permute-start(bf16[1,1,80,256]{3,2,1,0:T(8,128)(2,1)S(1)} %constant_dynamic-slice_fusion), channel_id=1, source_target_pairs={{0,2},{1,3},{2,0},{3,1},{4,6},{5,7},{6,4},{7,5},{8,10},{9,11},{10,... | collective-permute-start | bytes 122888 | tf_op jit(solution)/shard_map/ppermute | solution.py:17
  208.2 10.2 %collective-permute-start.17 = (bf16[1,1,1,320,640]{4,3,2,1,0:T(8,128)(2,1)S(1)}, bf16[1,1,1,320,640]{4,3,2,1,0:T(8,128)(2,1)S(1)}, u32[]{:S(2)}, u32[]{:S(2)}) collective-permute-start(bf16[1,1,1,320,640]{4,3,2,1,0:T(8,128)(2,1)S(1)} %constant_dynamic-slice_fusion.8), channel_id=1, source_target_pairs={{0,16},{4,20},{8,24},{12,28},{16,0},{20,4},{24,8},{28,12},{1,17},{... | collective-permute-start | bytes 1228808 | tf_op jit(solution)/shard_map/ppermute | solution.py:17
  211.9 8.6 %collective-permute-start.20 = (bf16[1,1,1,320,640]{4,3,2,1,0:T(8,128)(2,1)S(1)}, bf16[1,1,1,320,640]{4,3,2,1,0:T(8,128)(2,1)S(1)}, u32[]{:S(2)}, u32[]{:S(2)}) collective-permute-start(bf16[1,1,1,320,640]{4,3,2,1,0:T(8,128)(2,1)S(1)} %constant_dynamic-slice_fusion.5), channel_id=1, source_target_pairs={{0,8},{4,12},{8,0},{12,4},{16,24},{20,28},{24,16},{28,20},{1,9},{5... | collective-permute-start | bytes 1228808 | tf_op jit(solution)/shard_map/ppermute | solution.py:17
  (38 other events, 165.4 us)
Sparse Core Ops, SparseCore 0:
  9.9 49.4 all-gather.1
  150.5 54.6 reduce-scatter.1

commit v3 on v2

--- a/solution.py
+++ b/solution.py
@@ -39,19 +39,20 @@
     return array.reshape((-1,) + shard.shape[1:])
 
 
-def cube_scatter(partial, axis, order):
+def cube_scatter(keep, send, axis, order):
     bits = bits_of(axis)
-    rows = partial.shape[0] // lax.axis_size(axis)
-    array = partial.reshape((2,) * len(bits) + (rows,) + partial.shape[1:])
+    rows = 2 * keep.shape[0] // lax.axis_size(axis)
+    total = keep.astype(jnp.float32) + exchange(send, axis, 1).astype(jnp.float32)
+    total = total.reshape((2,) * (len(bits) - 1) + (rows,) + keep.shape[1:])
     for bit in order:
         dim = len(bits) - bit.bit_length()
         own = has_bit(axis, bit)
+        array = total.astype(jnp.bfloat16)
         keep = lax.dynamic_slice_in_dim(array, own, 1, dim)
         send = lax.dynamic_slice_in_dim(array, 1 - own, 1, dim)
         got = exchange(send, axis, bit)
         total = keep.astype(jnp.float32) + got.astype(jnp.float32)
-        array = total.astype(jnp.bfloat16)
-    return total.reshape((rows,) + partial.shape[1:])
+    return total.reshape((rows,) + total.shape[len(bits) :])
 
 
 def per_head(columns, pair):
@@ -187,24 +188,18 @@
 
 
 def outer_kernel(
-    scale, gated_ref, scaled_ref, part_ref, weight_ref, both_ref, inner_ref, state_ref, adjoint_ref,
-    heads_ref, grads_ref,
+    gated_ref, part_ref, weight_ref, both_ref, inner_ref, adjoint_ref, heads_ref, grads_ref
 ):
-    group = pl.program_id(1)
     state = both_ref.shape[1] // 2
     writer = both_ref[:, :state]
     adjoint = adjoint_ref[0]
-    cross = (((1,), (1,)), ((), ()))
-
-    @pl.when(group == 0)
+
+    @pl.when(pl.program_id(1) == 0)
     def _():
-        grads_ref[...] = inner_ref[...]
-
-    grads_ref[:, :state] += lax.dot_general(
-        gated_ref[...], adjoint, cross, preferred_element_type=jnp.float32
-    )
-    grads_ref[:, state:] += scale * lax.dot_general(
-        scaled_ref[...], state_ref[0], cross, preferred_element_type=jnp.float32
+        grads_ref[...] = inner_ref[:, :state]
+
+    grads_ref[...] += lax.dot_general(
+        gated_ref[...], adjoint, (((1,), (1,)), ((), ())), preferred_element_type=jnp.float32
     )
     weights = weight_ref[0, 0]
     for pair in range(gated_ref.shape[1] // PAIR):
@@ -214,7 +209,7 @@
         heads_ref[:, cols] = total.astype(jnp.bfloat16)
 
 
-def outer(gated, scaled, part, weight_cols, projected, inner_grads, state_in, adjoint_in):
+def outer(gated, part, weight_cols, projected, inner_grads, adjoint_in):
     rows, width = gated.shape
     blocks, groups, _, heads = weight_cols.shape
     cols = width // groups
@@ -222,30 +217,27 @@
     state = both // 2
     wide = pl.BlockSpec((BLOCK, cols), lambda b, g: (b, g))
     whole = pl.BlockSpec((BLOCK, both), lambda b, g: (b, 0))
-    carried = pl.BlockSpec((1, state, cols), lambda b, g: (b, 0, g))
     return pl.pallas_call(
-        functools.partial(outer_kernel, state ** (-0.5)),
+        outer_kernel,
         grid=(blocks, groups),
         in_specs=[
-            wide,
             wide,
             wide,
             pl.BlockSpec((1, 1, BLOCK, heads), lambda b, g: (b, g, 0, 0)),
             whole,
             whole,
-            carried,
-            carried,
-        ],
-        out_specs=[wide, whole],
+            pl.BlockSpec((1, state, cols), lambda b, g: (b, 0, g)),
+        ],
+        out_specs=[wide, pl.BlockSpec((BLOCK, state), lambda b, g: (b, 0))],
         out_shape=[
             jax.ShapeDtypeStruct((rows, width), jnp.bfloat16),
-            jax.ShapeDtypeStruct((rows, both), jnp.float32),
+            jax.ShapeDtypeStruct((rows, state), jnp.float32),
         ],
         cost_estimate=pl.CostEstimate(
-            flops=6 * rows * width * state, bytes_accessed=10 * rows * width, transcendentals=0
+            flops=4 * rows * width * state, bytes_accessed=8 * rows * width, transcendentals=0
         ),
         compiler_params=pltpu.CompilerParams(vmem_limit_bytes=VMEM_LIMIT),
-    )(gated, scaled, part, weight_cols, projected, inner_grads, state_in, adjoint_in)
+    )(gated, part, weight_cols, projected, inner_grads, adjoint_in)
 
 
 def span_logs(logs, first, last):
@@ -266,13 +258,15 @@
     return rows
 
 
-def arriving_step(carried, bit, between, passed, forward):
+def arriving_step(carried, bit, between, passed, forward, beside):
     total, entering = carried
-    got = exchange(total.astype(jnp.bfloat16), "ctx", bit).astype(jnp.float32)
+    got = exchange(total.astype(jnp.bfloat16), "ctx", bit)
+    got, beside = lax.optimization_barrier((got, beside))
+    got = got.astype(jnp.float32)
     takes = has_bit("ctx", bit) == (1 if forward else 0)
     entering = entering + jnp.where(takes, between[None] * got, 0.0)
     total = jnp.where(takes, got, total) * passed[None] + jnp.where(takes, total, got)
-    return (total, entering)
+    return (total, entering), beside
 
 
 def chain_gather(shard, axis):
@@ -312,33 +306,36 @@
     return total
 
 
-def product_kernel(left_ref, right_ref, out_ref):
+def product_kernel(parity_ref, left_ref, right_ref, out_ref):
     out_ref[...] = jnp.dot(
         left_ref[...], right_ref[...], preferred_element_type=jnp.float32
     ).astype(jnp.bfloat16)
 
 
-def columns_product(left, right, first, width):
+def columns_product(left, right, first, width, parity):
     rows, depth = left.shape
-    tile = rows // 5
+    tile = rows // lax.axis_size("ctx")
     if width % PAIR:
         right, first = right[:, first : first + width], 0
     return pl.pallas_call(
         product_kernel,
-        grid=(rows // tile,),
-        in_specs=[
-            pl.BlockSpec((tile, depth), lambda i: (i, 0)),
-            pl.BlockSpec((depth, width), lambda i: (0, first // width)),
-        ],
-        out_specs=pl.BlockSpec((tile, width), lambda i: (i, 0)),
-        out_shape=jax.ShapeDtypeStruct((rows, width), jnp.bfloat16),
+        grid_spec=pltpu.PrefetchScalarGridSpec(
+            num_scalar_prefetch=1,
+            grid=(rows // (2 * tile),),
+            in_specs=[
+                pl.BlockSpec((tile, depth), lambda i, parity: (2 * i + parity[0], 0)),
+                pl.BlockSpec((depth, width), lambda i, parity: (0, first // width)),
+            ],
+            out_specs=pl.BlockSpec((tile, width), lambda i, parity: (i, 0)),
+        ),
+        out_shape=jax.ShapeDtypeStruct((rows // 2, width), jnp.bfloat16),
         cost_estimate=pl.CostEstimate(
-            flops=2 * rows * depth * width,
-            bytes_accessed=2 * (rows * depth + rows * width + depth * width),
+            flops=rows * depth * width,
+            bytes_accessed=rows * depth + rows * width + 2 * depth * width,
             transcendentals=0,
         ),
         compiler_params=pltpu.CompilerParams(vmem_limit_bytes=VMEM_LIMIT),
-    )(left, right)
+    )(jnp.reshape(parity, (1,)).astype(jnp.int32), left, right)
 
 
 def shards(layer_input, proj_weight, state_weight, out_grad, log_decay, skip_gain):
@@ -391,10 +388,10 @@
     ahead = factors[blocks : blocks + len(ahead)]
     back = factors[blocks + len(ahead) :]
 
-    def step(carried, number, forward):
+    def step(carried, number, forward, beside=()):
         rows = ahead if forward else back
         return arriving_step(
-            carried, bits[number], rows[2 * number], rows[2 * number + 1], forward
+            carried, bits[number], rows[2 * number], rows[2 * number + 1], forward, beside
         )
 
     projected = jnp.dot(gathered, state_weight, preferred_element_type=jnp.float32).astype(
@@ -404,46 +401,66 @@
     scaled_cot, pending = weigh(out_grad, from_start_cols, turned[:, state:])
     pending = pending * scale
     total = piece_total(pending, block_decay, False)
-    adjoint = step((total, jnp.zeros_like(total)), 0, False)
+    adjoint, _ = step((total, jnp.zeros_like(total)), 0, False)
     adjoint, gathered = lax.optimization_barrier((adjoint, gathered))
     values = jnp.dot(gathered, full_weight, preferred_element_type=jnp.float32).astype(jnp.bfloat16)
-    adjoint = step(adjoint, 1, False)
+    adjoint, values = step(adjoint, 1, False, values)
     gated, written = weigh(values, gate_end_cols, turned[:, :state])
     total = piece_total(written, block_decay, True)
-    arriving = step((total, jnp.zeros_like(total)), 0, True)
+    arriving, _ = step((total, jnp.zeros_like(total)), 0, True)
     adjoint, arriving, values = lax.optimization_barrier((adjoint, arriving, values))
-    for number in range(2, len(bits)):
-        adjoint = step(adjoint, number, False)
-    for number in range(1, len(bits)):
-        arriving = step(arriving, number, True)
-    state_from, adjoint_from = arriving[1], adjoint[1]
     part, inner_grads = inner(
         values, out_grad, cum_cols, cum_rows, gate_cols, skip_lanes, projected
     )
-    state_in = entering_blocks(written, block_decay, state_from, True)
-    adjoint_in = entering_blocks(pending, block_decay, adjoint_from, False)
-    grad_heads, partial_grads = outer(
-        gated, scaled_cot, part, gate_end_cols, projected, inner_grads, state_in, adjoint_in
-    )
-    low_grads = partial_grads.astype(jnp.bfloat16)
-
-    turned_input = lax.optimization_barrier(gathered.T)
+    for number in range(2, len(bits)):
+        adjoint, part = step(adjoint, number, False, part)
+    for number in range(1, len(bits) - 1):
+        arriving, part = step(arriving, number, True, part)
+    adjoint_in = entering_blocks(pending, block_decay, adjoint[1], False)
+    turned_input, part = lax.optimization_barrier((gathered.T, part))
+    grad_heads, grad_writer = outer(
+        gated, part, gate_end_cols, projected, inner_grads, adjoint_in
+    )
+    own = has_bit("ctx", bits[0])
+    sends = [
+        columns_product(turned_input, grad_heads, first, half, 1 - own) for first in (0, half)
+    ]
+    arriving, (sends, grad_heads) = step(arriving, len(bits) - 1, True, (sends, grad_heads))
+    state_in = entering_blocks(written, block_decay, arriving[1], True)
+
     across = (((1,), (1,)), ((), ()))
     dot = functools.partial(lax.dot_general, preferred_element_type=jnp.float32)
+    read = jnp.einsum(
+        "bsw,bnw->bsn",
+        scaled_cot.reshape(blocks, BLOCK, width),
+        state_in,
+        preferred_element_type=jnp.float32,
+    ).reshape(-1, state)
+    grad_reader = inner_grads[:, state:] + scale * read
+    low_grads = jnp.concatenate([grad_writer, grad_reader], axis=1).astype(jnp.bfloat16)
     input_terms = (
         dot(grad_heads, full_weight, across) + dot(low_grads, state_weight, across)
     ).astype(jnp.bfloat16)
-    input_terms, turned_input = lax.optimization_barrier((input_terms, turned_input))
+    input_terms, turned_input, grad_heads, low_grads = lax.optimization_barrier(
+        (input_terms, turned_input, grad_heads, low_grads)
+    )
     grad_input = lax.psum_scatter(input_terms, "sp", scatter_dimension=0, tiled=True)
     grad_scale = (gathered.shape[0] * lax.axis_size("ctx")) ** (-0.5)
-    term_a = columns_product(turned_input, grad_heads, 0, half)
-    term_b = columns_product(turned_input, grad_heads, half, half)
-    term_s = columns_product(turned_input, low_grads, 0, 2 * state)
-    sum_a = cube_scatter(term_a, "ctx", bits[:1] + high)
-    sum_b = cube_scatter(term_b, "ctx", bits[:1] + high[::-1])
-    sum_s = cube_scatter(term_s, "ctx", bits)
+    high = bits[1:]
+    low_send = columns_product(turned_input, low_grads, 0, 2 * state, 1 - own)
+    keeps = [columns_product(turned_input, grad_heads, first, half, own) for first in (0, half)]
+    low_keep = columns_product(turned_input, low_grads, 0, 2 * state, own)
+    sum_a = cube_scatter(keeps[0], sends[0], "ctx", high)
+    sum_b = cube_scatter(keeps[1], sends[1], "ctx", high[::-1])
+    sum_s = cube_scatter(low_keep, low_send, "ctx", high)
     grad_proj = jnp.concatenate([sum_a, sum_b], axis=1) * grad_scale
-    grad_state = cube_scatter(sum_s.astype(jnp.bfloat16), "sp", bits_of("sp")) * grad_scale
+    low = sum_s.astype(jnp.bfloat16).reshape(-1, 2, sum_s.shape[0] // lax.axis_size("sp"), 2 * state)
+    pick = has_bit("sp", 1)
+    keep, send = (
+        lax.dynamic_index_in_dim(low, bit, 1, False).reshape(-1, 2 * state)
+        for bit in (pick, 1 - pick)
+    )
+    grad_state = cube_scatter(keep, send, "sp", bits_of("sp")[1:]) * grad_scale
     return (grad_input, grad_proj, grad_state)
 
 

time: 230 us -> 212 us (0.922)
  waiting for transfers between devices: 77.6 us -> 60.4 us
  other arithmetic: 20.5 us -> 26.6 us
  local copies, waits for them, and re-layouts: 31.4 us -> 26.6 us
    ppermute x20, waiting for transfers between devices: 56.3 us -> 36.2 us  [exchange(): return lax.ppermute(array, axis, [(i, i ^ bit) for i in range(peers)])]
    ppermute x3, waiting for transfers between devices: 11.5 us -> 19.5 us  [chain_gather(): lax.ppermute(from_left, axis, [(i, i + 1) for i in range(peers - 1)])]
    dynamic_slice x11 -> x7, local copies, waits for them, and re-layouts: 8.92 us -> 1.2 us  [cube_scatter(): send = lax.dynamic_slice_in_dim(array, 1 - own, 1, dim)]
    ppermute x3, waiting for transfers between devices: 9 us -> 4.01 us  [chain_gather(): lax.ppermute(from_right, axis, [(i, i - 1) for i in range(1, peers)])]
    unnamed x85 -> x67, local copies, waits for them, and re-layouts: 15 us -> 17 us
    pallas_call x4 -> x7, Pallas kernels: 14.7 us -> 14.3 us  [the longest x6 10.3 us: columns_product(): pl.pallas_call(product_kernel, grid_spec=pltpu.PrefetchScalarGridSpec(num...]
  transfers between devices with their start and end apart: 28 -> 28, of which waited for: 15 -> 13; matrix products, arithmetic and copies ran while one was open for 16% -> 20% of each run, Pallas kernels for 10% -> 13%
where the time goes in v3:
time: 212 us; the launch traced here: 211 us
  waiting for transfers between devices  60.4 us (28%)
  starting transfers between devices  36.5 us (17%)
  Pallas kernels  31.6 us (15%)
  local copies, waits for them, and re-layouts  26.6 us (13%)
  other arithmetic  26.6 us (13%)
  between operations  15 us (7%)
  matrix products  14.5 us (7%)
    ppermute x20, waiting for transfers between devices, exchange(): return lax.ppermute(array, axis, [(i, i ^ bit) for i in range(peers)])  36.2 us
    ppermute x3, waiting for transfers between devices, chain_gather(): lax.ppermute(from_left, axis, [(i, i + 1) for i in range(peers - 1)])  19.5 us
    ppermute x20, starting transfers between devices, exchange(): return lax.ppermute(array, axis, [(i, i ^ bit) for i in range(peers)])  17.9 us
    unnamed x67, local copies, waits for them, and re-layouts  17 us
    ppermute x3, starting transfers between devices, chain_gather(): lax.ppermute(from_left, axis, [(i, i + 1) for i in range(peers - 1)])  14.7 us
    pallas_call x1, Pallas kernels, inner(): pl.pallas_call(lambda x, c, cc, cr, gt, sk, bo, part, grads, mix, total:...  11.4 us
    pallas_call x6, Pallas kernels, columns_product(): pl.pallas_call(product_kernel, grid_spec=pltpu.PrefetchScalarGridSpec(num...  10.3 us
    convert_element_type x7, other arithmetic, cube_scatter(): array = total.astype(jnp.bfloat16)  8.08 us
  transfers between devices with their start and end apart: 28, of which 13 were waited for; matrix products, arithmetic and copies ran while one was open for 20% of the time, Pallas kernels for 13%

profile of v3, /device:TPU:0, one launch (start us, length us, event | category | flops | bytes accessed | tf_op | source)
XLA Modules:
  0.0 211.1 jit_solution(13611135017003588494)
XLA Ops:
  8.0 2.2 %copy.23 = bf16[128,2560]{0,1:T(8,128)(2,1)} copy(bf16[128,2560]{1,0:T(8,128)(2,1)} %param.6) | data formatting | bytes 1310720 | tf_op args[0]
  10.1 5.8 %collective-permute-start.3 = (bf16[128,2560]{0,1:T(8,128)(2,1)}, bf16[128,2560]{0,1:T(8,128)(2,1)}, u32[]{:S(2)}, u32[]{:S(2)}) collective-permute-start(bf16[128,2560]{0,1:T(8,128)(2,1)} %copy.23), channel_id=1, source_target_pairs={{0,1},{1,2},{2,3},{4,5},{5,6},{6,7},{8,9},{9,10},{10,11},{12,13},{... | collective-permute-start | bytes 1966088 | tf_op jit(solution)/shard_map/ppermute | solution.py:280
  17.3 2.3 %reduce-window.6 = f32[2,10,2,2,128]{4,1,2,3,0:T(8,128)S(1)} reduce-window(f32[2,10,2,2,128]{4,1,2,3,0:T(8,128)S(1)} %copy.18, f32[]{:T(128)} %constant.243.clone.1), window={size=1x1x1x1x128 pad=0_0x0_0x0_0x0_0x127_0}, to_apply=%region_0.1 | reduce-window | flops 1300480 | bytes 81924 | tf_op jit(solution)/shard_map/reduce-window
  23.7 1.9 collective-permute-done.1
  27.2 2.1 collective-permute-done.2
  29.8 4.6 %collective-permute-start.5 = (bf16[128,2560]{0,1:T(8,128)(2,1)}, bf16[128,2560]{0,1:T(8,128)(2,1)S(1)}, u32[]{:S(2)}, u32[]{:S(2)}) collective-permute-start(bf16[128,2560]{0,1:T(8,128)(2,1)} %collective-permute-done.3), channel_id=1, source_target_pairs={{0,1},{1,2},{2,3},{4,5},{5,6},{6,7},{8,9},{9,10},{10,11},{12,13},{... | collective-permute-start | bytes 1966088 | tf_op jit(solution)/shard_map/ppermute | solution.py:280
  38.6 9.1 %collective-permute-done.5 = bf16[128,2560]{0,1:T(8,128)(2,1)S(1)} collective-permute-done((bf16[128,2560]{0,1:T(8,128)(2,1)}, bf16[128,2560]{0,1:T(8,128)(2,1)S(1)}, u32[]{:S(2)}, u32[]{:S(2)}) %collective-permute-start.5) | collective-permute-done | bytes 655392 | tf_op jit(solution)/shard_map/ppermute | solution.py:280
  47.7 4.3 %collective-permute-start.7 = (bf16[128,2560]{0,1:T(8,128)(2,1)S(1)}, bf16[128,2560]{0,1:T(8,128)(2,1)S(1)}, u32[]{:S(2)}, u32[]{:S(2)}) collective-permute-start(bf16[128,2560]{0,1:T(8,128)(2,1)S(1)} %collective-permute-done.5), channel_id=1, source_target_pairs={{0,1},{1,2},{2,3},{4,5},{5,6},{6,7},{8,9},{9,10},{10,11},{12,13},{... | collective-permute-start | bytes 1966088 | tf_op jit(solution)/shard_map/ppermute | solution.py:280
  53.6 10.5 %collective-permute-done.7 = bf16[128,2560]{0,1:T(8,128)(2,1)S(1)} collective-permute-done((bf16[128,2560]{0,1:T(8,128)(2,1)S(1)}, bf16[128,2560]{0,1:T(8,128)(2,1)S(1)}, u32[]{:S(2)}, u32[]{:S(2)}) %collective-permute-start.7) | collective-permute-done | bytes 655392 | tf_op jit(solution)/shard_map/ppermute | solution.py:280
  64.3 4.0 %collective-permute-done.8 = bf16[128,2560]{0,1:T(8,128)(2,1)S(1)} collective-permute-done((bf16[128,2560]{0,1:T(8,128)(2,1)S(1)}, bf16[128,2560]{0,1:T(8,128)(2,1)S(1)}, u32[]{:S(2)}, u32[]{:S(2)}) %collective-permute-start.8) | collective-permute-done | bytes 655392 | tf_op jit(solution)/shard_map/ppermute | solution.py:281
  75.4 2.9 %shard_map.85 = (bf16[512,1280]{1,0:T(8,128)(2,1)S(1)}, f32[2,128,1280]{2,1,0:T(8,128)S(1)}) custom-call(bf16[512,1280]{1,0:T(8,128)(2,1)S(1)} %copy-done.11, f32[2,2,256,10]{3,2,1,0:T(8,128)S(1)} %copy-done.9, bf16[2,128,256]{2,1,0:T(8,128)(2,1)S(1)} %get-tuple-element.122.left_ref), custom_call_target="tpu_custom_call" | custom-call | flops 167772160 | bytes 3932160 | tf_op jit(solution)/shard_map/pallas_call | solution.py:78
  85.3 7.3 %convolution_convert_fusion.x_ref.x = bf16[512,1280]{1,0:T(8,128)(2,1)S(1)} fusion(bf16[512,2560]{0,1:T(8,128)(2,1)} %copy-done.2, bf16[2560,1280]{1,0:T(8,128)(2,1)} %all-gather.2.cloned.1.call-done), kind=kOutput, calls=%fused_computation.3 | convolution fusion | flops 3356098560 | bytes 10485760 | tf_op jit(solution)/shard_map/dot_general | solution.py:406
  93.9 2.9 %shard_map.86 = (bf16[512,1280]{1,0:T(8,128)(2,1)S(1)}, f32[2,128,1280]{2,1,0:T(8,128)S(1)}) custom-call(bf16[512,1280]{1,0:T(8,128)(2,1)S(1)} %convolution_convert_fusion.x_ref.x, f32[2,2,256,10]{3,2,1,0:T(8,128)S(1)} %get-tuple-element.52.weight_ref, bf16[2,128,256]{2,1,0:T(8,128)(2,1)S(1)} %get-tuple-element.121.left_ref), custom_call_target="tpu_custom_call" | custom-call | flops 167772160 | bytes 3932160 | tf_op jit(solution)/shard_map/pallas_call | solution.py:78
  97.0 2.6 %fusion.6 = f32[128,1280]{1,0:T(8,128)} fusion(f32[128,1280]{1,0:T(8,128)S(1)} %copy-done.27, bf16[128,1280]{1,0:T(8,128)(2,1)} %collective-permute-done.10, f32[1280]{0:T(1024)S(1)} %get-tuple-element.92, pred[]{:T(512)S(6)} %eq.53), kind=kLoop, calls=%fused_computation.30 | loop fusion | flops 655360 | bytes 1643521 | tf_op jit(solution)/shard_map/add | solution.py:267
  99.7 1.8 fusion.4
  109.1 11.4 %shard_map.87 = (f32[512,1280]{1,0:T(8,128)}, f32[512,256]{1,0:T(8,128)S(1)}) custom-call(bf16[512,1280]{1,0:T(8,128)(2,1)S(1)} %copy-done.14, bf16[512,1280]{1,0:T(8,128)(2,1)S(1)} %copy-done.12, f32[2,2,256,10]{3,2,1,0:T(8,128)S(1)} %bitcast.112, f32[2,2,10,256]{3,2,1,0:T(8,128)S(1)} %copy.27.cr, f32[2,2,256,10]{3,2,1,0:T(8,128)S(1)} %bitcast.114, ...), custom_call_target="tpu_custom_call" | custom-call | flops 2684354560 | bytes 5242880 | tf_op jit(solution)/shard_map/pallas_call | solution.py:160
  124.1 4.0 %shard_map.88 = (bf16[512,1280]{1,0:T(8,128)(2,1)S(1)}, f32[512,128]{1,0:T(8,128)S(1)}) custom-call(bf16[512,1280]{1,0:T(8,128)(2,1)S(1)} %copy-done.16, f32[512,1280]{1,0:T(8,128)} %get-tuple-element.67.part_ref, f32[2,2,256,10]{3,2,1,0:T(8,128)S(1)} %get-tuple-element.52.weight_ref, bf16[512,256]{1,0:T(8,128)(2,1)S(1)} %convolution_convert_fusion.1.bo.both_ref, ...), custom_call_target="tpu_custom_call" | custom-call | flops 335544320 | bytes 5242880 | tf_op jit(solution)/shard_map/pallas_call | solution.py:220
  128.1 2.9 %shard_map.90 = bf16[1280,640]{1,0:T(8,128)(2,1)} custom-call(s32[1]{0:T(128)} %bitcast.26.parity_ref, bf16[2560,512]{1,0:T(8,128)(2,1)S(1)} %bitcast.103, bf16[512,1280]{1,0:T(8,128)(2,1)S(1)} %get-tuple-element.79.right_ref), custom_call_target="tpu_custom_call" | custom-call | flops 838860800 | bytes 3604480 | tf_op jit(solution)/shard_map/pallas_call | solution.py:320
  131.0 1.8 shard_map.89
  137.9 5.0 %add_convert_fusion = bf16[512,2560]{1,0:T(8,128)(2,1)} fusion(f32[512,2560]{1,0:T(8,128)S(1)} %fusion.42, bf16[512,1280]{1,0:T(8,128)(2,1)S(1)} %get-tuple-element.79.right_ref, bf16[2560,1280]{1,0:T(8,128)(2,1)S(1)} %bitcast.142), kind=kOutput, calls=%fused_computation | convolution fusion | flops 3358064640 | bytes 15728640 | tf_op jit(solution)/shard_map/dot_general | solution.py:442
  142.9 1.7 copy-done.4
  150.9 9.2 %collective-permute-done.22 = bf16[2,1,320,256]{3,2,1,0:T(8,128)(2,1)S(1)} collective-permute-done((bf16[2,1,320,256]{3,2,1,0:T(8,128)(2,1)S(1)}, bf16[2,1,320,256]{3,2,1,0:T(8,128)(2,1)S(1)}, u32[]{:S(2)}, u32[]{:S(2)}) %collective-permute-start.22) | collective-permute-done | bytes 327712 | tf_op jit(solution)/shard_map/ppermute | solution.py:17
  161.4 1.8 copy-done.6
  163.2 1.8 shard_map.91
  165.0 1.8 shard_map.92
  166.9 1.9 add_convert_fusion.2
  169.5 1.9 add_convert_fusion.1
  174.6 6.8 %collective-permute-done.24 = bf16[160,256]{1,0:T(8,128)(2,1)S(1)} collective-permute-done((bf16[160,256]{1,0:T(8,128)(2,1)S(1)}, bf16[160,256]{1,0:T(8,128)(2,1)S(1)}, u32[]{:S(2)}, u32[]{:S(2)}) %collective-permute-start.24) | collective-permute-done | bytes 81952 | tf_op jit(solution)/shard_map/ppermute | solution.py:17
  182.4 5.9 %collective-permute-done.16 = bf16[2,1,320,640]{3,2,1,0:T(8,128)(2,1)} collective-permute-done((bf16[2,1,320,640]{3,2,1,0:T(8,128)(2,1)S(1)}, bf16[2,1,320,640]{3,2,1,0:T(8,128)(2,1)}, u32[]{:S(2)}, u32[]{:S(2)}) %collective-permute-start.16) | collective-permute-done | bytes 819232 | tf_op jit(solution)/shard_map/ppermute | solution.py:17
  193.9 2.2 %collective-permute-start.20 = (bf16[1,1,320,640]{3,2,1,0:T(8,128)(2,1)S(1)}, bf16[1,1,320,640]{3,2,1,0:T(8,128)(2,1)S(1)}, u32[]{:S(2)}, u32[]{:S(2)}) collective-permute-start(bf16[1,1,320,640]{3,2,1,0:T(8,128)(2,1)S(1)} %constant_dynamic-slice_fusion.5), channel_id=1, source_target_pairs={{0,8},{4,12},{8,0},{12,4},{16,24},{20,28},{24,16},{28,20},{1,9},{5... | collective-permute-start | bytes 1228808 | tf_op jit(solution)/shard_map/ppermute | solution.py:17
  196.8 3.6 %collective-permute-done.17 = bf16[1,1,320,640]{3,2,1,0:T(8,128)(2,1)S(1)} collective-permute-done((bf16[1,1,320,640]{3,2,1,0:T(8,128)(2,1)S(1)}, bf16[1,1,320,640]{3,2,1,0:T(8,128)(2,1)S(1)}, u32[]{:S(2)}, u32[]{:S(2)}) %collective-permute-start.17) | collective-permute-done | bytes 409632 | tf_op jit(solution)/shard_map/ppermute | solution.py:17
  200.5 2.1 collective-permute-done.20
  (194 shorter events, 66.1 us)
Async XLA Ops:
  7.2 62.5 %copy-start = (bf16[2560,256]{1,0:T(8,128)(2,1)S(1)}, bf16[2560,256]{1,0:T(8,128)(2,1)}, u32[]{:S(2)}) copy-start(bf16[2560,256]{1,0:T(8,128)(2,1)} %param.8) | copy-start | bytes 3932164
  7.2 10.0 %copy-start.29 = (f32[20,512]{1,0:T(8,128)S(1)}, f32[20,512]{1,0:T(8,128)}, u32[]{:S(2)}) copy-start(f32[20,512]{1,0:T(8,128)} %param.10) | copy-start | bytes 122884
  7.2 78.1 %all-gather.2.cloned.1.call-start = ((), (), s32[]{:S(2)}) async-start(), calls=%async_computation.1 | async-start | bytes 7372800 | tf_op jit(solution)/shard_map/all_gather | solution.py:355
  7.9 196.0 %reduce-scatter.2.cloned.1.call-start = ((), (), s32[]{:S(2)}) async-start(), calls=%async_computation.2 | async-start | bytes 3276800 | tf_op jit(solution)/shard_map/reduce_scatter | solution.py:447
  10.1 19.7 %collective-permute-start.3 = (bf16[128,2560]{0,1:T(8,128)(2,1)}, bf16[128,2560]{0,1:T(8,128)(2,1)}, u32[]{:S(2)}, u32[]{:S(2)}) collective-permute-start(bf16[128,2560]{0,1:T(8,128)(2,1)} %copy.23), channel_id=1, source_target_pairs={{0,1},{1,2},{2,3},{4,5},{5,6},{6,7},{8,9},{9,10},{10,11},{12,13},{... | collective-permute-start | bytes 1966088 | tf_op jit(solution)/shard_map/ppermute | solution.py:280
  15.9 18.5 %collective-permute-start.4 = (bf16[128,2560]{0,1:T(8,128)(2,1)}, bf16[128,2560]{0,1:T(8,128)(2,1)}, u32[]{:S(2)}, u32[]{:S(2)}) collective-permute-start(bf16[128,2560]{0,1:T(8,128)(2,1)} %copy.23), channel_id=1, source_target_pairs={{1,0},{2,1},{3,2},{5,4},{6,5},{7,6},{9,8},{10,9},{11,10},{13,12},{... | collective-permute-start | bytes 1966088 | tf_op jit(solution)/shard_map/ppermute | solution.py:281
  20.3 1.7 collective-permute-start
  22.0 3.6 %collective-permute-start.1 = (f32[1,1,2,1,20]{4,3,2,1,0:T(1,128)S(1)}, f32[1,1,2,1,20]{4,3,2,1,0:T(1,128)S(1)}, u32[]{:S(2)}, u32[]{:S(2)}) collective-permute-start(f32[1,1,2,1,20]{4,3,2,1,0:T(1,128)S(1)} %pad_maximum_fusion.4), channel_id=1, source_target_pairs={{0,8},{4,12},{8,0},{12,4},{16,24},{20,28},{24,16},{28,20},{1,9},{5... | collective-permute-start | bytes 488 | tf_op jit(solution)/shard_map/ppermute | solution.py:17
  25.7 3.7 %collective-permute-start.2 = (f32[1,2,2,1,20]{4,3,2,1,0:T(1,128)S(1)}, f32[1,2,2,1,20]{4,3,2,1,0:T(1,128)S(1)}, u32[]{:S(2)}, u32[]{:S(2)}) collective-permute-start(f32[1,2,2,1,20]{4,3,2,1,0:T(1,128)S(1)} %pad_maximum_fusion.3), channel_id=1, source_target_pairs={{0,16},{4,20},{8,24},{12,28},{16,0},{20,4},{24,8},{28,12},{1,17},{... | collective-permute-start | bytes 968 | tf_op jit(solution)/shard_map/ppermute | solution.py:17
  29.8 17.9 %collective-permute-start.5 = (bf16[128,2560]{0,1:T(8,128)(2,1)}, bf16[128,2560]{0,1:T(8,128)(2,1)S(1)}, u32[]{:S(2)}, u32[]{:S(2)}) collective-permute-start(bf16[128,2560]{0,1:T(8,128)(2,1)} %collective-permute-done.3), channel_id=1, source_target_pairs={{0,1},{1,2},{2,3},{4,5},{5,6},{6,7},{8,9},{9,10},{10,11},{12,13},{... | collective-permute-start | bytes 1966088 | tf_op jit(solution)/shard_map/ppermute | solution.py:280
  34.4 17.6 %collective-permute-start.6 = (bf16[128,2560]{0,1:T(8,128)(2,1)}, bf16[128,2560]{0,1:T(8,128)(2,1)S(1)}, u32[]{:S(2)}, u32[]{:S(2)}) collective-permute-start(bf16[128,2560]{0,1:T(8,128)(2,1)} %collective-permute-done.4), channel_id=1, source_target_pairs={{1,0},{2,1},{3,2},{5,4},{6,5},{7,6},{9,8},{10,9},{11,10},{13,12},{... | collective-permute-start | bytes 1966088 | tf_op jit(solution)/shard_map/ppermute | solution.py:281
  47.7 16.4 %collective-permute-start.7 = (bf16[128,2560]{0,1:T(8,128)(2,1)S(1)}, bf16[128,2560]{0,1:T(8,128)(2,1)S(1)}, u32[]{:S(2)}, u32[]{:S(2)}) collective-permute-start(bf16[128,2560]{0,1:T(8,128)(2,1)S(1)} %collective-permute-done.5), channel_id=1, source_target_pairs={{0,1},{1,2},{2,3},{4,5},{5,6},{6,7},{8,9},{9,10},{10,11},{12,13},{... | collective-permute-start | bytes 1966088 | tf_op jit(solution)/shard_map/ppermute | solution.py:280
  52.0 16.3 %collective-permute-start.8 = (bf16[128,2560]{0,1:T(8,128)(2,1)S(1)}, bf16[128,2560]{0,1:T(8,128)(2,1)S(1)}, u32[]{:S(2)}, u32[]{:S(2)}) collective-permute-start(bf16[128,2560]{0,1:T(8,128)(2,1)S(1)} %collective-permute-done.6), channel_id=1, source_target_pairs={{1,0},{2,1},{3,2},{5,4},{6,5},{7,6},{9,8},{10,9},{11,10},{13,12},{... | collective-permute-start | bytes 1966088 | tf_op jit(solution)/shard_map/ppermute | solution.py:281
  79.5 1.6 collective-permute-start.9
  83.8 10.1 %collective-permute-start.10 = (bf16[128,1280]{1,0:T(8,128)(2,1)}, bf16[128,1280]{1,0:T(8,128)(2,1)}, u32[]{:S(2)}, u32[]{:S(2)}) collective-permute-start(bf16[128,1280]{1,0:T(8,128)(2,1)} %convert_element_type.170), channel_id=1, source_target_pairs={{0,8},{4,12},{8,0},{12,4},{16,24},{20,28},{24,16},{28,20},{1,9},{5... | collective-permute-start | bytes 983048 | tf_op jit(solution)/shard_map/ppermute | solution.py:17
  96.9 4.5 %collective-permute-start.11 = (bf16[128,1280]{1,0:T(8,128)(2,1)S(1)}, bf16[128,1280]{1,0:T(8,128)(2,1)S(1)}, u32[]{:S(2)}, u32[]{:S(2)}) collective-permute-start(bf16[128,1280]{1,0:T(8,128)(2,1)S(1)} %fusion.26), channel_id=1, source_target_pairs={{0,4},{4,0},{8,12},{12,8},{16,20},{20,16},{24,28},{28,24},{1,5},{5... | collective-permute-start | bytes 983048 | tf_op jit(solution)/shard_map/ppermute | solution.py:17
  102.5 18.0 %collective-permute-start.13 = (bf16[128,1280]{1,0:T(8,128)(2,1)}, bf16[128,1280]{1,0:T(8,128)(2,1)}, u32[]{:S(2)}, u32[]{:S(2)}) collective-permute-start(bf16[128,1280]{1,0:T(8,128)(2,1)} %fusion.4), channel_id=1, source_target_pairs={{0,16},{4,20},{8,24},{12,28},{16,0},{20,4},{24,8},{28,12},{1,17},{... | collective-permute-start | bytes 983048 | tf_op jit(solution)/shard_map/ppermute | solution.py:17
  104.8 15.7 %collective-permute-start.12 = (bf16[128,1280]{1,0:T(8,128)(2,1)}, bf16[128,1280]{1,0:T(8,128)(2,1)}, u32[]{:S(2)}, u32[]{:S(2)}) collective-permute-start(bf16[128,1280]{1,0:T(8,128)(2,1)} %convert_element_type.175), channel_id=1, source_target_pairs={{0,8},{4,12},{8,0},{12,4},{16,24},{20,28},{24,16},{28,20},{1,9},{5... | collective-permute-start | bytes 983048 | tf_op jit(solution)/shard_map/ppermute | solution.py:17
  109.1 11.4 %copy-start.23 = (f32[128,1280]{1,0:T(8,128)S(1)}, f32[128,1280]{1,0:T(8,128)}, u32[]{:S(2)}) copy-start(f32[128,1280]{1,0:T(8,128)} %copy-done.22) | copy-start | bytes 1966084
  109.1 13.5 %copy-start.26 = (f32[128,1280]{1,0:T(8,128)S(1)}, f32[128,1280]{1,0:T(8,128)}, u32[]{:S(2)}) copy-start(f32[128,1280]{1,0:T(8,128)} %fusion.6) | copy-start | bytes 1966084
  121.8 11.1 %collective-permute-start.14 = (bf16[128,1280]{1,0:T(8,128)(2,1)S(1)}, bf16[128,1280]{1,0:T(8,128)(2,1)S(1)}, u32[]{:S(2)}, u32[]{:S(2)}) collective-permute-start(bf16[128,1280]{1,0:T(8,128)(2,1)S(1)} %fusion.12), channel_id=1, source_target_pairs={{0,16},{4,20},{8,24},{12,28},{16,0},{20,4},{24,8},{28,12},{1,17},{... | collective-permute-start | bytes 983048 | tf_op jit(solution)/shard_map/ppermute | solution.py:17
  145.6 3.4 %collective-permute-start.21 = (bf16[1280,256]{1,0:T(8,128)(2,1)S(1)}, bf16[1280,256]{1,0:T(8,128)(2,1)}, u32[]{:S(2)}, u32[]{:S(2)}) collective-permute-start(bf16[1280,256]{1,0:T(8,128)(2,1)S(1)} %shard_map.94), channel_id=1, source_target_pairs={{0,4},{4,0},{8,12},{12,8},{16,20},{20,16},{24,28},{28,24},{1,5},{5... | collective-permute-start | bytes 1966088 | tf_op jit(solution)/shard_map/ppermute | solution.py:17
  145.7 21.2 %collective-permute-start.15 = (bf16[1280,640]{1,0:T(8,128)(2,1)}, bf16[1280,640]{1,0:T(8,128)(2,1)}, u32[]{:S(2)}, u32[]{:S(2)}) collective-permute-start(bf16[1280,640]{1,0:T(8,128)(2,1)} %copy-done.10), channel_id=1, source_target_pairs={{0,4},{4,0},{8,12},{12,8},{16,20},{20,16},{24,28},{28,24},{1,5},{5... | collective-permute-start | bytes 4915208 | tf_op jit(solution)/shard_map/ppermute | solution.py:17
  150.3 9.8 %collective-permute-start.22 = (bf16[2,1,320,256]{3,2,1,0:T(8,128)(2,1)S(1)}, bf16[2,1,320,256]{3,2,1,0:T(8,128)(2,1)S(1)}, u32[]{:S(2)}, u32[]{:S(2)}) collective-permute-start(bf16[2,1,320,256]{3,2,1,0:T(8,128)(2,1)S(1)} %constant_dynamic-slice_fusion.4), channel_id=1, source_target_pairs={{0,8},{4,12},{8,0},{12,4},{16,24},{20,28},{24,16},{28,20},{1,9},{5... | collective-permute-start | bytes 983048 | tf_op jit(solution)/shard_map/ppermute | solution.py:17
  150.9 18.6 %collective-permute-start.18 = (bf16[1280,640]{1,0:T(8,128)(2,1)}, bf16[1280,640]{1,0:T(8,128)(2,1)}, u32[]{:S(2)}, u32[]{:S(2)}) collective-permute-start(bf16[1280,640]{1,0:T(8,128)(2,1)} %shard_map.90), channel_id=1, source_target_pairs={{0,4},{4,0},{8,12},{12,8},{16,20},{20,16},{24,28},{28,24},{1,5},{5... | collective-permute-start | bytes 4915208 | tf_op jit(solution)/shard_map/ppermute | solution.py:17
  160.2 6.6 %collective-permute-start.23 = (bf16[1,1,320,256]{3,2,1,0:T(8,128)(2,1)S(1)}, bf16[1,1,320,256]{3,2,1,0:T(8,128)(2,1)S(1)}, u32[]{:S(2)}, u32[]{:S(2)}) collective-permute-start(bf16[1,1,320,256]{3,2,1,0:T(8,128)(2,1)S(1)} %constant_dynamic-slice_fusion.3), channel_id=1, source_target_pairs={{0,16},{4,20},{8,24},{12,28},{16,0},{20,4},{24,8},{28,12},{1,17},{... | collective-permute-start | bytes 491528 | tf_op jit(solution)/shard_map/ppermute | solution.py:17
  168.9 19.4 %collective-permute-start.16 = (bf16[2,1,320,640]{3,2,1,0:T(8,128)(2,1)S(1)}, bf16[2,1,320,640]{3,2,1,0:T(8,128)(2,1)}, u32[]{:S(2)}, u32[]{:S(2)}) collective-permute-start(bf16[2,1,320,640]{3,2,1,0:T(8,128)(2,1)S(1)} %constant_dynamic-slice_fusion.8), channel_id=1, source_target_pairs={{0,8},{4,12},{8,0},{12,4},{16,24},{20,28},{24,16},{28,20},{1,9},{5... | collective-permute-start | bytes 2457608 | tf_op jit(solution)/shard_map/ppermute | solution.py:17
  172.3 20.2 %collective-permute-start.19 = (bf16[1,2,320,640]{3,2,1,0:T(8,128)(2,1)}, bf16[1,2,320,640]{3,2,1,0:T(8,128)(2,1)}, u32[]{:S(2)}, u32[]{:S(2)}) collective-permute-start(bf16[1,2,320,640]{3,2,1,0:T(8,128)(2,1)} %constant_dynamic-slice_fusion.6), channel_id=1, source_target_pairs={{0,16},{4,20},{8,24},{12,28},{16,0},{20,4},{24,8},{28,12},{1,17},{... | collective-permute-start | bytes 2457608 | tf_op jit(solution)/shard_map/ppermute | solution.py:17
  173.2 8.3 %collective-permute-start.24 = (bf16[160,256]{1,0:T(8,128)(2,1)S(1)}, bf16[160,256]{1,0:T(8,128)(2,1)S(1)}, u32[]{:S(2)}, u32[]{:S(2)}) collective-permute-start(bf16[160,256]{1,0:T(8,128)(2,1)S(1)} %bitcast.126), channel_id=1, source_target_pairs={{0,1},{1,0},{2,3},{3,2},{4,5},{5,4},{6,7},{7,6},{8,9},{9,8},{10,11... | collective-permute-start | bytes 245768 | tf_op jit(solution)/shard_map/ppermute | solution.py:17
  181.5 14.7 %collective-permute-start.25 = (bf16[1,80,256]{2,1,0:T(8,128)(2,1)S(1)}, bf16[1,80,256]{2,1,0:T(8,128)(2,1)S(1)}, u32[]{:S(2)}, u32[]{:S(2)}) collective-permute-start(bf16[1,80,256]{2,1,0:T(8,128)(2,1)S(1)} %constant_dynamic-slice_fusion), channel_id=1, source_target_pairs={{0,2},{1,3},{2,0},{3,1},{4,6},{5,7},{6,4},{7,5},{8,10},{9,11},{10,... | collective-permute-start | bytes 122888 | tf_op jit(solution)/shard_map/ppermute | solution.py:17
  189.9 10.4 %collective-permute-start.17 = (bf16[1,1,320,640]{3,2,1,0:T(8,128)(2,1)S(1)}, bf16[1,1,320,640]{3,2,1,0:T(8,128)(2,1)S(1)}, u32[]{:S(2)}, u32[]{:S(2)}) collective-permute-start(bf16[1,1,320,640]{3,2,1,0:T(8,128)(2,1)S(1)} %constant_dynamic-slice_fusion.7), channel_id=1, source_target_pairs={{0,16},{4,20},{8,24},{12,28},{16,0},{20,4},{24,8},{28,12},{1,17},{... | collective-permute-start | bytes 1228808 | tf_op jit(solution)/shard_map/ppermute | solution.py:17
  193.9 8.6 %collective-permute-start.20 = (bf16[1,1,320,640]{3,2,1,0:T(8,128)(2,1)S(1)}, bf16[1,1,320,640]{3,2,1,0:T(8,128)(2,1)S(1)}, u32[]{:S(2)}, u32[]{:S(2)}) collective-permute-start(bf16[1,1,320,640]{3,2,1,0:T(8,128)(2,1)S(1)} %constant_dynamic-slice_fusion.5), channel_id=1, source_target_pairs={{0,8},{4,12},{8,0},{12,4},{16,24},{20,28},{24,16},{28,20},{1,9},{5... | collective-permute-start | bytes 1228808 | tf_op jit(solution)/shard_map/ppermute | solution.py:17
  (29 other events, 65.3 us)
Sparse Core Ops, SparseCore 0:
  9.9 49.3 all-gather.1
  146.4 53.5 reduce-scatter.1

commit v4 on v3

--- a/solution.py
+++ b/solution.py
@@ -39,10 +39,10 @@
     return array.reshape((-1,) + shard.shape[1:])
 
 
-def cube_scatter(keep, send, axis, order):
+def cube_scatter(keep, got, axis, order):
     bits = bits_of(axis)
     rows = 2 * keep.shape[0] // lax.axis_size(axis)
-    total = keep.astype(jnp.float32) + exchange(send, axis, 1).astype(jnp.float32)
+    total = keep.astype(jnp.float32) + got.astype(jnp.float32)
     total = total.reshape((2,) * (len(bits) - 1) + (rows,) + keep.shape[1:])
     for bit in order:
         dim = len(bits) - bit.bit_length()
@@ -425,7 +425,9 @@
     sends = [
         columns_product(turned_input, grad_heads, first, half, 1 - own) for first in (0, half)
     ]
-    arriving, (sends, grad_heads) = step(arriving, len(bits) - 1, True, (sends, grad_heads))
+    sends, grad_heads = lax.optimization_barrier((sends, grad_heads))
+    moved = [exchange(send, "ctx", bits[0]) for send in sends]
+    arriving, grad_heads = step(arriving, len(bits) - 1, True, grad_heads)
     state_in = entering_blocks(written, block_decay, arriving[1], True)
 
     across = (((1,), (1,)), ((), ()))
@@ -447,12 +449,13 @@
     grad_input = lax.psum_scatter(input_terms, "sp", scatter_dimension=0, tiled=True)
     grad_scale = (gathered.shape[0] * lax.axis_size("ctx")) ** (-0.5)
     high = bits[1:]
+    moved, low_grads = lax.optimization_barrier((moved, low_grads))
     low_send = columns_product(turned_input, low_grads, 0, 2 * state, 1 - own)
     keeps = [columns_product(turned_input, grad_heads, first, half, own) for first in (0, half)]
     low_keep = columns_product(turned_input, low_grads, 0, 2 * state, own)
-    sum_a = cube_scatter(keeps[0], sends[0], "ctx", high)
-    sum_b = cube_scatter(keeps[1], sends[1], "ctx", high[::-1])
-    sum_s = cube_scatter(low_keep, low_send, "ctx", high)
+    sum_a = cube_scatter(keeps[0], moved[0], "ctx", high)
+    sum_b = cube_scatter(keeps[1], moved[1], "ctx", high[::-1])
+    sum_s = cube_scatter(low_keep, exchange(low_send, "ctx", bits[0]), "ctx", high)
     grad_proj = jnp.concatenate([sum_a, sum_b], axis=1) * grad_scale
     low = sum_s.astype(jnp.bfloat16).reshape(-1, 2, sum_s.shape[0] // lax.axis_size("sp"), 2 * state)
     pick = has_bit("sp", 1)
@@ -460,7 +463,7 @@
         lax.dynamic_index_in_dim(low, bit, 1, False).reshape(-1, 2 * state)
         for bit in (pick, 1 - pick)
     )
-    grad_state = cube_scatter(keep, send, "sp", bits_of("sp")[1:]) * grad_scale
+    grad_state = cube_scatter(keep, exchange(send, "sp", 1), "sp", bits_of("sp")[1:]) * grad_scale
     return (grad_input, grad_proj, grad_state)
 
 

time: 212 us -> 209 us (0.986)
  local copies, waits for them, and re-layouts: 26.6 us -> 21.5 us
  other arithmetic: 26.6 us -> 22.5 us
  waiting for transfers between devices: 60.4 us -> 63 us
  starting transfers between devices: 36.5 us -> 38.9 us
    unnamed x67 -> x59, local copies, waits for them, and re-layouts: 17 us -> 12.9 us
    convert_element_type x7, other arithmetic: 8.08 us -> 4.44 us  [cube_scatter(): array = total.astype(jnp.bfloat16)]
    ppermute x20, waiting for transfers between devices: 36.2 us -> 38.7 us  [exchange(): return lax.ppermute(array, axis, [(i, i ^ bit) for i in range(peers)])]
    ppermute x20, starting transfers between devices: 17.9 us -> 20.3 us  [exchange(): return lax.ppermute(array, axis, [(i, i ^ bit) for i in range(peers)])]
  transfers between devices with their start and end apart: 28 -> 28, of which waited for: 13 -> 12; matrix products, arithmetic and copies ran while one was open for 20% -> 22% of each run, Pallas kernels for 13% -> 14%
where the time goes in v4:
time: 209 us; the launch traced here: 208 us
  waiting for transfers between devices  63 us (30%)
  starting transfers between devices  38.9 us (19%)
  Pallas kernels  32.7 us (16%)
  other arithmetic  22.5 us (11%)
  local copies, waits for them, and re-layouts  21.5 us (10%)
  between operations  14.9 us (7%)
  matrix products  14.5 us (7%)
    ppermute x20, waiting for transfers between devices, exchange(): return lax.ppermute(array, axis, [(i, i ^ bit) for i in range(peers)])  38.7 us
    ppermute x20, starting transfers between devices, exchange(): return lax.ppermute(array, axis, [(i, i ^ bit) for i in range(peers)])  20.3 us
    ppermute x3, waiting for transfers between devices, chain_gather(): lax.ppermute(from_left, axis, [(i, i + 1) for i in range(peers - 1)])  19.5 us
    ppermute x3, starting transfers between devices, chain_gather(): lax.ppermute(from_left, axis, [(i, i + 1) for i in range(peers - 1)])  14.7 us
    unnamed x59, local copies, waits for them, and re-layouts  12.9 us
    pallas_call x1, Pallas kernels, inner(): pl.pallas_call(lambda x, c, cc, cr, gt, sk, bo, part, grads, mix, total:...  11.4 us
    pallas_call x6, Pallas kernels, columns_product(): pl.pallas_call(product_kernel, grid_spec=pltpu.PrefetchScalarGridSpec(num...  11.4 us
    dot_general x1, matrix products, shards(): jnp.dot(gathered, full_weight, preferred_element_type=jnp.float32)  7.28 us
  transfers between devices with their start and end apart: 28, of which 12 were waited for; matrix products, arithmetic and copies ran while one was open for 22% of the time, Pallas kernels for 14%

profile of v4, /device:TPU:0, one launch (start us, length us, event | category | flops | bytes accessed | tf_op | source)
XLA Modules:
  0.0 208.0 jit_solution(6345734766691849441)
XLA Ops:
  8.0 2.2 %copy.23 = bf16[128,2560]{0,1:T(8,128)(2,1)} copy(bf16[128,2560]{1,0:T(8,128)(2,1)} %param.6) | data formatting | bytes 1310720 | tf_op args[0]
  10.1 5.8 %collective-permute-start.3 = (bf16[128,2560]{0,1:T(8,128)(2,1)}, bf16[128,2560]{0,1:T(8,128)(2,1)}, u32[]{:S(2)}, u32[]{:S(2)}) collective-permute-start(bf16[128,2560]{0,1:T(8,128)(2,1)} %copy.23), channel_id=1, source_target_pairs={{0,1},{1,2},{2,3},{4,5},{5,6},{6,7},{8,9},{9,10},{10,11},{12,13},{... | collective-permute-start | bytes 1966088 | tf_op jit(solution)/shard_map/ppermute | solution.py:280
  17.3 2.3 %reduce-window.6 = f32[2,10,2,2,128]{4,1,2,3,0:T(8,128)S(1)} reduce-window(f32[2,10,2,2,128]{4,1,2,3,0:T(8,128)S(1)} %copy.18, f32[]{:T(128)} %constant.243.clone.1), window={size=1x1x1x1x128 pad=0_0x0_0x0_0x0_0x127_0}, to_apply=%region_0.1 | reduce-window | flops 1300480 | bytes 81924 | tf_op jit(solution)/shard_map/reduce-window
  23.7 1.9 collective-permute-done.1
  27.2 2.1 collective-permute-done.2
  29.8 4.6 %collective-permute-start.5 = (bf16[128,2560]{0,1:T(8,128)(2,1)}, bf16[128,2560]{0,1:T(8,128)(2,1)S(1)}, u32[]{:S(2)}, u32[]{:S(2)}) collective-permute-start(bf16[128,2560]{0,1:T(8,128)(2,1)} %collective-permute-done.3), channel_id=1, source_target_pairs={{0,1},{1,2},{2,3},{4,5},{5,6},{6,7},{8,9},{9,10},{10,11},{12,13},{... | collective-permute-start | bytes 1966088 | tf_op jit(solution)/shard_map/ppermute | solution.py:280
  38.6 9.1 %collective-permute-done.5 = bf16[128,2560]{0,1:T(8,128)(2,1)S(1)} collective-permute-done((bf16[128,2560]{0,1:T(8,128)(2,1)}, bf16[128,2560]{0,1:T(8,128)(2,1)S(1)}, u32[]{:S(2)}, u32[]{:S(2)}) %collective-permute-start.5) | collective-permute-done | bytes 655392 | tf_op jit(solution)/shard_map/ppermute | solution.py:280
  47.7 4.3 %collective-permute-start.7 = (bf16[128,2560]{0,1:T(8,128)(2,1)S(1)}, bf16[128,2560]{0,1:T(8,128)(2,1)S(1)}, u32[]{:S(2)}, u32[]{:S(2)}) collective-permute-start(bf16[128,2560]{0,1:T(8,128)(2,1)S(1)} %collective-permute-done.5), channel_id=1, source_target_pairs={{0,1},{1,2},{2,3},{4,5},{5,6},{6,7},{8,9},{9,10},{10,11},{12,13},{... | collective-permute-start | bytes 1966088 | tf_op jit(solution)/shard_map/ppermute | solution.py:280
  53.6 10.5 %collective-permute-done.7 = bf16[128,2560]{0,1:T(8,128)(2,1)S(1)} collective-permute-done((bf16[128,2560]{0,1:T(8,128)(2,1)S(1)}, bf16[128,2560]{0,1:T(8,128)(2,1)S(1)}, u32[]{:S(2)}, u32[]{:S(2)}) %collective-permute-start.7) | collective-permute-done | bytes 655392 | tf_op jit(solution)/shard_map/ppermute | solution.py:280
  64.3 4.0 %collective-permute-done.8 = bf16[128,2560]{0,1:T(8,128)(2,1)S(1)} collective-permute-done((bf16[128,2560]{0,1:T(8,128)(2,1)S(1)}, bf16[128,2560]{0,1:T(8,128)(2,1)S(1)}, u32[]{:S(2)}, u32[]{:S(2)}) %collective-permute-start.8) | collective-permute-done | bytes 655392 | tf_op jit(solution)/shard_map/ppermute | solution.py:281
  75.4 2.9 %shard_map.85 = (bf16[512,1280]{1,0:T(8,128)(2,1)S(1)}, f32[2,128,1280]{2,1,0:T(8,128)S(1)}) custom-call(bf16[512,1280]{1,0:T(8,128)(2,1)S(1)} %copy-done.8, f32[2,2,256,10]{3,2,1,0:T(8,128)S(1)} %copy-done.7, bf16[2,128,256]{2,1,0:T(8,128)(2,1)S(1)} %get-tuple-element.130.left_ref), custom_call_target="tpu_custom_call" | custom-call | flops 167772160 | bytes 3932160 | tf_op jit(solution)/shard_map/pallas_call | solution.py:78
  79.4 1.6 collective-permute-done.9
  85.2 7.3 %convolution_convert_fusion.x_ref.x = bf16[512,1280]{1,0:T(8,128)(2,1)S(1)} fusion(bf16[512,2560]{0,1:T(8,128)(2,1)} %copy-done.2, bf16[2560,1280]{1,0:T(8,128)(2,1)} %all-gather.2.cloned.1.call-done), kind=kOutput, calls=%fused_computation.3 | convolution fusion | flops 3356098560 | bytes 10485760 | tf_op jit(solution)/shard_map/dot_general | solution.py:406
  93.8 2.9 %shard_map.86 = (bf16[512,1280]{1,0:T(8,128)(2,1)S(1)}, f32[2,128,1280]{2,1,0:T(8,128)S(1)}) custom-call(bf16[512,1280]{1,0:T(8,128)(2,1)S(1)} %convolution_convert_fusion.x_ref.x, f32[2,2,256,10]{3,2,1,0:T(8,128)S(1)} %get-tuple-element.56.weight_ref, bf16[2,128,256]{2,1,0:T(8,128)(2,1)S(1)} %get-tuple-element.129.left_ref), custom_call_target="tpu_custom_call" | custom-call | flops 167772160 | bytes 3932160 | tf_op jit(solution)/shard_map/pallas_call | solution.py:78
  97.0 2.7 %fusion.6 = f32[128,1280]{1,0:T(8,128)} fusion(f32[128,1280]{1,0:T(8,128)S(1)} %copy-done.23, bf16[128,1280]{1,0:T(8,128)(2,1)} %collective-permute-done.10, f32[1280]{0:T(1024)S(1)} %get-tuple-element.100, pred[]{:T(512)S(6)} %eq.53), kind=kLoop, calls=%fused_computation.30 | loop fusion | flops 655360 | bytes 1643521 | tf_op jit(solution)/shard_map/add | solution.py:267
  99.7 1.8 fusion.4
  109.1 11.4 %shard_map.87 = (f32[512,1280]{1,0:T(8,128)}, f32[512,256]{1,0:T(8,128)S(1)}) custom-call(bf16[512,1280]{1,0:T(8,128)(2,1)S(1)} %copy-done.11, bf16[512,1280]{1,0:T(8,128)(2,1)S(1)} %copy-done.9, f32[2,2,256,10]{3,2,1,0:T(8,128)S(1)} %bitcast.112, f32[2,2,10,256]{3,2,1,0:T(8,128)S(1)} %copy.27.cr, f32[2,2,256,10]{3,2,1,0:T(8,128)S(1)} %bitcast.114, ...), custom_call_target="tpu_custom_call" | custom-call | flops 2684354560 | bytes 5242880 | tf_op jit(solution)/shard_map/pallas_call | solution.py:160
  124.1 4.0 %shard_map.88 = (bf16[512,1280]{1,0:T(8,128)(2,1)S(1)}, f32[512,128]{1,0:T(8,128)S(1)}) custom-call(bf16[512,1280]{1,0:T(8,128)(2,1)S(1)} %copy-done.13, f32[512,1280]{1,0:T(8,128)} %get-tuple-element.71.part_ref, f32[2,2,256,10]{3,2,1,0:T(8,128)S(1)} %get-tuple-element.56.weight_ref, bf16[512,256]{1,0:T(8,128)(2,1)S(1)} %convolution_convert_fusion.1.bo.both_ref, ...), custom_call_target="tpu_custom_call" | custom-call | flops 335544320 | bytes 5242880 | tf_op jit(solution)/shard_map/pallas_call | solution.py:220
  128.1 2.9 %shard_map.90 = bf16[1280,640]{1,0:T(8,128)(2,1)} custom-call(s32[1]{0:T(128)} %bitcast.26.parity_ref, bf16[2560,512]{1,0:T(8,128)(2,1)S(1)} %bitcast.103, bf16[512,1280]{1,0:T(8,128)(2,1)S(1)} %get-tuple-element.84.right_ref), custom_call_target="tpu_custom_call" | custom-call | flops 838860800 | bytes 3604480 | tf_op jit(solution)/shard_map/pallas_call | solution.py:320
  131.0 2.9 %shard_map.89 = bf16[1280,640]{1,0:T(8,128)(2,1)} custom-call(s32[1]{0:T(128)} %bitcast.26.parity_ref, bf16[2560,512]{1,0:T(8,128)(2,1)S(1)} %bitcast.104, bf16[512,1280]{1,0:T(8,128)(2,1)S(1)} %get-tuple-element.84.right_ref), custom_call_target="tpu_custom_call" | custom-call | flops 838860800 | bytes 3604480 | tf_op jit(solution)/shard_map/pallas_call | solution.py:320
  138.8 4.9 %add_convert_fusion = bf16[512,2560]{1,0:T(8,128)(2,1)} fusion(f32[512,2560]{1,0:T(8,128)S(1)} %fusion.42, bf16[512,1280]{1,0:T(8,128)(2,1)S(1)} %get-tuple-element.84.right_ref, bf16[2560,1280]{1,0:T(8,128)(2,1)S(1)} %bitcast.142), kind=kOutput, calls=%fused_computation | convolution fusion | flops 3358064640 | bytes 15728640 | tf_op jit(solution)/shard_map/dot_general | solution.py:444
  143.8 1.7 copy-done.4
  145.6 1.8 shard_map.91
  147.4 1.8 shard_map.92
  150.4 1.9 add_convert_fusion.2
  153.0 1.8 add_convert_fusion.1
  158.9 14.5 %collective-permute-done.17 = bf16[2,1,320,640]{3,2,1,0:T(8,128)(2,1)S(1)} collective-permute-done((bf16[2,1,320,640]{3,2,1,0:T(8,128)(2,1)S(1)}, bf16[2,1,320,640]{3,2,1,0:T(8,128)(2,1)S(1)}, u32[]{:S(2)}, u32[]{:S(2)}) %collective-permute-start.17) | collective-permute-done | bytes 819232 | tf_op jit(solution)/shard_map/ppermute | solution.py:17
  174.9 5.1 %collective-permute-done.22 = bf16[2,1,320,256]{3,2,1,0:T(8,128)(2,1)S(1)} collective-permute-done((bf16[2,1,320,256]{3,2,1,0:T(8,128)(2,1)S(1)}, bf16[2,1,320,256]{3,2,1,0:T(8,128)(2,1)S(1)}, u32[]{:S(2)}, u32[]{:S(2)}) %collective-permute-start.22) | collective-permute-done | bytes 327712 | tf_op jit(solution)/shard_map/ppermute | solution.py:17
  181.6 6.4 %collective-permute-done.23 = bf16[1,1,320,256]{3,2,1,0:T(8,128)(2,1)S(1)} collective-permute-done((bf16[1,1,320,256]{3,2,1,0:T(8,128)(2,1)S(1)}, bf16[1,1,320,256]{3,2,1,0:T(8,128)(2,1)S(1)}, u32[]{:S(2)}, u32[]{:S(2)}) %collective-permute-start.23) | collective-permute-done | bytes 163872 | tf_op jit(solution)/shard_map/ppermute | solution.py:17
  190.7 4.0 %collective-permute-done.24 = bf16[160,256]{1,0:T(8,128)(2,1)S(1)} collective-permute-done((bf16[160,256]{1,0:T(8,128)(2,1)S(1)}, bf16[160,256]{1,0:T(8,128)(2,1)S(1)}, u32[]{:S(2)}, u32[]{:S(2)}) %collective-permute-start.24) | collective-permute-done | bytes 81952 | tf_op jit(solution)/shard_map/ppermute | solution.py:17
  194.7 2.5 %collective-permute-start.25 = (bf16[1,80,256]{2,1,0:T(8,128)(2,1)S(1)}, bf16[1,80,256]{2,1,0:T(8,128)(2,1)S(1)}, u32[]{:S(2)}, u32[]{:S(2)}) collective-permute-start(bf16[1,80,256]{2,1,0:T(8,128)(2,1)S(1)} %constant_dynamic-slice_fusion), channel_id=1, source_target_pairs={{0,2},{1,3},{2,0},{3,1},{4,6},{5,7},{6,4},{7,5},{8,10},{9,11},{10,... | collective-permute-start | bytes 122888 | tf_op jit(solution)/shard_map/ppermute | solution.py:17
  197.3 1.9 collective-permute-done.20
  (186 shorter events, 57.7 us)
Async XLA Ops:
  7.2 62.5 %copy-start = (bf16[2560,256]{1,0:T(8,128)(2,1)S(1)}, bf16[2560,256]{1,0:T(8,128)(2,1)}, u32[]{:S(2)}) copy-start(bf16[2560,256]{1,0:T(8,128)(2,1)} %param.8) | copy-start | bytes 3932164
  7.2 10.0 %copy-start.25 = (f32[20,512]{1,0:T(8,128)S(1)}, f32[20,512]{1,0:T(8,128)}, u32[]{:S(2)}) copy-start(f32[20,512]{1,0:T(8,128)} %param.10) | copy-start | bytes 122884
  7.2 78.1 %all-gather.2.cloned.1.call-start = ((), (), s32[]{:S(2)}) async-start(), calls=%async_computation.1 | async-start | bytes 7372800 | tf_op jit(solution)/shard_map/all_gather | solution.py:355
  7.9 193.3 %reduce-scatter.2.cloned.1.call-start = ((), (), s32[]{:S(2)}) async-start(), calls=%async_computation.2 | async-start | bytes 3276800 | tf_op jit(solution)/shard_map/reduce_scatter | solution.py:449
  10.1 19.7 %collective-permute-start.3 = (bf16[128,2560]{0,1:T(8,128)(2,1)}, bf16[128,2560]{0,1:T(8,128)(2,1)}, u32[]{:S(2)}, u32[]{:S(2)}) collective-permute-start(bf16[128,2560]{0,1:T(8,128)(2,1)} %copy.23), channel_id=1, source_target_pairs={{0,1},{1,2},{2,3},{4,5},{5,6},{6,7},{8,9},{9,10},{10,11},{12,13},{... | collective-permute-start | bytes 1966088 | tf_op jit(solution)/shard_map/ppermute | solution.py:280
  15.9 18.5 %collective-permute-start.4 = (bf16[128,2560]{0,1:T(8,128)(2,1)}, bf16[128,2560]{0,1:T(8,128)(2,1)}, u32[]{:S(2)}, u32[]{:S(2)}) collective-permute-start(bf16[128,2560]{0,1:T(8,128)(2,1)} %copy.23), channel_id=1, source_target_pairs={{1,0},{2,1},{3,2},{5,4},{6,5},{7,6},{9,8},{10,9},{11,10},{13,12},{... | collective-permute-start | bytes 1966088 | tf_op jit(solution)/shard_map/ppermute | solution.py:281
  20.3 1.7 collective-permute-start
  22.0 3.6 %collective-permute-start.1 = (f32[1,1,2,1,20]{4,3,2,1,0:T(1,128)S(1)}, f32[1,1,2,1,20]{4,3,2,1,0:T(1,128)S(1)}, u32[]{:S(2)}, u32[]{:S(2)}) collective-permute-start(f32[1,1,2,1,20]{4,3,2,1,0:T(1,128)S(1)} %pad_maximum_fusion.4), channel_id=1, source_target_pairs={{0,8},{4,12},{8,0},{12,4},{16,24},{20,28},{24,16},{28,20},{1,9},{5... | collective-permute-start | bytes 488 | tf_op jit(solution)/shard_map/ppermute | solution.py:17
  25.7 3.7 %collective-permute-start.2 = (f32[1,2,2,1,20]{4,3,2,1,0:T(1,128)S(1)}, f32[1,2,2,1,20]{4,3,2,1,0:T(1,128)S(1)}, u32[]{:S(2)}, u32[]{:S(2)}) collective-permute-start(f32[1,2,2,1,20]{4,3,2,1,0:T(1,128)S(1)} %pad_maximum_fusion.3), channel_id=1, source_target_pairs={{0,16},{4,20},{8,24},{12,28},{16,0},{20,4},{24,8},{28,12},{1,17},{... | collective-permute-start | bytes 968 | tf_op jit(solution)/shard_map/ppermute | solution.py:17
  29.8 17.9 %collective-permute-start.5 = (bf16[128,2560]{0,1:T(8,128)(2,1)}, bf16[128,2560]{0,1:T(8,128)(2,1)S(1)}, u32[]{:S(2)}, u32[]{:S(2)}) collective-permute-start(bf16[128,2560]{0,1:T(8,128)(2,1)} %collective-permute-done.3), channel_id=1, source_target_pairs={{0,1},{1,2},{2,3},{4,5},{5,6},{6,7},{8,9},{9,10},{10,11},{12,13},{... | collective-permute-start | bytes 1966088 | tf_op jit(solution)/shard_map/ppermute | solution.py:280
  34.4 17.6 %collective-permute-start.6 = (bf16[128,2560]{0,1:T(8,128)(2,1)}, bf16[128,2560]{0,1:T(8,128)(2,1)S(1)}, u32[]{:S(2)}, u32[]{:S(2)}) collective-permute-start(bf16[128,2560]{0,1:T(8,128)(2,1)} %collective-permute-done.4), channel_id=1, source_target_pairs={{1,0},{2,1},{3,2},{5,4},{6,5},{7,6},{9,8},{10,9},{11,10},{13,12},{... | collective-permute-start | bytes 1966088 | tf_op jit(solution)/shard_map/ppermute | solution.py:281
  47.7 16.4 %collective-permute-start.7 = (bf16[128,2560]{0,1:T(8,128)(2,1)S(1)}, bf16[128,2560]{0,1:T(8,128)(2,1)S(1)}, u32[]{:S(2)}, u32[]{:S(2)}) collective-permute-start(bf16[128,2560]{0,1:T(8,128)(2,1)S(1)} %collective-permute-done.5), channel_id=1, source_target_pairs={{0,1},{1,2},{2,3},{4,5},{5,6},{6,7},{8,9},{9,10},{10,11},{12,13},{... | collective-permute-start | bytes 1966088 | tf_op jit(solution)/shard_map/ppermute | solution.py:280
  52.0 16.3 %collective-permute-start.8 = (bf16[128,2560]{0,1:T(8,128)(2,1)S(1)}, bf16[128,2560]{0,1:T(8,128)(2,1)S(1)}, u32[]{:S(2)}, u32[]{:S(2)}) collective-permute-start(bf16[128,2560]{0,1:T(8,128)(2,1)S(1)} %collective-permute-done.6), channel_id=1, source_target_pairs={{1,0},{2,1},{3,2},{5,4},{6,5},{7,6},{9,8},{10,9},{11,10},{13,12},{... | collective-permute-start | bytes 1966088 | tf_op jit(solution)/shard_map/ppermute | solution.py:281
  79.4 1.6 collective-permute-start.9
  83.7 10.1 %collective-permute-start.10 = (bf16[128,1280]{1,0:T(8,128)(2,1)}, bf16[128,1280]{1,0:T(8,128)(2,1)}, u32[]{:S(2)}, u32[]{:S(2)}) collective-permute-start(bf16[128,1280]{1,0:T(8,128)(2,1)} %convert_element_type.170), channel_id=1, source_target_pairs={{0,8},{4,12},{8,0},{12,4},{16,24},{20,28},{24,16},{28,20},{1,9},{5... | collective-permute-start | bytes 983048 | tf_op jit(solution)/shard_map/ppermute | solution.py:17
  96.9 4.6 %collective-permute-start.11 = (bf16[128,1280]{1,0:T(8,128)(2,1)S(1)}, bf16[128,1280]{1,0:T(8,128)(2,1)S(1)}, u32[]{:S(2)}, u32[]{:S(2)}) collective-permute-start(bf16[128,1280]{1,0:T(8,128)(2,1)S(1)} %fusion.26), channel_id=1, source_target_pairs={{0,4},{4,0},{8,12},{12,8},{16,20},{20,16},{24,28},{28,24},{1,5},{5... | collective-permute-start | bytes 983048 | tf_op jit(solution)/shard_map/ppermute | solution.py:17
  102.5 18.0 %collective-permute-start.13 = (bf16[128,1280]{1,0:T(8,128)(2,1)}, bf16[128,1280]{1,0:T(8,128)(2,1)}, u32[]{:S(2)}, u32[]{:S(2)}) collective-permute-start(bf16[128,1280]{1,0:T(8,128)(2,1)} %fusion.4), channel_id=1, source_target_pairs={{0,16},{4,20},{8,24},{12,28},{16,0},{20,4},{24,8},{28,12},{1,17},{... | collective-permute-start | bytes 983048 | tf_op jit(solution)/shard_map/ppermute | solution.py:17
  104.8 15.7 %collective-permute-start.12 = (bf16[128,1280]{1,0:T(8,128)(2,1)}, bf16[128,1280]{1,0:T(8,128)(2,1)}, u32[]{:S(2)}, u32[]{:S(2)}) collective-permute-start(bf16[128,1280]{1,0:T(8,128)(2,1)} %convert_element_type.175), channel_id=1, source_target_pairs={{0,8},{4,12},{8,0},{12,4},{16,24},{20,28},{24,16},{28,20},{1,9},{5... | collective-permute-start | bytes 983048 | tf_op jit(solution)/shard_map/ppermute | solution.py:17
  109.1 11.4 %copy-start.19 = (f32[128,1280]{1,0:T(8,128)S(1)}, f32[128,1280]{1,0:T(8,128)}, u32[]{:S(2)}) copy-start(f32[128,1280]{1,0:T(8,128)} %copy-done.18) | copy-start | bytes 1966084
  109.1 13.6 %copy-start.22 = (f32[128,1280]{1,0:T(8,128)S(1)}, f32[128,1280]{1,0:T(8,128)}, u32[]{:S(2)}) copy-start(f32[128,1280]{1,0:T(8,128)} %fusion.6) | copy-start | bytes 1966084
  121.8 12.7 %collective-permute-start.14 = (bf16[128,1280]{1,0:T(8,128)(2,1)S(1)}, bf16[128,1280]{1,0:T(8,128)(2,1)S(1)}, u32[]{:S(2)}, u32[]{:S(2)}) collective-permute-start(bf16[128,1280]{1,0:T(8,128)(2,1)S(1)} %fusion.12), channel_id=1, source_target_pairs={{0,16},{4,20},{8,24},{12,28},{16,0},{20,4},{24,8},{28,12},{1,17},{... | collective-permute-start | bytes 983048 | tf_op jit(solution)/shard_map/ppermute | solution.py:17
  133.9 15.2 %collective-permute-start.15 = (bf16[1280,640]{1,0:T(8,128)(2,1)}, bf16[1280,640]{1,0:T(8,128)(2,1)}, u32[]{:S(2)}, u32[]{:S(2)}) collective-permute-start(bf16[1280,640]{1,0:T(8,128)(2,1)} %shard_map.89), channel_id=1, source_target_pairs={{0,4},{4,0},{8,12},{12,8},{16,20},{20,16},{24,28},{28,24},{1,5},{5... | collective-permute-start | bytes 4915208 | tf_op jit(solution)/shard_map/ppermute | solution.py:17
  134.0 15.2 %collective-permute-start.16 = (bf16[1280,640]{1,0:T(8,128)(2,1)}, bf16[1280,640]{1,0:T(8,128)(2,1)}, u32[]{:S(2)}, u32[]{:S(2)}) collective-permute-start(bf16[1280,640]{1,0:T(8,128)(2,1)} %shard_map.90), channel_id=1, source_target_pairs={{0,4},{4,0},{8,12},{12,8},{16,20},{20,16},{24,28},{28,24},{1,5},{5... | collective-permute-start | bytes 4915208 | tf_op jit(solution)/shard_map/ppermute | solution.py:17
  150.2 7.0 %collective-permute-start.21 = (bf16[1280,256]{1,0:T(8,128)(2,1)S(1)}, bf16[1280,256]{1,0:T(8,128)(2,1)S(1)}, u32[]{:S(2)}, u32[]{:S(2)}) collective-permute-start(bf16[1280,256]{1,0:T(8,128)(2,1)S(1)} %shard_map.94), channel_id=1, source_target_pairs={{0,4},{4,0},{8,12},{12,8},{16,20},{20,16},{24,28},{28,24},{1,5},{5... | collective-permute-start | bytes 1966088 | tf_op jit(solution)/shard_map/ppermute | solution.py:17
  152.3 21.1 %collective-permute-start.17 = (bf16[2,1,320,640]{3,2,1,0:T(8,128)(2,1)S(1)}, bf16[2,1,320,640]{3,2,1,0:T(8,128)(2,1)S(1)}, u32[]{:S(2)}, u32[]{:S(2)}) collective-permute-start(bf16[2,1,320,640]{3,2,1,0:T(8,128)(2,1)S(1)} %constant_dynamic-slice_fusion.8), channel_id=1, source_target_pairs={{0,8},{4,12},{8,0},{12,4},{16,24},{20,28},{24,16},{28,20},{1,9},{5... | collective-permute-start | bytes 2457608 | tf_op jit(solution)/shard_map/ppermute | solution.py:17
  154.9 26.4 %collective-permute-start.19 = (bf16[1,2,320,640]{3,2,1,0:T(8,128)(2,1)S(1)}, bf16[1,2,320,640]{3,2,1,0:T(8,128)(2,1)S(1)}, u32[]{:S(2)}, u32[]{:S(2)}) collective-permute-start(bf16[1,2,320,640]{3,2,1,0:T(8,128)(2,1)S(1)} %constant_dynamic-slice_fusion.6), channel_id=1, source_target_pairs={{0,16},{4,20},{8,24},{12,28},{16,0},{20,4},{24,8},{28,12},{1,17},{... | collective-permute-start | bytes 2457608 | tf_op jit(solution)/shard_map/ppermute | solution.py:17
  157.5 22.5 %collective-permute-start.22 = (bf16[2,1,320,256]{3,2,1,0:T(8,128)(2,1)S(1)}, bf16[2,1,320,256]{3,2,1,0:T(8,128)(2,1)S(1)}, u32[]{:S(2)}, u32[]{:S(2)}) collective-permute-start(bf16[2,1,320,256]{3,2,1,0:T(8,128)(2,1)S(1)} %constant_dynamic-slice_fusion.4), channel_id=1, source_target_pairs={{0,8},{4,12},{8,0},{12,4},{16,24},{20,28},{24,16},{28,20},{1,9},{5... | collective-permute-start | bytes 983048 | tf_op jit(solution)/shard_map/ppermute | solution.py:17
  173.7 23.5 %collective-permute-start.18 = (bf16[1,1,320,640]{3,2,1,0:T(8,128)(2,1)S(1)}, bf16[1,1,320,640]{3,2,1,0:T(8,128)(2,1)S(1)}, u32[]{:S(2)}, u32[]{:S(2)}) collective-permute-start(bf16[1,1,320,640]{3,2,1,0:T(8,128)(2,1)S(1)} %constant_dynamic-slice_fusion.7), channel_id=1, source_target_pairs={{0,16},{4,20},{8,24},{12,28},{16,0},{20,4},{24,8},{28,12},{1,17},{... | collective-permute-start | bytes 1228808 | tf_op jit(solution)/shard_map/ppermute | solution.py:17
  180.1 7.8 %collective-permute-start.23 = (bf16[1,1,320,256]{3,2,1,0:T(8,128)(2,1)S(1)}, bf16[1,1,320,256]{3,2,1,0:T(8,128)(2,1)S(1)}, u32[]{:S(2)}, u32[]{:S(2)}) collective-permute-start(bf16[1,1,320,256]{3,2,1,0:T(8,128)(2,1)S(1)} %constant_dynamic-slice_fusion.3), channel_id=1, source_target_pairs={{0,16},{4,20},{8,24},{12,28},{16,0},{20,4},{24,8},{28,12},{1,17},{... | collective-permute-start | bytes 491528 | tf_op jit(solution)/shard_map/ppermute | solution.py:17
  188.0 6.6 %collective-permute-start.24 = (bf16[160,256]{1,0:T(8,128)(2,1)S(1)}, bf16[160,256]{1,0:T(8,128)(2,1)S(1)}, u32[]{:S(2)}, u32[]{:S(2)}) collective-permute-start(bf16[160,256]{1,0:T(8,128)(2,1)S(1)} %bitcast.126), channel_id=1, source_target_pairs={{0,1},{1,0},{2,3},{3,2},{4,5},{5,4},{6,7},{7,6},{8,9},{9,8},{10,11... | collective-permute-start | bytes 245768 | tf_op jit(solution)/shard_map/ppermute | solution.py:17
  189.5 9.6 %collective-permute-start.20 = (bf16[1,1,320,640]{3,2,1,0:T(8,128)(2,1)S(1)}, bf16[1,1,320,640]{3,2,1,0:T(8,128)(2,1)S(1)}, u32[]{:S(2)}, u32[]{:S(2)}) collective-permute-start(bf16[1,1,320,640]{3,2,1,0:T(8,128)(2,1)S(1)} %constant_dynamic-slice_fusion.5), channel_id=1, source_target_pairs={{0,8},{4,12},{8,0},{12,4},{16,24},{20,28},{24,16},{28,20},{1,9},{5... | collective-permute-start | bytes 1228808 | tf_op jit(solution)/shard_map/ppermute | solution.py:17
  194.7 5.9 %collective-permute-start.25 = (bf16[1,80,256]{2,1,0:T(8,128)(2,1)S(1)}, bf16[1,80,256]{2,1,0:T(8,128)(2,1)S(1)}, u32[]{:S(2)}, u32[]{:S(2)}) collective-permute-start(bf16[1,80,256]{2,1,0:T(8,128)(2,1)S(1)} %constant_dynamic-slice_fusion), channel_id=1, source_target_pairs={{0,2},{1,3},{2,0},{3,1},{4,6},{5,7},{6,4},{7,5},{8,10},{9,11},{10,... | collective-permute-start | bytes 122888 | tf_op jit(solution)/shard_map/ppermute | solution.py:17
  (25 other events, 59.7 us)
Sparse Core Ops, SparseCore 0:
  9.9 49.3 all-gather.1
  143.9 52.2 reduce-scatter.1
